TPU v7x, 32 devices: a whole 2x2x4 slice. The times are simulated.
32 devices in a mesh: ctx: 8 (over y, x, core), head: 4 (over z).
Axes of the slice: x: 2, y: 2, z: 4, core: 2. Of those that a mesh axis runs over, the one named last changes fastest.
Arguments:
- packets: float32 [2048, 1024], P('ctx', 'head')
- baseline: float32 [2048, 1024], P('ctx', 'head'), may hold values from -3 to 3
- w_query: float32 [1024, 1024], P('head'), may hold values from -0.1875 to 0.1875
- w_key: float32 [1024, 1024], P('head'), may hold values from -0.1875 to 0.1875
- w_value: float32 [1024, 1024], P('head'), may hold values from -0.1875 to 0.1875
- w_out: float32 [1024, 1024], P('head'), may hold values from -0.1875 to 0.1875
- gain: float32 [1024], P('head'), may hold values from 0.1 to 1.9
- probe: float32 [2048, 1024], P('ctx', 'head'), may hold values from -6 to 6
- sessions: int32 [2048], replicated, may hold values from 0 to 3, never falling along the last dimension, each value on 1 to 1024 neighbouring positions
- block_lists: int32 [16, 5], P('ctx'), may hold values from 0 to 15, as said below
Outputs:
- attributions: float32 [2048, 1024], P('ctx', 'head')
Inputs may be any that keep to these rules, and one draw needn't show every extreme that they name: `block_lists`: row b lists 5 different blocks, b itself first, all within 4 blocks of b.
All inputs are finite; a program needn't handle non-finite values.
Results may differ from a plain program's by a relative error of at most 0.0003.
Values sent between devices are 32-bit elements; how exact they have to be, the bound alone decides.
No kernel may reach another device: no remote copies, remote signals or barrier semaphores. Data moves between devices by JAX's collectives and lax.ppermute only.
A program may use at most 128 MiB of HBM per device.

v0:
```python
import math

import jax
import jax.numpy as jnp
from jax import lax
from jax.sharding import PartitionSpec as P

HEADS = 16
BLK = 128
KVB = 5
REACH = 2


ALPHAS = (0.25, 0.75)
EPS = 1e-05
HIGHEST = lax.Precision.HIGHEST


def from_behind(x, axis, by):
    size = lax.axis_size(axis)
    pairs = [(i, i + by) for i in range(size) if 0 <= i + by < size]
    return lax.ppermute(x, axis, pairs)


def integrate(points, weights_qkv, w_out, gain, probe, sessions, block_lists):
    steps, rows, feats = points.shape
    width = weights_qkv.shape[1]
    head_dim = width // HEADS
    local_heads = feats // head_dim
    blocks = rows // BLK
    where = lax.axis_index("ctx")
    first = (where - REACH) * blocks
    slots = (2 * REACH + 1) * blocks
    scale = 1.0 / math.sqrt(head_dim)
    part_cols = weights_qkv
    qkv = jnp.einsum(
        "std,ed->ste",
        lax.all_gather(points, "head", axis=2, tiled=True),
        part_cols,
        precision=HIGHEST,
    )
    query = qkv[:, :, :feats]
    pairs = qkv[:, :, feats:]
    below = []
    above = []
    for dist in range(1, REACH + 1):
        below.append(from_behind(pairs, "ctx", dist))
        above.append(from_behind(pairs, "ctx", -dist))
    window = jnp.concatenate(below[::-1] + [pairs] + above, axis=1)
    local = (block_lists - first).reshape(-1)
    tiles = window.reshape(steps, slots, BLK, 2 * feats)
    picked = jnp.take(tiles, local, axis=1).reshape(
        steps, blocks, KVB * BLK, 2, local_heads, head_dim
    )
    keys = picked[:, :, :, 0]
    values = picked[:, :, :, 1]
    token_index = block_lists[:, :, None] * BLK + jnp.arange(BLK, dtype=jnp.int32)[None, None, :]
    key_sessions = jnp.take(sessions, token_index.reshape(blocks, KVB * BLK), axis=0)
    query_sessions = lax.dynamic_slice_in_dim(sessions, where * rows, rows, 0).reshape(blocks, BLK)
    keep = query_sessions[:, :, None] == key_sessions[:, None, :]
    query_heads = query.reshape(steps, blocks, BLK, local_heads, head_dim)
    scores = jnp.einsum("sbqhd,sbkhd->sbhqk", query_heads, keys, precision=HIGHEST) * scale
    scores = jnp.where(keep[None, :, None], scores, -1e30)
    top = jnp.max(scores, axis=-1, keepdims=True)
    expo = jnp.exp(scores - top)
    probs = expo / jnp.sum(expo, axis=-1, keepdims=True)
    mixed = jnp.einsum("sbhqk,sbkhd->sbqhd", probs, values, precision=HIGHEST)
    heads_out = mixed.reshape(steps, rows, feats)
    part_cols = w_out
    projected = jnp.einsum(
        "std,ed->ste",
        lax.all_gather(heads_out, "head", axis=2, tiled=True),
        part_cols,
        precision=HIGHEST,
    )
    summed = points + projected
    first_sum, second_sum = lax.psum(
        (jnp.sum(summed, axis=-1), jnp.sum(summed * summed, axis=-1)), "head"
    )
    mean = first_sum / width
    inverse = lax.rsqrt(second_sum / width - mean * mean + EPS)
    normed = (summed - mean[..., None]) * inverse[..., None]
    upstream = probe * gain
    upstream_sum, upstream_dot = lax.psum(
        (jnp.sum(upstream, axis=-1), jnp.sum(upstream * normed, axis=-1)), "head"
    )
    direct = inverse[..., None] * (
        upstream - upstream_sum[..., None] / width - normed * (upstream_dot / width)[..., None]
    )
    partial_heads = jnp.einsum("ste,ed->std", direct, w_out, precision=HIGHEST)
    grad_heads = lax.psum_scatter(partial_heads, "head", scatter_dimension=2, tiled=True)
    grad_mixed = grad_heads.reshape(steps, blocks, BLK, local_heads, head_dim)
    delta = jnp.einsum("sbqhd,sbqhd->sbhq", grad_mixed, mixed, precision=HIGHEST)
    grad_probs = jnp.einsum("sbqhd,sbkhd->sbhqk", grad_mixed, values, precision=HIGHEST)
    grad_scores = probs * (grad_probs - delta[..., None]) * scale
    grad_query = jnp.einsum("sbhqk,sbkhd->sbqhd", grad_scores, keys, precision=HIGHEST)
    grad_keys = jnp.einsum("sbhqk,sbqhd->sbkhd", grad_scores, query_heads, precision=HIGHEST)
    grad_values = jnp.einsum("sbhqk,sbqhd->sbkhd", probs, grad_mixed, precision=HIGHEST)
    grad_picked = jnp.stack([grad_keys, grad_values], axis=3).reshape(
        steps, blocks * KVB, BLK, 2 * feats
    )
    selector = (local[:, None] == jnp.arange(slots, dtype=jnp.int32)[None, :]).astype(jnp.float32)
    grad_window = jnp.einsum("snlc,nw->swlc", grad_picked, selector, precision=HIGHEST).reshape(
        steps, slots * BLK, 2 * feats
    )
    owned = grad_window[:, REACH * rows : (REACH + 1) * rows]
    for dist in range(1, REACH + 1):
        upper = grad_window[:, (REACH + dist) * rows : (REACH + dist + 1) * rows]
        lower = grad_window[:, (REACH - dist) * rows : (REACH - dist + 1) * rows]
        owned = owned + from_behind(upper, "ctx", dist)
        owned = owned + from_behind(lower, "ctx", -dist)
    grad_qkv = jnp.concatenate([grad_query.reshape(steps, rows, feats), owned], axis=-1)
    partial_input = jnp.einsum("ste,ed->std", grad_qkv, weights_qkv, precision=HIGHEST)
    return (direct, partial_input)


def collect_inputs(partial_input):
    return lax.psum_scatter(partial_input, "head", scatter_dimension=2, tiled=True)


def shards(packets, baseline, w_query, w_key, w_value, w_out, gain, probe, sessions, block_lists):
    weights_qkv = jnp.concatenate([w_query, w_key, w_value], axis=0)
    travel = packets - baseline
    points = jnp.stack([baseline + alpha * travel for alpha in ALPHAS])
    passes = [
        integrate(points[index : index + 1], weights_qkv, w_out, gain, probe, sessions, block_lists)
        for index in range(len(ALPHAS))
    ]
    grads = jnp.zeros_like(packets)
    for direct, partial_input in passes:
        grads = grads + direct.sum(axis=0) + collect_inputs(partial_input).sum(axis=0)
    return travel * grads / len(ALPHAS)


def solution(mesh):
    return jax.shard_map(
        shards,
        mesh=mesh,
        in_specs=(
            P("ctx", "head"),
            P("ctx", "head"),
            P("head", None),
            P("head", None),
            P("head", None),
            P("head", None),
            P("head"),
            P("ctx", "head"),
            P(),
            P("ctx", None),
        ),
        out_specs=P("ctx", "head"),
        check_vma=False,
    )
```

profile of v0, /device:TPU:0, one launch (start us, length us, event | category | flops | bytes accessed | tf_op | source)
XLA Modules:
  0.0 534.8 jit_solution(7361849702621125985)
XLA Ops:
  10.7 7.1 %gather_fusion.1 = s32[1280]{0:T(1024)S(1)} fusion(s32[2048]{0:T(1024)S(1)} %copy-done.2, s32[2048]{0:T(1024)S(1)} %pad_clamp_fusion), kind=kCustom, calls=%fused_computation.1.clone | custom fusion | bytes 15360 | tf_op jit(solution)/shard_map/jit(_take)/gather | solution.py:58
  21.2 19.2 %all-gather.11.cloned.1.call-done = f32[256,1024]{0,1:T(8,128)} async-done(((f32[256,256]{0,1:T(8,128)}), f32[256,1024]{0,1:T(8,128)}) %all-gather.11.cloned.1.call-update) | async-done | bytes 1048592 | tf_op jit(solution)/shard_map/all_gather | solution.py:38
  40.4 7.3 %convolution_bitcast_fusion.9 = f32[1,256,768]{2,1,0:T(8,128)S(1)} fusion(f32[256,1024]{0,1:T(8,128)} %all-gather.11.cloned.1.call-done, f32[768,1024]{1,0:T(8,128)} %constant_dynamic-update-slice_fusion), kind=kOutput, calls=%fused_computation.42 | convolution fusion | flops 2415919104 | bytes 4980736 | tf_op jit(solution)/shard_map/std,ed->ste/dot_general | solution.py:36
  52.8 16.6 %all-gather.13.cloned.1.call-done = f32[256,1024]{0,1:T(8,128)} async-done(((f32[256,256]{0,1:T(8,128)}), f32[256,1024]{0,1:T(8,128)}) %all-gather.13.cloned.1.call-update) | async-done | bytes 1048592 | tf_op jit(solution)/shard_map/all_gather | solution.py:38
  69.4 7.3 %convolution_bitcast_fusion.8 = f32[1,256,768]{2,1,0:T(8,128)S(1)} fusion(f32[256,1024]{0,1:T(8,128)} %all-gather.13.cloned.1.call-done, f32[768,1024]{1,0:T(8,128)} %constant_dynamic-update-slice_fusion), kind=kOutput, calls=%fused_computation.41 | convolution fusion | flops 2415919104 | bytes 4980736 | tf_op jit(solution)/shard_map/std,ed->ste/dot_general | solution.py:36
  108.6 30.5 %collective-permute-done.3 = f32[1,256,512]{2,1,0:T(8,128)S(1)} collective-permute-done((f32[1,256,512]{2,1,0:T(8,128)}, f32[1,256,512]{2,1,0:T(8,128)S(1)}, u32[]{:S(2)}, u32[]{:S(2)}) %collective-permute-start.3) | collective-permute-done | bytes 524320 | tf_op jit(solution)/shard_map/ppermute | solution.py:22
  154.5 5.9 %bitcast_select_fusion.1 = (f32[1,10,128,512]{3,2,1,0:T(8,128)}, f32[1,10,128,512]{3,2,1,0:T(8,128)}) fusion(f32[10,128,512]{2,1,0:T(8,128)} %gather_fusion, pred[10]{0:T(512)(128)(4,1)S(1)} %compare_and_fusion, f32[10,128,512]{2,1,0:T(8,128)} %gather_fusion.2), kind=kLoop, calls=%fused_computation.6 | loop fusion | flops 1310720 | bytes 10485770 | tf_op jit(solution)/shard_map/jit(_take)/select_n | solution.py:52
  160.4 5.8 %reshape.369 = f32[1,2,640,2,4,64]{5,4,3,2,1,0:T(4,128)} reshape(f32[1,10,128,512]{3,2,1,0:T(8,128)} %get-tuple-element.43) | data formatting | bytes 5242880 | tf_op jit(solution)/shard_map/reshape | solution.py:52
  166.1 5.1 fusion.62
  178.1 5.8 %reshape.371 = f32[1,2,640,2,4,64]{5,4,3,2,1,0:T(4,128)} reshape(f32[1,10,128,512]{3,2,1,0:T(8,128)} %get-tuple-element.44) | data formatting | bytes 5242880 | tf_op jit(solution)/shard_map/reshape | solution.py:52
  183.9 5.2 fusion.63
  196.2 4.7 fusion.3
  212.5 5.3 fusion.11
  219.9 12.8 %all-gather.7.cloned.1.call-done = f32[1,256,1024]{1,0,2:T(1,128)} async-done(((f32[1,256,256]{1,0,2:T(1,128)}), f32[1,256,1024]{1,0,2:T(1,128)}) %all-gather.7.cloned.1.call-update) | async-done | bytes 1048592 | tf_op jit(solution)/shard_map/all_gather | solution.py:72
  235.0 26.6 %all-gather.9.cloned.1.call-done = f32[1,256,1024]{1,0,2:T(1,128)} async-done(((f32[1,256,256]{1,0,2:T(1,128)}), f32[1,256,1024]{1,0,2:T(1,128)}) %all-gather.9.cloned.1.call-update) | async-done | bytes 1048592 | tf_op jit(solution)/shard_map/all_gather | solution.py:72
  263.9 10.3 %all-reduce.1 = (f32[1,256]{1,0:T(1,128)S(1)}, f32[1,256]{1,0:T(1,128)S(1)}, f32[1,256]{1,0:T(1,128)S(1)}, f32[1,256]{1,0:T(1,128)S(1)}) all-reduce(f32[1,256]{1,0:T(1,128)S(1)} %bitcast.230, f32[1,256]{1,0:T(1,128)S(1)} %bitcast.229, f32[1,256]{1,0:T(1,128)S(1)} %bitcast.231, ...), channel_id=1, replica_groups=mesh['ctx'=8,'head'=4] {'head'}, use_global_device_ids=true, to_apply=%region_5.8 | all-reduce | flops 1024 | bytes 8192 | tf_op jit(solution)/shard_map/psum | solution.py:77
  274.4 8.5 %all-reduce = (f32[1,256]{1,0:T(1,128)S(1)}, f32[256]{0:T(256)S(1)}, f32[1,256]{1,0:T(1,128)S(1)}) all-reduce(f32[1,256]{1,0:T(1,128)S(1)} %bitcast.228, f32[256]{0:T(256)S(1)} %get-tuple-element.9, f32[1,256]{1,0:T(1,128)S(1)} %bitcast.227), channel_id=1, replica_groups=mesh['ctx'=8,'head'=4] {'head'}, use_global_device_ids=true, to_apply=%region_19.22 | all-reduce | flops 768 | bytes 6144 | tf_op jit(solution)/shard_map/psum | solution.py:84
  287.5 24.3 %reduce-scatter.5.cloned.1.call-done = f32[1,256,256]{2,1,0:T(8,128)} async-done(((f32[1,256,1024]{2,1,0:T(8,128)}), f32[1,256,256]{2,1,0:T(8,128)}) %reduce-scatter.5.cloned.1.call-update) | async-done | bytes 262160 | tf_op jit(solution)/shard_map/reduce_scatter | solution.py:91
  314.0 25.9 %reduce-scatter.9.cloned.1.call-done = f32[1,256,256]{2,1,0:T(8,128)} async-done(((f32[1,256,1024]{2,1,0:T(8,128)}), f32[1,256,256]{2,1,0:T(8,128)}) %reduce-scatter.9.cloned.1.call-update) | async-done | bytes 262160 | tf_op jit(solution)/shard_map/reduce_scatter | solution.py:91
  354.2 5.1 multiply_multiply_fusion.1
  359.3 5.3 reshape.312
  364.6 5.6 %copy.134 = f32[10,128,512]{2,0,1:T(8,128)} copy(f32[10,128,512]{1,0,2:T(8,128)} %reshape.312) | data formatting | bytes 5242880 | tf_op jit(solution)/shard_map/reshape.101
  381.7 5.4 %collective-permute-start.14 = (f32[1,256,512]{2,1,0:T(8,128)}, f32[1,256,512]{2,1,0:T(8,128)}, u32[]{:S(2)}, u32[]{:S(2)}) collective-permute-start(f32[1,256,512]{2,1,0:T(8,128)} %get-tuple-element.35), channel_id=1, source_target_pairs={{0,8},{4,12},{8,16},{12,20},{16,24},{20,28},{1,9},{5,13},{9,17},{1... | collective-permute-start | bytes 1572872 | tf_op jit(solution)/shard_map/ppermute | solution.py:22
  392.2 5.1 convolution_bitcast_fusion.2
  400.9 8.0 %convolution_bitcast_fusion.4 = f32[1,256,1024]{1,2,0:T(8,128)} fusion(f32[768,1024]{1,0:T(8,128)} %constant_dynamic-update-slice_fusion, f32[1,256,512]{2,1,0:T(8,128)S(1)} %fusion.36, f32[1,256,256]{2,1,0:T(8,128)S(1)} %copy.136), kind=kOutput, calls=%fused_computation.23 | convolution fusion | flops 2416115712 | bytes 4980736 | tf_op jit(solution)/shard_map/ste,ed->std/dot_general | solution.py:113
  416.5 5.3 reshape.299
  421.8 5.6 %copy.117 = f32[10,128,512]{2,0,1:T(8,128)} copy(f32[10,128,512]{1,0,2:T(8,128)} %reshape.299) | data formatting | bytes 5242880 | tf_op jit(solution)/shard_map/reshape.57
  434.8 20.8 %collective-permute-start.4 = (f32[1,256,512]{2,1,0:T(8,128)}, f32[1,256,512]{2,1,0:T(8,128)S(1)}, u32[]{:S(2)}, u32[]{:S(2)}) collective-permute-start(f32[1,256,512]{2,1,0:T(8,128)} %get-tuple-element.29), channel_id=1, source_target_pairs={{0,4},{4,8},{8,12},{12,16},{16,20},{20,24},{24,28},{1,5},{5,9},{9,... | collective-permute-start | bytes 1572872 | tf_op jit(solution)/shard_map/ppermute | solution.py:22
  456.9 5.4 %collective-permute-start.6 = (f32[1,256,512]{2,1,0:T(8,128)}, f32[1,256,512]{2,1,0:T(8,128)}, u32[]{:S(2)}, u32[]{:S(2)}) collective-permute-start(f32[1,256,512]{2,1,0:T(8,128)} %get-tuple-element.31), channel_id=1, source_target_pairs={{0,8},{4,12},{8,16},{12,20},{16,24},{20,28},{1,9},{5,13},{9,17},{1... | collective-permute-start | bytes 1572872 | tf_op jit(solution)/shard_map/ppermute | solution.py:22
  467.5 5.2 collective-permute-done.7
  475.0 8.0 %convolution_bitcast_fusion.6 = f32[1,256,1024]{1,2,0:T(8,128)} fusion(f32[768,1024]{1,0:T(8,128)} %constant_dynamic-update-slice_fusion, f32[1,256,512]{2,1,0:T(8,128)S(1)} %fusion.39, f32[1,256,256]{2,1,0:T(8,128)S(1)} %copy.119), kind=kOutput, calls=%fused_computation.25 | convolution fusion | flops 2416115712 | bytes 4980736 | tf_op jit(solution)/shard_map/ste,ed->std/dot_general | solution.py:113
  483.1 42.4 %reduce-scatter.7.cloned.1.call-done = f32[1,256,256]{1,2,0:T(8,128)} async-done(((f32[1,256,1024]{1,2,0:T(8,128)}), f32[1,256,256]{1,2,0:T(8,128)}) %reduce-scatter.7.cloned.1.call-update) | async-done | bytes 262160 | tf_op jit(solution)/shard_map/reduce_scatter | solution.py:118
  (200 shorter events, 158.7 us)
Async XLA Ops:
  6.5 226.2 %copy-start = (f32[256,1024]{1,0:T(8,128)S(1)}, f32[256,1024]{1,0:T(8,128)}, u32[]{:S(2)}) copy-start(f32[256,1024]{1,0:T(8,128)} %param.19) | copy-start | bytes 3145732
  6.5 33.8 %all-gather.11.cloned.1.call-start = ((), (), s32[]{:S(2)}) async-start(), calls=%async_computation.10 | async-start | bytes 1310720 | tf_op jit(solution)/shard_map/all_gather | solution.py:38
  9.6 59.8 %all-gather.13.cloned.1.call-start = ((), (), s32[]{:S(2)}) async-start(), calls=%async_computation.11 | async-start | bytes 1310720 | tf_op jit(solution)/shard_map/all_gather | solution.py:38
  10.4 222.3 %all-gather.7.cloned.1.call-start = ((), (), s32[]{:S(2)}) async-start(), calls=%async_computation.4 | async-start | bytes 1310720 | tf_op jit(solution)/shard_map/all_gather | solution.py:72
  48.6 45.5 %collective-permute-start = (f32[1,256,512]{2,1,0:T(8,128)}, f32[1,256,512]{2,1,0:T(8,128)}, u32[]{:S(2)}, u32[]{:S(2)}) collective-permute-start(f32[1,256,512]{2,1,0:T(8,128)} %slice.78), channel_id=1, source_target_pairs={{0,8},{4,12},{8,16},{12,20},{16,24},{20,28},{1,9},{5,13},{9,17},{1... | collective-permute-start | bytes 1572872 | tf_op jit(solution)/shard_map/ppermute | solution.py:22
  77.6 19.6 %collective-permute-start.8 = (f32[1,256,512]{2,1,0:T(8,128)}, f32[1,256,512]{2,1,0:T(8,128)}, u32[]{:S(2)}, u32[]{:S(2)}) collective-permute-start(f32[1,256,512]{2,1,0:T(8,128)} %slice.87), channel_id=1, source_target_pairs={{0,8},{4,12},{8,16},{12,20},{16,24},{20,28},{1,9},{5,13},{9,17},{1... | collective-permute-start | bytes 1572872 | tf_op jit(solution)/shard_map/ppermute | solution.py:22
  82.0 18.4 %collective-permute-start.1 = (f32[1,256,512]{2,1,0:T(8,128)}, f32[1,256,512]{2,1,0:T(8,128)}, u32[]{:S(2)}, u32[]{:S(2)}) collective-permute-start(f32[1,256,512]{2,1,0:T(8,128)} %slice.78), channel_id=1, source_target_pairs={{0,4},{4,8},{8,12},{12,16},{16,20},{20,24},{24,28},{1,5},{5,9},{9,... | collective-permute-start | bytes 1572872 | tf_op jit(solution)/shard_map/ppermute | solution.py:22
  85.2 63.4 %collective-permute-start.11 = (f32[1,256,512]{2,1,0:T(8,128)}, f32[1,256,512]{2,1,0:T(8,128)}, u32[]{:S(2)}, u32[]{:S(2)}) collective-permute-start(f32[1,256,512]{2,1,0:T(8,128)} %slice.87), channel_id=1, source_target_pairs={{8,0},{12,4},{16,8},{20,12},{24,16},{28,20},{9,1},{13,5},{17,9},{2... | collective-permute-start | bytes 1572872 | tf_op jit(solution)/shard_map/ppermute | solution.py:22
  86.5 60.2 %collective-permute-start.10 = (f32[1,256,512]{2,1,0:T(8,128)}, f32[1,256,512]{2,1,0:T(8,128)}, u32[]{:S(2)}, u32[]{:S(2)}) collective-permute-start(f32[1,256,512]{2,1,0:T(8,128)} %slice.87), channel_id=1, source_target_pairs={{4,0},{8,4},{12,8},{16,12},{20,16},{24,20},{28,24},{5,1},{9,5},{13... | collective-permute-start | bytes 1572872 | tf_op jit(solution)/shard_map/ppermute | solution.py:22
  90.0 103.4 %copy-start.14 = (f32[2,128,4,64]{1,3,2,0:T(8,128)}, f32[2,128,4,64]{1,3,2,0:T(8,128)S(1)}, u32[]{:S(2)}) copy-start(f32[2,128,4,64]{1,3,2,0:T(8,128)S(1)} %copy.108) | copy-start | bytes 786436
  94.1 13.7 %collective-permute-start.2 = (f32[1,256,512]{2,1,0:T(8,128)}, f32[1,256,512]{2,1,0:T(8,128)S(1)}, u32[]{:S(2)}, u32[]{:S(2)}) collective-permute-start(f32[1,256,512]{2,1,0:T(8,128)} %slice.78), channel_id=1, source_target_pairs={{4,0},{8,4},{12,8},{16,12},{20,16},{24,20},{28,24},{5,1},{9,5},{13... | collective-permute-start | bytes 1572872 | tf_op jit(solution)/shard_map/ppermute | solution.py:22
  97.2 41.9 %collective-permute-start.3 = (f32[1,256,512]{2,1,0:T(8,128)}, f32[1,256,512]{2,1,0:T(8,128)S(1)}, u32[]{:S(2)}, u32[]{:S(2)}) collective-permute-start(f32[1,256,512]{2,1,0:T(8,128)} %slice.78), channel_id=1, source_target_pairs={{8,0},{12,4},{16,8},{20,12},{24,16},{28,20},{9,1},{13,5},{17,9},{2... | collective-permute-start | bytes 1572872 | tf_op jit(solution)/shard_map/ppermute | solution.py:22
  100.4 43.5 %collective-permute-start.9 = (f32[1,256,512]{2,1,0:T(8,128)}, f32[1,256,512]{2,1,0:T(8,128)}, u32[]{:S(2)}, u32[]{:S(2)}) collective-permute-start(f32[1,256,512]{2,1,0:T(8,128)} %slice.87), channel_id=1, source_target_pairs={{0,4},{4,8},{8,12},{12,16},{16,20},{20,24},{24,28},{1,5},{5,9},{9,... | collective-permute-start | bytes 1572872 | tf_op jit(solution)/shard_map/ppermute | solution.py:22
  205.7 55.8 %all-gather.9.cloned.1.call-start = ((), (), s32[]{:S(2)}) async-start(), calls=%async_computation.7 | async-start | bytes 1310720 | tf_op jit(solution)/shard_map/all_gather | solution.py:72
  212.5 20.2 %copy-start.20 = (f32[256,256]{0,1:T(8,128)S(1)}, f32[256,256]{0,1:T(8,128)}, u32[]{:S(2)}) copy-start(f32[256,256]{0,1:T(8,128)} %get-tuple-element.23) | copy-start | bytes 786436
  218.7 93.1 %reduce-scatter.5.cloned.1.call-start = ((), (), s32[]{:S(2)}) async-start(), calls=%async_computation.5 | async-start | bytes 1310720 | tf_op jit(solution)/shard_map/reduce_scatter | solution.py:91
  219.9 54.4 %copy-start.31 = (f32[256]{0:T(256)S(1)}, f32[256]{0:T(256)}, u32[]{:S(2)}) copy-start(f32[256]{0:T(256)} %param.20) | copy-start | bytes 3076
  285.0 54.9 %reduce-scatter.9.cloned.1.call-start = ((), (), s32[]{:S(2)}) async-start(), calls=%async_computation.8 | async-start | bytes 1310720 | tf_op jit(solution)/shard_map/reduce_scatter | solution.py:91
  287.2 195.9 %reduce-scatter.11.cloned.1.call-start = ((), (), s32[]{:S(2)}) async-start(), calls=%async_computation.9 | async-start | bytes 1310720 | tf_op jit(solution)/shard_map/reduce_scatter | solution.py:118
  377.7 19.6 %collective-permute-start.12 = (f32[1,256,512]{2,1,0:T(8,128)}, f32[1,256,512]{2,1,0:T(8,128)}, u32[]{:S(2)}, u32[]{:S(2)}) collective-permute-start(f32[1,256,512]{2,1,0:T(8,128)} %get-tuple-element.33), channel_id=1, source_target_pairs={{0,4},{4,8},{8,12},{12,16},{16,20},{20,24},{24,28},{1,5},{5,9},{9,... | collective-permute-start | bytes 1572872 | tf_op jit(solution)/shard_map/ppermute | solution.py:22
  380.4 17.1 %collective-permute-start.15 = (f32[1,256,512]{2,1,0:T(8,128)}, f32[1,256,512]{2,1,0:T(8,128)}, u32[]{:S(2)}, u32[]{:S(2)}) collective-permute-start(f32[1,256,512]{2,1,0:T(8,128)} %get-tuple-element.34), channel_id=1, source_target_pairs={{8,0},{12,4},{16,8},{20,12},{24,16},{28,20},{9,1},{13,5},{17,9},{2... | collective-permute-start | bytes 1572872 | tf_op jit(solution)/shard_map/ppermute | solution.py:22
  381.7 17.2 %collective-permute-start.14 = (f32[1,256,512]{2,1,0:T(8,128)}, f32[1,256,512]{2,1,0:T(8,128)}, u32[]{:S(2)}, u32[]{:S(2)}) collective-permute-start(f32[1,256,512]{2,1,0:T(8,128)} %get-tuple-element.35), channel_id=1, source_target_pairs={{0,8},{4,12},{8,16},{12,20},{16,24},{20,28},{1,9},{5,13},{9,17},{1... | collective-permute-start | bytes 1572872 | tf_op jit(solution)/shard_map/ppermute | solution.py:22
  387.1 11.9 %collective-permute-start.13 = (f32[1,256,512]{2,1,0:T(8,128)}, f32[1,256,512]{2,1,0:T(8,128)}, u32[]{:S(2)}, u32[]{:S(2)}) collective-permute-start(f32[1,256,512]{2,1,0:T(8,128)} %get-tuple-element.36), channel_id=1, source_target_pairs={{4,0},{8,4},{12,8},{16,12},{20,16},{24,20},{28,24},{5,1},{9,5},{13... | collective-permute-start | bytes 1572872 | tf_op jit(solution)/shard_map/ppermute | solution.py:22
  408.9 116.5 %reduce-scatter.7.cloned.1.call-start = ((), (), s32[]{:S(2)}) async-start(), calls=%async_computation.6 | async-start | bytes 1310720 | tf_op jit(solution)/shard_map/reduce_scatter | solution.py:118
  433.4 33.7 %copy-start.10 = (f32[10,128,512]{2,1,0:T(8,128)}, f32[10,128,512]{2,1,0:T(8,128)S(1)}, u32[]{:S(2)}) copy-start(f32[10,128,512]{2,1,0:T(8,128)S(1)} %copy.118) | copy-start | bytes 7864324
  433.4 30.4 %copy-start.11 = (f32[2,4,128,640]{3,2,1,0:T(8,128)S(1)}, f32[2,4,128,640]{3,2,1,0:T(8,128)}, u32[]{:S(2)}) copy-start(f32[2,4,128,640]{3,2,1,0:T(8,128)} %multiply_multiply_fusion.1) | copy-start | bytes 7864324
  434.8 32.7 %collective-permute-start.4 = (f32[1,256,512]{2,1,0:T(8,128)}, f32[1,256,512]{2,1,0:T(8,128)S(1)}, u32[]{:S(2)}, u32[]{:S(2)}) collective-permute-start(f32[1,256,512]{2,1,0:T(8,128)} %get-tuple-element.29), channel_id=1, source_target_pairs={{0,4},{4,8},{8,12},{12,16},{16,20},{20,24},{24,28},{1,5},{5,9},{9,... | collective-permute-start | bytes 1572872 | tf_op jit(solution)/shard_map/ppermute | solution.py:22
  455.6 17.1 %collective-permute-start.7 = (f32[1,256,512]{2,1,0:T(8,128)}, f32[1,256,512]{2,1,0:T(8,128)}, u32[]{:S(2)}, u32[]{:S(2)}) collective-permute-start(f32[1,256,512]{2,1,0:T(8,128)} %get-tuple-element.30), channel_id=1, source_target_pairs={{8,0},{12,4},{16,8},{20,12},{24,16},{28,20},{9,1},{13,5},{17,9},{2... | collective-permute-start | bytes 1572872 | tf_op jit(solution)/shard_map/ppermute | solution.py:22
  456.9 16.2 %collective-permute-start.6 = (f32[1,256,512]{2,1,0:T(8,128)}, f32[1,256,512]{2,1,0:T(8,128)}, u32[]{:S(2)}, u32[]{:S(2)}) collective-permute-start(f32[1,256,512]{2,1,0:T(8,128)} %get-tuple-element.31), channel_id=1, source_target_pairs={{0,8},{4,12},{8,16},{12,20},{16,24},{20,28},{1,9},{5,13},{9,17},{1... | collective-permute-start | bytes 1572872 | tf_op jit(solution)/shard_map/ppermute | solution.py:22
  462.3 10.9 %collective-permute-start.5 = (f32[1,256,512]{2,1,0:T(8,128)}, f32[1,256,512]{2,1,0:T(8,128)}, u32[]{:S(2)}, u32[]{:S(2)}) collective-permute-start(f32[1,256,512]{2,1,0:T(8,128)} %get-tuple-element.32), channel_id=1, source_target_pairs={{4,0},{8,4},{12,8},{16,12},{20,16},{24,20},{28,24},{5,1},{9,5},{13... | collective-permute-start | bytes 1572872 | tf_op jit(solution)/shard_map/ppermute | solution.py:22
  475.0 50.5 %copy-start.19 = (f32[256,256]{0,1:T(8,128)S(1)}, f32[256,256]{0,1:T(8,128)}, u32[]{:S(2)}) copy-start(f32[256,256]{0,1:T(8,128)} %copy-done.18) | copy-start | bytes 786436
  475.0 52.5 %copy-start.1 = (f32[256,1024]{1,0:T(8,128)S(1)}, f32[256,1024]{1,0:T(8,128)}, u32[]{:S(2)}) copy-start(f32[256,1024]{1,0:T(8,128)} %param.19) | copy-start | bytes 3145732
  (25 other events, 138.2 us)
Sparse Core Ops, SparseCore 0:
  9.7 30.6 all-gather.10
  41.9 27.4 all-gather.12
  205.9 26.7 all-gather.6
  234.1 27.4 all-gather.8
  285.1 26.5 reduce-scatter.4
  314.0 25.8 reduce-scatter.8
  409.0 43.1 reduce-scatter.10
  483.2 42.2 reduce-scatter.6
where the time goes:
time: 545 us; the launch traced here: 535 us
  waiting for transfers between devices  206 us (38%)
  local copies, waits for them, and re-layouts  123 us (23%)
  matrix products  94.5 us (17%)
  starting transfers between devices  61 us (11%)
  blocking collectives  18.8 us (3%)
  other arithmetic  16.8 us (3%)
  between operations  14.8 us (3%)
    ppermute x16, starting transfers between devices, from_behind(): return lax.ppermute(x, axis, pairs)  60.3 us
    reduce_scatter x2, waiting for transfers between devices, integrate(): lax.psum_scatter(partial_heads, 'head', scatter_dimension=2, tiled=True)  50.2 us
    reduce_scatter x2, waiting for transfers between devices, collect_inputs(): lax.psum_scatter(partial_input, 'head', scatter_dimension=2, tiled=True)  42.4 us
    all_gather x2, waiting for transfers between devices, integrate(): lax.all_gather(heads_out, 'head', axis=2, tiled=True)  39.4 us
    ppermute x16, waiting for transfers between devices, from_behind(): return lax.ppermute(x, axis, pairs)  37.9 us
    all_gather x2, waiting for transfers between devices, integrate(): lax.all_gather(points, 'head', axis=2, tiled=True)  35.8 us
    unnamed x84, local copies, waits for them, and re-layouts  32.9 us
    another operation x10, local copies, waits for them, and re-layouts  28.4 us
  transfers between devices with their start and end apart: 24, of which 12 were waited for; matrix products, arithmetic and copies ran while one was open for 22% of the time, Pallas kernels for 0%

commit v1 on v0

--- a/solution.py
+++ b/solution.py
@@ -3,6 +3,8 @@
 import jax
 import jax.numpy as jnp
 from jax import lax
+from jax.experimental import pallas as pl
+from jax.experimental.pallas import tpu as pltpu
 from jax.sharding import PartitionSpec as P
 
 HEADS = 16
@@ -118,7 +120,7 @@
     return lax.psum_scatter(partial_input, "head", scatter_dimension=2, tiled=True)
 
 
-def shards(packets, baseline, w_query, w_key, w_value, w_out, gain, probe, sessions, block_lists):
+def general_shards(packets, baseline, w_query, w_key, w_value, w_out, gain, probe, sessions, block_lists):
     weights_qkv = jnp.concatenate([w_query, w_key, w_value], axis=0)
     travel = packets - baseline
     points = jnp.stack([baseline + alpha * travel for alpha in ALPHAS])
@@ -132,9 +134,370 @@
     return travel * grads / len(ALPHAS)
 
 
+F32 = jnp.float32
+BF16 = jnp.bfloat16
+LIMIT = 48 * 1024 * 1024
+VM = pl.BlockSpec(memory_space=pltpu.VMEM)
+SM = pl.BlockSpec(memory_space=pltpu.SMEM)
+
+
+def halves(x):
+    high = x.astype(BF16)
+    low = (x - high.astype(F32)).astype(BF16)
+    return high, low
+
+
+def halves_outside(x):
+    rounded = lax.reduce_precision(x, 8, 7)
+    return rounded.astype(BF16), (x - rounded).astype(BF16)
+
+
+def mm(a, b):
+    return lax.dot_general(a, b, (((1,), (0,)), ((), ())), preferred_element_type=F32)
+
+
+def mm_nt(a, b):
+    return lax.dot_general(a, b, (((1,), (1,)), ((), ())), preferred_element_type=F32)
+
+
+def call(kernel, outs, scratch, n_smem, *args):
+    return pl.pallas_call(
+        kernel,
+        out_shape=outs,
+        in_specs=[SM] * n_smem + [VM] * (len(args) - n_smem),
+        out_specs=jax.tree.map(lambda _: VM, outs),
+        scratch_shapes=scratch,
+        compiler_params=pltpu.CompilerParams(vmem_limit_bytes=LIMIT),
+    )(*args)
+
+
+def shift(x, by, low, high):
+    return lax.ppermute(x, "head", [(i, i + by) for i in range(low, high + 1)])
+
+
+def rotate(x, by):
+    size = lax.axis_size("head")
+    return lax.ppermute(x, "head", [(i, (i + by) % size) for i in range(size)])
+
+
+def exchange(pieces):
+    return [pieces[0]] + [rotate(pieces[k], k) for k in range(1, len(pieces))]
+
+
+def project_kernel(z_ref, w3, own0, own1, *rest):
+    ups = [rest[0:2], rest[2:4], rest[4:6]]
+    downs = [rest[6:8], rest[8:10], rest[10:12]]
+    out, rows, x3 = rest[12:]
+    z = z_ref[0]
+    n = 4
+    quarter = rows.shape[1]
+    width = rows.shape[2]
+    for s, own in enumerate((own0, own1)):
+        tokens, feats = own.shape
+        for k in range(n):
+            column = lax.rem(z - k + n, n) * feats
+            at = pl.ds(pl.multiple_of(z * quarter, quarter), quarter)
+            if k == 0:
+                x = own[...]
+                mine = own[at, :]
+            else:
+                up, down = ups[k - 1][s], downs[n - k - 1][s]
+                x = up[...] + down[...]
+                mine = up[at, :] + down[at, :]
+            rows[s, :, pl.ds(pl.multiple_of(column, feats), feats)] = mine
+            high, low = halves(x)
+            span = pl.ds(s * tokens, tokens)
+            x3[span, pl.ds(pl.multiple_of(column, feats), feats)] = high
+            x3[span, pl.ds(pl.multiple_of(width + column, feats), feats)] = high
+            x3[span, pl.ds(pl.multiple_of(2 * width + column, feats), feats)] = low
+    part = out.shape[1]
+    for s in range(2):
+        for h in range(n):
+            out[2 * h + s] = mm_nt(
+                w3[h * part : (h + 1) * part, :], x3[s * tokens : (s + 1) * tokens, :]
+            )
+
+
+def attend_kernel(lists, session_col, session_row, qkv, mixed, p_high, p_low, q3, k3, v2):
+    for b in range(NBLOCKS):
+        t = qkv[b // 2, :, (b % 2) * BLK : (b % 2 + 1) * BLK]
+        q_high, q_low = halves(t[:HD] * SCALE)
+        q3[b] = jnp.concatenate([q_high, q_high, q_low], axis=0)
+        k_high, k_low = halves(t[HD : 2 * HD].T)
+        k3[b] = jnp.concatenate([k_high, k_low, k_high], axis=1)
+        v_high, v_low = halves(t[2 * HD :])
+        v2[b] = jnp.concatenate([v_high, v_low], axis=0)
+
+    def body(c, carry):
+        for e in range(2):
+            b = 2 * c + e
+            query = q3[b]
+            mine = session_row[pl.ds(b, 1), :]
+            scores = []
+            for j in range(KVB):
+                other = lists[b, j]
+                s = mm(k3[other], query)
+                scores.append(jnp.where(session_col[other] == mine, s, -1e30))
+            s = jnp.concatenate(scores, axis=0)
+            top = jnp.max(s, axis=0, keepdims=True)
+            expo = jnp.exp(s - top)
+            probs = expo * (1.0 / jnp.sum(expo, axis=0, keepdims=True))
+            high, low = halves(probs)
+            p_high[b] = high
+            p_low[b] = low
+            values = jnp.concatenate([v2[lists[b, j]] for j in range(KVB)], axis=1)
+            both = mm(values, high)
+            mixed[c, :, e * BLK : (e + 1) * BLK] = both[:HD] + both[HD:] + mm(values[:HD], low)
+        return carry
+
+    lax.fori_loop(0, NBLOCKS // 2, body, 0)
+
+
+def attend_back_kernel(lists, qkv, p_high, p_low, grad, mixed, out, q2, k2, v3, acc):
+    for b in range(NBLOCKS):
+        t = qkv[b // 2, :, (b % 2) * BLK : (b % 2 + 1) * BLK]
+        q_high, q_low = halves(t[:HD])
+        q2[b] = jnp.concatenate([q_high, q_low], axis=0)
+        k_high, k_low = halves(t[HD : 2 * HD])
+        k2[b] = jnp.concatenate([k_high, k_low], axis=0)
+        v_high, v_low = halves(t[2 * HD :].T)
+        v3[b] = jnp.concatenate([v_high, v_low, v_high], axis=1)
+    acc[...] = jnp.zeros_like(acc)
+
+    def body(c, carry):
+        for e in range(2):
+            b = 2 * c + e
+            lanes = slice(e * BLK, (e + 1) * BLK)
+            g = grad[c, :, lanes]
+            delta = jnp.sum(g * mixed[c, :, lanes], axis=0, keepdims=True)
+            g_high, g_low = halves(g)
+            g3 = jnp.concatenate([g_high, g_high, g_low], axis=0)
+            g2 = jnp.concatenate([g_high, g_low], axis=0)
+            grad_probs = jnp.concatenate([mm(v3[lists[b, j]], g3) for j in range(KVB)], axis=0)
+            ph, pw = p_high[b], p_low[b]
+            probs = ph.astype(F32) + pw.astype(F32)
+            s_high, s_low = halves(probs * (grad_probs - delta) * SCALE)
+            keys = jnp.concatenate([k2[lists[b, j]] for j in range(KVB)], axis=1)
+            both = mm(keys, s_high)
+            out[c, 0:HD, lanes] = both[:HD] + both[HD:] + mm(keys[:HD], s_low)
+            query = q2[b]
+            both = mm_nt(query, s_high)
+            grad_keys = both[:HD] + both[HD:] + mm_nt(query[:HD], s_low)
+            both = mm_nt(g2, ph)
+            grad_values = both[:HD] + both[HD:] + mm_nt(g2[:HD], pw)
+            for j in range(KVB):
+                at = slice(j * BLK, (j + 1) * BLK)
+                acc[lists[b, j]] += jnp.concatenate([grad_keys[:, at], grad_values[:, at]], axis=0)
+        return carry
+
+    lax.fori_loop(0, NBLOCKS // 2, body, 0)
+    for b in range(NBLOCKS):
+        out[b // 2, HD : 3 * HD, (b % 2) * BLK : (b % 2 + 1) * BLK] = acc[b]
+
+
+def to_tokens_kernel(z_ref, mixed, o0, o1, o2, o3, turned):
+    z = z_ref[0]
+    n = 4
+    quarter = o0.shape[1]
+    for s in range(2):
+        turned[s] = jnp.concatenate([mixed[2 * h + s] for h in range(n)], axis=0).T
+    for k, o in enumerate((o0, o1, o2, o3)):
+        start = pl.multiple_of(lax.rem(z + k, n) * quarter, quarter)
+        o[...] = turned[:, pl.ds(start, quarter), :]
+
+
+def to_heads_kernel(z_ref, g0, g1, g2, g3, out, turned):
+    z = z_ref[0]
+    n = 4
+    quarter = g0.shape[1]
+    for k, g in enumerate((g0, g1, g2, g3)):
+        start = pl.multiple_of(lax.rem(z - k + n, n) * quarter, quarter)
+        turned[:, pl.ds(start, quarter), :] = g[...]
+    for s in range(2):
+        t = turned[s].T
+        for h in range(n):
+            out[2 * h + s] = t[h * HD : (h + 1) * HD]
+
+
+def norm_kernel(
+    z_ref, w_high, w_low, rows, u0, u1, u2, u3, m0, m1, m2, m3,
+    g0, g1, g2, g3, direct_sum, mixed, upstream, grad,
+):
+    z = z_ref[0]
+    n = 4
+    quarter, width = rows.shape[1:]
+    feats = width // n
+    for k, (u, m) in enumerate(((u0, m0), (u1, m1), (u2, m2), (u3, m3))):
+        at = pl.ds(pl.multiple_of(lax.rem(z - k + n, n) * feats, feats), feats)
+        upstream[:, at] = u[...]
+        for s in range(2):
+            mixed[s * quarter : (s + 1) * quarter, at] = m[s]
+    m_high, m_low = halves(mixed[...])
+    projected = mm_nt(m_high, w_high[...]) + mm_nt(m_low, w_high[...]) + mm_nt(m_high, w_low[...])
+    summed = rows[...].reshape(2 * quarter, width) + projected
+    mean = jnp.sum(summed, axis=-1, keepdims=True) / width
+    second = jnp.sum(summed * summed, axis=-1, keepdims=True) / width
+    inverse = lax.rsqrt(second - mean * mean + EPS)
+    normed = (summed - mean) * inverse
+    up = jnp.concatenate([upstream[...], upstream[...]], axis=0)
+    up_mean = jnp.sum(up, axis=-1, keepdims=True) / width
+    up_dot = jnp.sum(up * normed, axis=-1, keepdims=True) / width
+    direct = inverse * (up - up_mean - normed * up_dot)
+    direct_sum[...] = direct[:quarter] + direct[quarter:]
+    d_high, d_low = halves(direct)
+    grad[...] = mm(d_high, w_high[...]) + mm(d_low, w_high[...]) + mm(d_high, w_low[...])
+    for k, g in enumerate((g0, g1, g2, g3)):
+        at = pl.ds(pl.multiple_of(lax.rem(z + k, n) * feats, feats), feats)
+        for s in range(2):
+            g[s] = grad[s * quarter : (s + 1) * quarter, at]
+
+
+def input_kernel(z_ref, w3, grads, direct_sum, f0, f1, f2, f3):
+    z = z_ref[0]
+    n = 4
+    quarter, width = direct_sum.shape
+    feats = width // n
+    g = jnp.concatenate([grads[2 * h] + grads[2 * h + 1] for h in range(n)], axis=0).T
+    g_high, g_low = halves(g)
+    mine = pl.ds(pl.multiple_of(z * quarter, quarter), quarter)
+    for k, f in enumerate((f0, f1, f2, f3)):
+        column = lax.rem(z + k, n) * feats
+        at = pl.ds(pl.multiple_of(column, feats), feats)
+        w_high = w3[:, at]
+        w_low = w3[:, pl.ds(pl.multiple_of(width + column, feats), feats)]
+        f[...] = mm(g_high, w_high) + mm(g_low, w_high) + mm(g_high, w_low)
+        f[mine, :] += direct_sum[:, at]
+
+
+HD = 64
+NBLOCKS = 16
+SCALE = 1.0 / math.sqrt(HD)
+
+
+def shape(dims, kind=F32):
+    return jax.ShapeDtypeStruct(dims, kind)
+
+
+def shards(packets, baseline, w_query, w_key, w_value, w_out, gain, probe, sessions, block_lists):
+    tokens, feats = packets.shape
+    width = w_query.shape[1]
+    n = lax.axis_size("head")
+    heads = feats // HD
+    members = lax.axis_size("ctx")
+    quarter = tokens // n
+    z = lax.axis_index("head")
+    z_ref = z.reshape(1)
+    slab = feats // members
+    part = 3 * HD
+
+    travel = packets - baseline
+    own = [baseline + alpha * travel for alpha in ALPHAS]
+    ups, downs = [own], [own]
+    for step in range(1, n):
+        ups.append([shift(x, 1, step - 1, n - 2) for x in ups[-1]])
+        downs.append([shift(x, -1, 1, n - step) for x in downs[-1]])
+
+    lists = lax.all_gather(block_lists, "ctx", axis=0, tiled=True)
+    slab_rows = lax.dynamic_slice_in_dim(w_out, lax.axis_index("ctx") * slab, slab, 0)
+    whole_out = lax.all_gather(slab_rows, ("head", "ctx"), axis=0, tiled=True)
+    out_high, out_low = halves_outside(whole_out)
+    weights = jnp.concatenate(
+        [w.reshape(heads, HD, width) for w in (w_query, w_key, w_value)], axis=1
+    ).reshape(heads * part, width)
+    high, low = halves_outside(weights)
+    w3 = jnp.concatenate([high, low, high], axis=1)
+
+    upstream = probe * gain
+    up_pieces = exchange(
+        [
+            lax.dynamic_slice_in_dim(upstream, lax.rem(z + k, n) * quarter, quarter, 0)
+            for k in range(n)
+        ]
+    )
+
+    received = [x for group in (ups[1:], downs[1:]) for pair in group for x in pair]
+    qkv, rows = call(
+        project_kernel,
+        (shape((members, part, tokens)), shape((2, quarter, width))),
+        [pltpu.VMEM((2 * tokens, 3 * width), BF16)],
+        1, z_ref, w3, own[0], own[1], *received,
+    )
+    qkv = lax.all_to_all(qkv, "ctx", 0, 0, tiled=True)
+
+    blocks = members * tokens // BLK
+    session_row = sessions.reshape(blocks, BLK)
+    session_col = sessions.reshape(blocks, BLK, 1)
+    mixed, p_high, p_low = call(
+        attend_kernel,
+        (
+            shape((members, HD, tokens)),
+            shape((blocks, KVB * BLK, BLK), BF16),
+            shape((blocks, KVB * BLK, BLK), BF16),
+        ),
+        [
+            pltpu.VMEM((blocks, part, BLK), BF16),
+            pltpu.VMEM((blocks, BLK, part), BF16),
+            pltpu.VMEM((blocks, 2 * HD, BLK), BF16),
+        ],
+        1, lists, session_col, session_row, qkv,
+    )
+    arrived = lax.all_to_all(mixed, "ctx", 0, 0, tiled=True)
+    pieces = call(
+        to_tokens_kernel,
+        (shape((2, quarter, feats)),) * n,
+        [pltpu.VMEM((2, tokens, feats), F32)],
+        1, z_ref, arrived,
+    )
+    pieces = exchange(pieces)
+    *grads, direct_sum = call(
+        norm_kernel,
+        (shape((2, quarter, feats)),) * n + (shape((quarter, width)),),
+        [
+            pltpu.VMEM((2 * quarter, width), F32),
+            pltpu.VMEM((quarter, width), F32),
+            pltpu.VMEM((2 * quarter, width), F32),
+        ],
+        1, z_ref, out_high, out_low, rows, *up_pieces, *pieces,
+    )
+    grads = exchange(grads)
+    grad = call(
+        to_heads_kernel,
+        shape((members, HD, tokens)),
+        [pltpu.VMEM((2, tokens, feats), F32)],
+        1, z_ref, *grads,
+    )
+    grad = lax.all_to_all(grad, "ctx", 0, 0, tiled=True)
+    grad_qkv = call(
+        attend_back_kernel,
+        shape((members, part, tokens)),
+        [
+            pltpu.VMEM((blocks, 2 * HD, BLK), BF16),
+            pltpu.VMEM((blocks, 2 * HD, BLK), BF16),
+            pltpu.VMEM((blocks, BLK, part), BF16),
+            pltpu.VMEM((blocks, 2 * HD, BLK), F32),
+        ],
+        1, lists, qkv, p_high, p_low, grad, mixed,
+    )
+    grad_qkv = lax.all_to_all(grad_qkv, "ctx", 0, 0, tiled=True)
+    totals = exchange(
+        call(
+            input_kernel,
+            (shape((tokens, feats)),) * n,
+            [],
+            1, z_ref, w3, grad_qkv, direct_sum,
+        )
+    )
+    return travel * (totals[0] + totals[1] + totals[2] + totals[3]) / len(ALPHAS)
+
+
+def pick_shards(mesh):
+    members, n = mesh.shape["ctx"], mesh.shape["head"]
+    return shards if n == 4 and members == 2 * HEADS // n else general_shards
+
+
 def solution(mesh):
     return jax.shard_map(
-        shards,
+        pick_shards(mesh),
         mesh=mesh,
         in_specs=(
             P("ctx", "head"),

time: 545 us -> 251 us (0.46); the launches traced: 535 us -> 247 us
  waiting for transfers between devices: 206 us -> 48.1 us
  local copies, waits for them, and re-layouts: 123 us -> 9.46 us
  matrix products: 94.5 us -> 0 us
  blocking collectives: 18.8 us -> 59.9 us
  Pallas kernels: 0 us -> 40.8 us
    dot_general x22 -> x0, matrix products: 94.5 us -> none  [the longest x2 16 us: integrate(): jnp.einsum('ste,ed->std', grad_qkv, weights_qkv, precision=HIGHEST)]
    reduce_scatter x4 -> x0, waiting for transfers between devices: 92.6 us -> none  [the longest x2 50.2 us: integrate(): lax.psum_scatter(partial_heads, 'head', scatter_dimension=2, tiled=True)]
    all_gather x4 -> x1, waiting for transfers between devices: 75.2 us -> 0.02 us  [shards(): whole_out = lax.all_gather(slab_rows, ('head', 'ctx'), axis=0, tiled=True)]
    pallas_call x0 -> x7, Pallas kernels: none -> 40.8 us  [call(): pl.pallas_call(kernel, out_shape=outs, in_specs=[SM] * n_smem + [VM] * (l...]
    all_to_all x0 -> x2, blocking collectives: none -> 37.2 us  [the longest x1 23.4 us: shards(): grad_qkv = lax.all_to_all(grad_qkv, 'ctx', 0, 0, tiled=True)]
    another operation x12 -> x0, local copies, waits for them, and re-layouts: 35.5 us -> none
    unnamed x84 -> x38, local copies, waits for them, and re-layouts: 32.9 us -> 6.77 us
    all_gather x0 -> x1, blocking collectives: none -> 22.7 us  [shards(): lists = lax.all_gather(block_lists, 'ctx', axis=0, tiled=True)]
  transfers between devices with their start and end apart: 24 -> 27, of which waited for: 12 -> 11; matrix products, arithmetic and copies ran while one was open for 22% -> 6% of each run, Pallas kernels for 0% -> 8%
where the time goes in v1:
time: 251 us; the launch traced here: 247 us
  starting transfers between devices  61.4 us (24%)
  blocking collectives  59.9 us (24%)
  waiting for transfers between devices  48.1 us (19%)
  Pallas kernels  40.8 us (16%)
  between operations  13.8 us (5%)
  other arithmetic  13.7 us (5%)
  local copies, waits for them, and re-layouts  9.46 us (4%)
    pallas_call x7, Pallas kernels, call(): pl.pallas_call(kernel, out_shape=outs, in_specs=[SM] * n_smem + [VM] * (l...  40.8 us
    ppermute x12, starting transfers between devices, rotate(): return lax.ppermute(x, 'head', [(i, (i + by) % size) for i in range(size)])  33.5 us
    ppermute x12, waiting for transfers between devices, rotate(): return lax.ppermute(x, 'head', [(i, (i + by) % size) for i in range(size)])  25.9 us
    all_to_all x1, blocking collectives, shards(): grad_qkv = lax.all_to_all(grad_qkv, 'ctx', 0, 0, tiled=True)  23.4 us
    all_gather x1, blocking collectives, shards(): lists = lax.all_gather(block_lists, 'ctx', axis=0, tiled=True)  22.7 us
    ppermute x12, waiting for transfers between devices, shift(): return lax.ppermute(x, 'head', [(i, i + by) for i in range(low, high + 1)])  22.1 us
    ppermute x12, starting transfers between devices, shift(): return lax.ppermute(x, 'head', [(i, i + by) for i in range(low, high + 1)])  20.5 us
    all_to_all x1, blocking collectives, shards(): grad = lax.all_to_all(grad, 'ctx', 0, 0, tiled=True)  13.8 us
  transfers between devices with their start and end apart: 27, of which 11 were waited for; matrix products, arithmetic and copies ran while one was open for 6% of the time, Pallas kernels for 8%

profile of v1, /device:TPU:0, one launch (start us, length us, event | category | flops | bytes accessed | tf_op | source)
XLA Modules:
  0.0 247.1 jit_solution(9637718613114367996)
XLA Ops:
  11.9 5.6 %collective-permute-start = (f32[256,256]{1,0:T(8,128)S(1)}, f32[256,256]{1,0:T(8,128)S(1)}, u32[]{:S(2)}, u32[]{:S(2)}) collective-permute-start(f32[256,256]{1,0:T(8,128)S(1)} %multiply_add_fusion.1.own0), channel_id=1, source_target_pairs={{0,1},{1,2},{2,3},{4,5},{5,6},{6,7},{8,9},{9,10},{10,11},{12,13},{... | collective-permute-start | bytes 786440 | tf_op jit(solution)/shard_map/ppermute | solution.py:175
  18.8 4.6 %collective-permute-start.1 = (f32[256,256]{1,0:T(8,128)S(1)}, f32[256,256]{1,0:T(8,128)S(1)}, u32[]{:S(2)}, u32[]{:S(2)}) collective-permute-start(f32[256,256]{1,0:T(8,128)S(1)} %get-tuple-element.41.own1), channel_id=1, source_target_pairs={{0,1},{1,2},{2,3},{4,5},{5,6},{6,7},{8,9},{9,10},{10,11},{12,13},{... | collective-permute-start | bytes 786440 | tf_op jit(solution)/shard_map/ppermute | solution.py:175
  23.4 2.3 pad_maximum_fusion.1
  32.5 5.1 %collective-permute-done.8.rest_8_ = f32[256,256]{1,0:T(8,128)S(1)} collective-permute-done((f32[256,256]{1,0:T(8,128)S(1)}, f32[256,256]{1,0:T(8,128)S(1)}, u32[]{:S(2)}, u32[]{:S(2)}) %collective-permute-start.8) | collective-permute-done | bytes 262176 | tf_op jit(solution)/shard_map/ppermute | solution.py:175
  39.6 5.8 %collective-permute-done.9.rest_9_ = f32[256,256]{1,0:T(8,128)S(1)} collective-permute-done((f32[256,256]{1,0:T(8,128)S(1)}, f32[256,256]{1,0:T(8,128)S(1)}, u32[]{:S(2)}, u32[]{:S(2)}) %collective-permute-start.9) | collective-permute-done | bytes 262176 | tf_op jit(solution)/shard_map/ppermute | solution.py:175
  47.4 2.4 pad_maximum_fusion.w3
  49.8 4.7 %collective-permute-done.10.rest_10_ = f32[256,256]{1,0:T(8,128)S(1)} collective-permute-done((f32[256,256]{1,0:T(8,128)S(1)}, f32[256,256]{1,0:T(8,128)S(1)}, u32[]{:S(2)}, u32[]{:S(2)}) %collective-permute-start.10) | collective-permute-done | bytes 262176 | tf_op jit(solution)/shard_map/ppermute | solution.py:175
  54.5 4.3 %collective-permute-done.11.rest_11_ = f32[256,256]{1,0:T(8,128)S(1)} collective-permute-done((f32[256,256]{1,0:T(8,128)S(1)}, f32[256,256]{1,0:T(8,128)S(1)}, u32[]{:S(2)}, u32[]{:S(2)}) %collective-permute-start.11) | collective-permute-done | bytes 262176 | tf_op jit(solution)/shard_map/ppermute | solution.py:175
  58.9 6.9 %shard_map.100 = (f32[8,192,256]{2,1,0:T(8,128)S(1)}, f32[2,64,1024]{2,1,0:T(8,128)S(1)}) custom-call(s32[1]{0:T(128)} %bitcast.z_ref, bf16[768,3072]{1,0:T(8,128)(2,1)} %pad_maximum_fusion.w3, f32[256,256]{1,0:T(8,128)S(1)} %multiply_add_fusion.1.own0, f32[256,256]{1,0:T(8,128)S(1)} %get-tuple-element.41.own1, f32[256,256]{1,0:T(8,128)S(1)} %copy-done.9, ...), custom_call_target="tpu_custom_call" | custom-call | tf_op jit(solution)/shard_map/pallas_call | solution.py:164
  67.7 3.8 %all-to-all-start = ((f32[8,192,256]{2,1,0:T(8,128)}), f32[8,192,256]{2,1,0:T(8,128)S(1)}, u32[]{:S(2)}, u32[]{:S(2)}) async-start(f32[8,192,256]{2,1,0:T(8,128)} %copy-done.5), calls=%async_computation | async-start | bytes 3145728 | tf_op jit(solution)/shard_map/all_to_all | solution.py:425
  72.9 22.7 %all-gather = s32[8,2,5]{2,1,0:T(2,128)S(1)} all-gather(s32[1,2,5]{2,1,0:T(2,128)S(1)} %bitcast.18), channel_id=1, replica_groups=mesh['ctx'=8,'head'=4] {'ctx'}, dimensions={0}, use_global_device_ids=true | all-gather | bytes 360 | tf_op jit(solution)/shard_map/all_gather | solution.py:400
  96.8 10.9 %shard_map.101 = (f32[8,64,256]{2,1,0:T(8,128)S(1)}, bf16[16,640,128]{2,1,0:T(8,128)(2,1)S(1)}, bf16[16,640,128]{2,1,0:T(8,128)(2,1)}) custom-call(s32[16,5]{1,0:T(8,128)S(1)} %bitcast.11, s32[16,128,1]{2,1,0:T(8,128)S(1)} %copy-done.1, s32[16,128]{1,0:T(8,128)S(1)} %bitcast.14, f32[8,192,256]{2,1,0:T(8,128)S(1)} %all-to-all-done.qkv), custom_call_target="tpu_custom_call" | custom-call | tf_op jit(solution)/shard_map/pallas_call | solution.py:164
  107.7 1.5 copy-done.2
  110.0 3.5 %all-to-all-start.1 = ((f32[8,64,256]{2,1,0:T(8,128)}), f32[8,64,256]{2,1,0:T(8,128)S(1)}, u32[]{:S(2)}, u32[]{:S(2)}) async-start(f32[8,64,256]{2,1,0:T(8,128)} %copy-done.3), calls=%async_computation.1 | async-start | bytes 1048576 | tf_op jit(solution)/shard_map/all_to_all | solution.py:444
  115.2 13.7 %collective-permute-start.14 = (f32[64,256]{1,0:T(8,128)}, f32[64,256]{1,0:T(8,128)S(1)}, u32[]{:S(2)}, u32[]{:S(2)}) collective-permute-start(f32[64,256]{1,0:T(8,128)} %get-tuple-element.47), channel_id=1, source_target_pairs={{0,3},{1,0},{2,1},{3,2},{4,7},{5,4},{6,5},{7,6},{8,11},{9,8},{10,9... | collective-permute-start | bytes 196616 | tf_op jit(solution)/shard_map/ppermute | solution.py:180
  130.5 2.9 %collective-permute-start.15 = (f32[2,64,256]{2,1,0:T(8,128)}, f32[2,64,256]{2,1,0:T(8,128)S(1)}, u32[]{:S(2)}, u32[]{:S(2)}) collective-permute-start(f32[2,64,256]{2,1,0:T(8,128)} %get-tuple-element.29), channel_id=1, source_target_pairs={{0,1},{1,2},{2,3},{3,0},{4,5},{5,6},{6,7},{7,4},{8,9},{9,10},{10,1... | collective-permute-start | bytes 393224 | tf_op jit(solution)/shard_map/ppermute | solution.py:180
  133.4 5.0 %collective-permute-start.16 = (f32[2,64,256]{2,1,0:T(8,128)}, f32[2,64,256]{2,1,0:T(8,128)}, u32[]{:S(2)}, u32[]{:S(2)}) collective-permute-start(f32[2,64,256]{2,1,0:T(8,128)} %get-tuple-element.30), channel_id=1, source_target_pairs={{0,2},{1,3},{2,0},{3,1},{4,6},{5,7},{6,4},{7,5},{8,10},{9,11},{10,... | collective-permute-start | bytes 393224 | tf_op jit(solution)/shard_map/ppermute | solution.py:180
  138.5 4.5 %fusion = (bf16[1024,1024]{1,0:T(8,128)(2,1)}, bf16[1024,1024]{1,0:T(8,128)(2,1)S(1)}) fusion(f32[1024,1024]{1,0:T(8,128)} %all-gather.3.cloned.1.call-done), kind=kLoop, calls=%fused_computation.5 | loop fusion | flops 4194304 | bytes 8388608 | tf_op jit(solution)/shard_map/convert_element_type | solution.py:152
  142.9 2.8 %collective-permute-done.16.m2 = f32[2,64,256]{2,1,0:T(8,128)} collective-permute-done((f32[2,64,256]{2,1,0:T(8,128)}, f32[2,64,256]{2,1,0:T(8,128)}, u32[]{:S(2)}, u32[]{:S(2)}) %collective-permute-start.16) | collective-permute-done | bytes 131104 | tf_op jit(solution)/shard_map/ppermute | solution.py:180
  145.7 5.2 %shard_map.103 = (f32[2,64,256]{2,1,0:T(8,128)S(1)}, f32[2,64,256]{2,1,0:T(8,128)S(1)}, f32[2,64,256]{2,1,0:T(8,128)S(1)}, f32[2,64,256]{2,1,0:T(8,128)S(1)}, f32[64,1024]{1,0:T(8,128)S(1)}) custom-call(s32[1]{0:T(128)} %bitcast.z_ref, bf16[1024,1024]{1,0:T(8,128)(2,1)S(1)} %get-tuple-element.44.w_high, bf16[1024,1024]{1,0:T(8,128)(2,1)} %get-tuple-element.43.w_low, ...), custom_call_target="tpu_custom_call" | custom-call | tf_op jit(solution)/shard_map/pallas_call | solution.py:164
  150.9 3.1 %collective-permute-start.18 = (f32[2,64,256]{2,1,0:T(8,128)S(1)}, f32[2,64,256]{2,1,0:T(8,128)S(1)}, u32[]{:S(2)}, u32[]{:S(2)}) collective-permute-start(f32[2,64,256]{2,1,0:T(8,128)S(1)} %get-tuple-element.33), channel_id=1, source_target_pairs={{0,1},{1,2},{2,3},{3,0},{4,5},{5,6},{6,7},{7,4},{8,9},{9,10},{10,1... | collective-permute-start | bytes 393224 | tf_op jit(solution)/shard_map/ppermute | solution.py:180
  154.0 1.7 collective-permute-start.19
  156.5 3.1 %collective-permute-done.18.g1 = f32[2,64,256]{2,1,0:T(8,128)S(1)} collective-permute-done((f32[2,64,256]{2,1,0:T(8,128)S(1)}, f32[2,64,256]{2,1,0:T(8,128)S(1)}, u32[]{:S(2)}, u32[]{:S(2)}) %collective-permute-start.18) | collective-permute-done | bytes 131104 | tf_op jit(solution)/shard_map/ppermute | solution.py:180
  159.6 4.3 %collective-permute-done.19.g2 = f32[2,64,256]{2,1,0:T(8,128)S(1)} collective-permute-done((f32[2,64,256]{2,1,0:T(8,128)S(1)}, f32[2,64,256]{2,1,0:T(8,128)S(1)}, u32[]{:S(2)}, u32[]{:S(2)}) %collective-permute-start.19) | collective-permute-done | bytes 131104 | tf_op jit(solution)/shard_map/ppermute | solution.py:180
  164.1 13.8 %all_to_all.20.grad = f32[8,64,256]{2,1,0:T(8,128)S(1)} all-to-all(f32[8,64,256]{2,1,0:T(8,128)S(1)} %shard_map.104), channel_id=1, replica_groups=mesh['ctx'=8,'head'=4] {'ctx'}, dimensions={0} | all-to-all | bytes 1048576 | tf_op jit(solution)/shard_map/all_to_all | solution.py:469
  177.9 12.7 %shard_map.105 = f32[8,192,256]{2,1,0:T(8,128)S(1)} custom-call(s32[16,5]{1,0:T(8,128)S(1)} %bitcast.12, f32[8,192,256]{2,1,0:T(8,128)S(1)} %all-to-all-done.qkv, bf16[16,640,128]{2,1,0:T(8,128)(2,1)} %copy-done.2, bf16[16,640,128]{2,1,0:T(8,128)(2,1)} %get-tuple-element.25.p_low, f32[8,64,256]{2,1,0:T(8,128)S(1)} %all_to_all.20.grad, ...), custom_call_target="tpu_custom_call" | custom-call | tf_op jit(solution)/shard_map/pallas_call | solution.py:164
  190.6 23.4 %all_to_all.21.grads = f32[8,192,256]{2,1,0:T(8,128)S(1)} all-to-all(f32[8,192,256]{2,1,0:T(8,128)S(1)} %shard_map.105), channel_id=1, replica_groups=mesh['ctx'=8,'head'=4] {'ctx'}, dimensions={0} | all-to-all | bytes 3145728 | tf_op jit(solution)/shard_map/all_to_all | solution.py:481
  214.1 3.9 %shard_map.106 = (f32[256,256]{1,0:T(8,128)S(1)}, f32[256,256]{1,0:T(8,128)S(1)}, f32[256,256]{1,0:T(8,128)S(1)}, f32[256,256]{1,0:T(8,128)S(1)}) custom-call(s32[1]{0:T(128)} %bitcast.z_ref, bf16[768,3072]{1,0:T(8,128)(2,1)} %pad_maximum_fusion.w3, f32[8,192,256]{2,1,0:T(8,128)S(1)} %all_to_all.21.grads, f32[64,1024]{1,0:T(8,128)S(1)} %get-tuple-element.36.direct_sum), custom_call_target="tpu_custom_call" | custom-call | tf_op jit(solution)/shard_map/pallas_call | solution.py:164
  217.9 3.3 %collective-permute-start.21 = (f32[256,256]{1,0:T(8,128)S(1)}, f32[256,256]{1,0:T(8,128)S(1)}, u32[]{:S(2)}, u32[]{:S(2)}) collective-permute-start(f32[256,256]{1,0:T(8,128)S(1)} %get-tuple-element.38), channel_id=1, source_target_pairs={{0,1},{1,2},{2,3},{3,0},{4,5},{5,6},{6,7},{7,4},{8,9},{9,10},{10,1... | collective-permute-start | bytes 786440 | tf_op jit(solution)/shard_map/ppermute | solution.py:180
  221.3 1.7 collective-permute-start.22
  223.7 6.1 %collective-permute-done.21 = f32[256,256]{1,0:T(8,128)S(1)} collective-permute-done((f32[256,256]{1,0:T(8,128)S(1)}, f32[256,256]{1,0:T(8,128)S(1)}, u32[]{:S(2)}, u32[]{:S(2)}) %collective-permute-start.21) | collective-permute-done | bytes 262176 | tf_op jit(solution)/shard_map/ppermute | solution.py:180
  229.8 9.7 %collective-permute-done.22 = f32[256,256]{1,0:T(8,128)S(1)} collective-permute-done((f32[256,256]{1,0:T(8,128)S(1)}, f32[256,256]{1,0:T(8,128)S(1)}, u32[]{:S(2)}, u32[]{:S(2)}) %collective-permute-start.22) | collective-permute-done | bytes 262176 | tf_op jit(solution)/shard_map/ppermute | solution.py:180
  (82 shorter events, 28.4 us)
Async XLA Ops:
  6.5 131.9 %all-gather.3.cloned.1.call-start = ((), (), s32[]{:S(2)}) async-start(), calls=%async_computation.4 | async-start | bytes 4325376 | tf_op jit(solution)/shard_map/all_gather | solution.py:402
  10.6 15.0 %collective-permute-start.6 = (f32[256,256]{1,0:T(8,128)S(1)}, f32[256,256]{1,0:T(8,128)S(1)}, u32[]{:S(2)}, u32[]{:S(2)}) collective-permute-start(f32[256,256]{1,0:T(8,128)S(1)} %multiply_add_fusion.1.own0), channel_id=1, source_target_pairs={{1,0},{2,1},{3,2},{5,4},{6,5},{7,6},{9,8},{10,9},{11,10},{13,12},{... | collective-permute-start | bytes 786440 | tf_op jit(solution)/shard_map/ppermute | solution.py:175
  11.9 15.0 %collective-permute-start = (f32[256,256]{1,0:T(8,128)S(1)}, f32[256,256]{1,0:T(8,128)S(1)}, u32[]{:S(2)}, u32[]{:S(2)}) collective-permute-start(f32[256,256]{1,0:T(8,128)S(1)} %multiply_add_fusion.1.own0), channel_id=1, source_target_pairs={{0,1},{1,2},{2,3},{4,5},{5,6},{6,7},{8,9},{9,10},{10,11},{12,13},{... | collective-permute-start | bytes 786440 | tf_op jit(solution)/shard_map/ppermute | solution.py:175
  17.5 11.0 %collective-permute-start.7 = (f32[256,256]{1,0:T(8,128)S(1)}, f32[256,256]{1,0:T(8,128)S(1)}, u32[]{:S(2)}, u32[]{:S(2)}) collective-permute-start(f32[256,256]{1,0:T(8,128)S(1)} %get-tuple-element.41.own1), channel_id=1, source_target_pairs={{1,0},{2,1},{3,2},{5,4},{6,5},{7,6},{9,8},{10,9},{11,10},{13,12},{... | collective-permute-start | bytes 786440 | tf_op jit(solution)/shard_map/ppermute | solution.py:175
  18.8 12.3 %collective-permute-start.1 = (f32[256,256]{1,0:T(8,128)S(1)}, f32[256,256]{1,0:T(8,128)S(1)}, u32[]{:S(2)}, u32[]{:S(2)}) collective-permute-start(f32[256,256]{1,0:T(8,128)S(1)} %get-tuple-element.41.own1), channel_id=1, source_target_pairs={{0,1},{1,2},{2,3},{4,5},{5,6},{6,7},{8,9},{9,10},{10,11},{12,13},{... | collective-permute-start | bytes 786440 | tf_op jit(solution)/shard_map/ppermute | solution.py:175
  25.7 11.9 %collective-permute-start.8 = (f32[256,256]{1,0:T(8,128)S(1)}, f32[256,256]{1,0:T(8,128)S(1)}, u32[]{:S(2)}, u32[]{:S(2)}) collective-permute-start(f32[256,256]{1,0:T(8,128)S(1)} %collective-permute-done.6.rest_6_), channel_id=1, source_target_pairs={{1,0},{2,1},{5,4},{6,5},{9,8},{10,9},{13,12},{14,13},{17,16},{18,1... | collective-permute-start | bytes 786440 | tf_op jit(solution)/shard_map/ppermute | solution.py:175
  27.0 11.9 %collective-permute-start.2 = (f32[256,256]{1,0:T(8,128)S(1)}, f32[256,256]{1,0:T(8,128)S(1)}, u32[]{:S(2)}, u32[]{:S(2)}) collective-permute-start(f32[256,256]{1,0:T(8,128)S(1)} %collective-permute-done.rest_0_), channel_id=1, source_target_pairs={{1,2},{2,3},{5,6},{6,7},{9,10},{10,11},{13,14},{14,15},{17,18},{18... | collective-permute-start | bytes 786440 | tf_op jit(solution)/shard_map/ppermute | solution.py:175
  28.5 16.8 %collective-permute-start.9 = (f32[256,256]{1,0:T(8,128)S(1)}, f32[256,256]{1,0:T(8,128)S(1)}, u32[]{:S(2)}, u32[]{:S(2)}) collective-permute-start(f32[256,256]{1,0:T(8,128)S(1)} %collective-permute-done.7.rest_7_), channel_id=1, source_target_pairs={{1,0},{2,1},{5,4},{6,5},{9,8},{10,9},{13,12},{14,13},{17,16},{18,1... | collective-permute-start | bytes 786440 | tf_op jit(solution)/shard_map/ppermute | solution.py:175
  31.1 15.5 %collective-permute-start.3 = (f32[256,256]{1,0:T(8,128)S(1)}, f32[256,256]{1,0:T(8,128)S(1)}, u32[]{:S(2)}, u32[]{:S(2)}) collective-permute-start(f32[256,256]{1,0:T(8,128)S(1)} %collective-permute-done.1.rest_1_), channel_id=1, source_target_pairs={{1,2},{2,3},{5,6},{6,7},{9,10},{10,11},{13,14},{14,15},{17,18},{18... | collective-permute-start | bytes 786440 | tf_op jit(solution)/shard_map/ppermute | solution.py:175
  37.6 16.9 %collective-permute-start.10 = (f32[256,256]{1,0:T(8,128)S(1)}, f32[256,256]{1,0:T(8,128)S(1)}, u32[]{:S(2)}, u32[]{:S(2)}) collective-permute-start(f32[256,256]{1,0:T(8,128)S(1)} %collective-permute-done.8.rest_8_), channel_id=1, source_target_pairs={{1,0},{5,4},{9,8},{13,12},{17,16},{21,20},{25,24},{29,28}} | collective-permute-start | bytes 786440 | tf_op jit(solution)/shard_map/ppermute | solution.py:175
  38.9 15.6 %collective-permute-start.4 = (f32[256,256]{1,0:T(8,128)S(1)}, f32[256,256]{1,0:T(8,128)S(1)}, u32[]{:S(2)}, u32[]{:S(2)}) collective-permute-start(f32[256,256]{1,0:T(8,128)S(1)} %collective-permute-done.2.rest_2_), channel_id=1, source_target_pairs={{2,3},{6,7},{10,11},{14,15},{18,19},{22,23},{26,27},{30,31}} | collective-permute-start | bytes 786440 | tf_op jit(solution)/shard_map/ppermute | solution.py:175
  45.4 13.5 %collective-permute-start.11 = (f32[256,256]{1,0:T(8,128)S(1)}, f32[256,256]{1,0:T(8,128)S(1)}, u32[]{:S(2)}, u32[]{:S(2)}) collective-permute-start(f32[256,256]{1,0:T(8,128)S(1)} %collective-permute-done.9.rest_9_), channel_id=1, source_target_pairs={{1,0},{5,4},{9,8},{13,12},{17,16},{21,20},{25,24},{29,28}} | collective-permute-start | bytes 786440 | tf_op jit(solution)/shard_map/ppermute | solution.py:175
  46.7 12.2 %collective-permute-start.5 = (f32[256,256]{1,0:T(8,128)S(1)}, f32[256,256]{1,0:T(8,128)S(1)}, u32[]{:S(2)}, u32[]{:S(2)}) collective-permute-start(f32[256,256]{1,0:T(8,128)S(1)} %collective-permute-done.3.rest_3_), channel_id=1, source_target_pairs={{2,3},{6,7},{10,11},{14,15},{18,19},{22,23},{26,27},{30,31}} | collective-permute-start | bytes 786440 | tf_op jit(solution)/shard_map/ppermute | solution.py:175
  47.3 11.5 %copy-start.9 = (f32[256,256]{1,0:T(8,128)S(1)}, f32[256,256]{1,0:T(8,128)}, u32[]{:S(2)}) copy-start(f32[256,256]{1,0:T(8,128)} %copy-done.8) | copy-start | bytes 786436
  47.4 11.5 %copy-start.11 = (f32[256,256]{1,0:T(8,128)S(1)}, f32[256,256]{1,0:T(8,128)}, u32[]{:S(2)}) copy-start(f32[256,256]{1,0:T(8,128)} %copy-done.10) | copy-start | bytes 786436
  67.7 27.9 %all-to-all-start = ((f32[8,192,256]{2,1,0:T(8,128)}), f32[8,192,256]{2,1,0:T(8,128)S(1)}, u32[]{:S(2)}, u32[]{:S(2)}) async-start(f32[8,192,256]{2,1,0:T(8,128)} %copy-done.5), calls=%async_computation | async-start | bytes 3145728 | tf_op jit(solution)/shard_map/all_to_all | solution.py:425
  71.5 42.0 %copy-start.17 = (f32[256]{0:T(256)S(1)}, f32[256]{0:T(256)}, u32[]{:S(2)}) copy-start(f32[256]{0:T(256)} %param.16) | copy-start | bytes 3076
  110.0 19.4 %all-to-all-start.1 = ((f32[8,64,256]{2,1,0:T(8,128)}), f32[8,64,256]{2,1,0:T(8,128)S(1)}, u32[]{:S(2)}, u32[]{:S(2)}) async-start(f32[8,64,256]{2,1,0:T(8,128)} %copy-done.3), calls=%async_computation.1 | async-start | bytes 1048576 | tf_op jit(solution)/shard_map/all_to_all | solution.py:444
  115.2 23.2 %collective-permute-start.14 = (f32[64,256]{1,0:T(8,128)}, f32[64,256]{1,0:T(8,128)S(1)}, u32[]{:S(2)}, u32[]{:S(2)}) collective-permute-start(f32[64,256]{1,0:T(8,128)} %get-tuple-element.47), channel_id=1, source_target_pairs={{0,3},{1,0},{2,1},{3,2},{4,7},{5,4},{6,5},{7,6},{8,11},{9,8},{10,9... | collective-permute-start | bytes 196616 | tf_op jit(solution)/shard_map/ppermute | solution.py:180
  128.9 14.0 %collective-permute-start.13 = (f32[64,256]{1,0:T(8,128)}, f32[64,256]{1,0:T(8,128)}, u32[]{:S(2)}, u32[]{:S(2)}) collective-permute-start(f32[64,256]{1,0:T(8,128)} %get-tuple-element.48), channel_id=1, source_target_pairs={{0,2},{1,3},{2,0},{3,1},{4,6},{5,7},{6,4},{7,5},{8,10},{9,11},{10,... | collective-permute-start | bytes 196616 | tf_op jit(solution)/shard_map/ppermute | solution.py:180
  128.9 14.0 %collective-permute-start.12 = (f32[64,256]{1,0:T(8,128)}, f32[64,256]{1,0:T(8,128)}, u32[]{:S(2)}, u32[]{:S(2)}) collective-permute-start(f32[64,256]{1,0:T(8,128)} %get-tuple-element.49), channel_id=1, source_target_pairs={{0,1},{1,2},{2,3},{3,0},{4,5},{5,6},{6,7},{7,4},{8,9},{9,10},{10,1... | collective-permute-start | bytes 196616 | tf_op jit(solution)/shard_map/ppermute | solution.py:180
  130.5 12.5 %collective-permute-start.15 = (f32[2,64,256]{2,1,0:T(8,128)}, f32[2,64,256]{2,1,0:T(8,128)S(1)}, u32[]{:S(2)}, u32[]{:S(2)}) collective-permute-start(f32[2,64,256]{2,1,0:T(8,128)} %get-tuple-element.29), channel_id=1, source_target_pairs={{0,1},{1,2},{2,3},{3,0},{4,5},{5,6},{6,7},{7,4},{8,9},{9,10},{10,1... | collective-permute-start | bytes 393224 | tf_op jit(solution)/shard_map/ppermute | solution.py:180
  133.4 12.3 %collective-permute-start.16 = (f32[2,64,256]{2,1,0:T(8,128)}, f32[2,64,256]{2,1,0:T(8,128)}, u32[]{:S(2)}, u32[]{:S(2)}) collective-permute-start(f32[2,64,256]{2,1,0:T(8,128)} %get-tuple-element.30), channel_id=1, source_target_pairs={{0,2},{1,3},{2,0},{3,1},{4,6},{5,7},{6,4},{7,5},{8,10},{9,11},{10,... | collective-permute-start | bytes 393224 | tf_op jit(solution)/shard_map/ppermute | solution.py:180
  138.4 7.3 %collective-permute-start.17 = (f32[2,64,256]{2,1,0:T(8,128)}, f32[2,64,256]{2,1,0:T(8,128)}, u32[]{:S(2)}, u32[]{:S(2)}) collective-permute-start(f32[2,64,256]{2,1,0:T(8,128)} %get-tuple-element.31), channel_id=1, source_target_pairs={{0,3},{1,0},{2,1},{3,2},{4,7},{5,4},{6,5},{7,6},{8,11},{9,8},{10,9... | collective-permute-start | bytes 393224 | tf_op jit(solution)/shard_map/ppermute | solution.py:180
  145.7 32.2 %copy-start.4 = (f32[8,64,256]{2,1,0:T(8,128)S(1)}, f32[8,64,256]{2,1,0:T(8,128)}, u32[]{:S(2)}) copy-start(f32[8,64,256]{2,1,0:T(8,128)} %copy-done.3) | copy-start | bytes 1572868
  150.9 8.6 %collective-permute-start.18 = (f32[2,64,256]{2,1,0:T(8,128)S(1)}, f32[2,64,256]{2,1,0:T(8,128)S(1)}, u32[]{:S(2)}, u32[]{:S(2)}) collective-permute-start(f32[2,64,256]{2,1,0:T(8,128)S(1)} %get-tuple-element.33), channel_id=1, source_target_pairs={{0,1},{1,2},{2,3},{3,0},{4,5},{5,6},{6,7},{7,4},{8,9},{9,10},{10,1... | collective-permute-start | bytes 393224 | tf_op jit(solution)/shard_map/ppermute | solution.py:180
  154.0 9.8 %collective-permute-start.19 = (f32[2,64,256]{2,1,0:T(8,128)S(1)}, f32[2,64,256]{2,1,0:T(8,128)S(1)}, u32[]{:S(2)}, u32[]{:S(2)}) collective-permute-start(f32[2,64,256]{2,1,0:T(8,128)S(1)} %get-tuple-element.34), channel_id=1, source_target_pairs={{0,2},{1,3},{2,0},{3,1},{4,6},{5,7},{6,4},{7,5},{8,10},{9,11},{10,... | collective-permute-start | bytes 393224 | tf_op jit(solution)/shard_map/ppermute | solution.py:180
  155.8 8.1 %collective-permute-start.20 = (f32[2,64,256]{2,1,0:T(8,128)S(1)}, f32[2,64,256]{2,1,0:T(8,128)S(1)}, u32[]{:S(2)}, u32[]{:S(2)}) collective-permute-start(f32[2,64,256]{2,1,0:T(8,128)S(1)} %get-tuple-element.35), channel_id=1, source_target_pairs={{0,3},{1,0},{2,1},{3,2},{4,7},{5,4},{6,5},{7,6},{8,11},{9,8},{10,9... | collective-permute-start | bytes 393224 | tf_op jit(solution)/shard_map/ppermute | solution.py:180
  214.1 25.4 %copy-start.16 = (f32[256,256]{1,0:T(8,128)S(1)}, f32[256,256]{1,0:T(8,128)}, u32[]{:S(2)}) copy-start(f32[256,256]{1,0:T(8,128)} %copy-done.15) | copy-start | bytes 786436
  217.9 11.9 %collective-permute-start.21 = (f32[256,256]{1,0:T(8,128)S(1)}, f32[256,256]{1,0:T(8,128)S(1)}, u32[]{:S(2)}, u32[]{:S(2)}) collective-permute-start(f32[256,256]{1,0:T(8,128)S(1)} %get-tuple-element.38), channel_id=1, source_target_pairs={{0,1},{1,2},{2,3},{3,0},{4,5},{5,6},{6,7},{7,4},{8,9},{9,10},{10,1... | collective-permute-start | bytes 786440 | tf_op jit(solution)/shard_map/ppermute | solution.py:180
  221.3 18.2 %collective-permute-start.22 = (f32[256,256]{1,0:T(8,128)S(1)}, f32[256,256]{1,0:T(8,128)S(1)}, u32[]{:S(2)}, u32[]{:S(2)}) collective-permute-start(f32[256,256]{1,0:T(8,128)S(1)} %get-tuple-element.39), channel_id=1, source_target_pairs={{0,2},{1,3},{2,0},{3,1},{4,6},{5,7},{6,4},{7,5},{8,10},{9,11},{10,... | collective-permute-start | bytes 786440 | tf_op jit(solution)/shard_map/ppermute | solution.py:180
  223.0 16.5 %collective-permute-start.23 = (f32[256,256]{1,0:T(8,128)S(1)}, f32[256,256]{1,0:T(8,128)S(1)}, u32[]{:S(2)}, u32[]{:S(2)}) collective-permute-start(f32[256,256]{1,0:T(8,128)S(1)} %get-tuple-element.40), channel_id=1, source_target_pairs={{0,3},{1,0},{2,1},{3,2},{4,7},{5,4},{6,5},{7,6},{8,11},{9,8},{10,9... | collective-permute-start | bytes 786440 | tf_op jit(solution)/shard_map/ppermute | solution.py:180
  (14 other events, 46.4 us)
Sparse Core Ops, SparseCore 0:
  10.2 65.5 all-gather.2

commit v2 on v1

--- a/solution.py
+++ b/solution.py
@@ -1,3 +1,4 @@
+import functools
 import math
 
 import jax
@@ -184,43 +185,53 @@
     return [pieces[0]] + [rotate(pieces[k], k) for k in range(1, len(pieces))]
 
 
-def project_kernel(z_ref, w3, own0, own1, *rest):
-    ups = [rest[0:2], rest[2:4], rest[4:6]]
-    downs = [rest[6:8], rest[8:10], rest[10:12]]
-    out, rows, x3 = rest[12:]
+def project_kernel(z_ref, w3, own, u1, u2, u3, d1, d2, d3, out, rows, x3):
+    ups, downs = (u1, u2, u3), (d1, d2, d3)
     z = z_ref[0]
     n = 4
-    quarter = rows.shape[1]
-    width = rows.shape[2]
-    for s, own in enumerate((own0, own1)):
-        tokens, feats = own.shape
-        for k in range(n):
-            column = lax.rem(z - k + n, n) * feats
-            at = pl.ds(pl.multiple_of(z * quarter, quarter), quarter)
-            if k == 0:
-                x = own[...]
-                mine = own[at, :]
-            else:
-                up, down = ups[k - 1][s], downs[n - k - 1][s]
-                x = up[...] + down[...]
-                mine = up[at, :] + down[at, :]
-            rows[s, :, pl.ds(pl.multiple_of(column, feats), feats)] = mine
-            high, low = halves(x)
-            span = pl.ds(s * tokens, tokens)
-            x3[span, pl.ds(pl.multiple_of(column, feats), feats)] = high
-            x3[span, pl.ds(pl.multiple_of(width + column, feats), feats)] = high
-            x3[span, pl.ds(pl.multiple_of(2 * width + column, feats), feats)] = low
+    quarter, width = rows.shape[1:]
+    both, feats = own.shape
+    tokens = both // 2
+    for k in range(n):
+        column = pl.multiple_of(lax.rem(z - k + n, n) * feats, feats)
+        x = own[...] if k == 0 else ups[k - 1][...] + downs[n - k - 1][...]
+        for s in range(2):
+            t = x[s * tokens : (s + 1) * tokens]
+            rows[s, :, pl.ds(column, feats)] = jnp.where(
+                lax.rem(z, 2) == 0, t[:quarter], t[quarter:]
+            )
+        high, low = halves(x)
+        x3[:, pl.ds(column, feats)] = high
+        x3[:, pl.ds(pl.multiple_of(width + column, feats), feats)] = high
+        x3[:, pl.ds(pl.multiple_of(2 * width + column, feats), feats)] = low
     part = out.shape[1]
-    for s in range(2):
-        for h in range(n):
-            out[2 * h + s] = mm_nt(
-                w3[h * part : (h + 1) * part, :], x3[s * tokens : (s + 1) * tokens, :]
-            )
-
-
-def attend_kernel(lists, session_col, session_row, qkv, mixed, p_high, p_low, q3, k3, v2):
+    for h in range(n):
+        r = mm_nt(w3[h * part : (h + 1) * part, :], x3[...])
+        for s in range(2):
+            out[2 * h + s] = r[:, s * tokens : (s + 1) * tokens]
+
+
+def fold(x):
+    top, bottom = x[: HD // 2], x[HD // 2 :]
+    left = lax.broadcasted_iota(jnp.int32, top.shape, 1) < HD
+    return jnp.where(left, top, pltpu.roll(bottom, HD, 1)), jnp.where(
+        left, pltpu.roll(top, HD, 1), bottom
+    )
+
+
+def unfold(first, second):
+    left = lax.broadcasted_iota(jnp.int32, first.shape, 1) < HD
+    top = jnp.where(left, first, pltpu.roll(second, HD, 1))
+    bottom = jnp.where(left, pltpu.roll(first, HD, 1), second)
+    return jnp.concatenate([top, bottom], axis=0)
+
+
+def attend_kernel(
+    lists, session_col, session_row, qkv0, qkv1, mixed, folded, p_high, p_low, q3, k3, v2
+):
+    qkv = (qkv0, qkv1)
     for b in range(NBLOCKS):
-        t = qkv[b // 2, :, (b % 2) * BLK : (b % 2 + 1) * BLK]
+        t = qkv[b % 2][b // 2]
         q_high, q_low = halves(t[:HD] * SCALE)
         q3[b] = jnp.concatenate([q_high, q_high, q_low], axis=0)
         k_high, k_low = halves(t[HD : 2 * HD].T)
@@ -247,15 +258,20 @@
             p_low[b] = low
             values = jnp.concatenate([v2[lists[b, j]] for j in range(KVB)], axis=1)
             both = mm(values, high)
-            mixed[c, :, e * BLK : (e + 1) * BLK] = both[:HD] + both[HD:] + mm(values[:HD], low)
+            block = both[:HD] + both[HD:] + mm(values[:HD], low)
+            mixed[b] = block
+            folded[4 * c + 2 * e], folded[4 * c + 2 * e + 1] = fold(block)
         return carry
 
     lax.fori_loop(0, NBLOCKS // 2, body, 0)
 
 
-def attend_back_kernel(lists, qkv, p_high, p_low, grad, mixed, out, q2, k2, v3, acc):
+def attend_back_kernel(
+    lists, qkv0, qkv1, p_high, p_low, grad, mixed, out0, out1, q2, k2, v3, acc
+):
+    qkv, out = (qkv0, qkv1), (out0, out1)
     for b in range(NBLOCKS):
-        t = qkv[b // 2, :, (b % 2) * BLK : (b % 2 + 1) * BLK]
+        t = qkv[b % 2][b // 2]
         q_high, q_low = halves(t[:HD])
         q2[b] = jnp.concatenate([q_high, q_low], axis=0)
         k_high, k_low = halves(t[HD : 2 * HD])
@@ -267,9 +283,8 @@
     def body(c, carry):
         for e in range(2):
             b = 2 * c + e
-            lanes = slice(e * BLK, (e + 1) * BLK)
-            g = grad[c, :, lanes]
-            delta = jnp.sum(g * mixed[c, :, lanes], axis=0, keepdims=True)
+            g = unfold(grad[4 * c + 2 * e], grad[4 * c + 2 * e + 1])
+            delta = jnp.sum(g * mixed[b], axis=0, keepdims=True)
             g_high, g_low = halves(g)
             g3 = jnp.concatenate([g_high, g_high, g_low], axis=0)
             g2 = jnp.concatenate([g_high, g_low], axis=0)
@@ -279,7 +294,7 @@
             s_high, s_low = halves(probs * (grad_probs - delta) * SCALE)
             keys = jnp.concatenate([k2[lists[b, j]] for j in range(KVB)], axis=1)
             both = mm(keys, s_high)
-            out[c, 0:HD, lanes] = both[:HD] + both[HD:] + mm(keys[:HD], s_low)
+            out[e][c, 0:HD] = both[:HD] + both[HD:] + mm(keys[:HD], s_low)
             query = q2[b]
             both = mm_nt(query, s_high)
             grad_keys = both[:HD] + both[HD:] + mm_nt(query[:HD], s_low)
@@ -292,49 +307,27 @@
 
     lax.fori_loop(0, NBLOCKS // 2, body, 0)
     for b in range(NBLOCKS):
-        out[b // 2, HD : 3 * HD, (b % 2) * BLK : (b % 2 + 1) * BLK] = acc[b]
-
-
-def to_tokens_kernel(z_ref, mixed, o0, o1, o2, o3, turned):
-    z = z_ref[0]
-    n = 4
-    quarter = o0.shape[1]
-    for s in range(2):
-        turned[s] = jnp.concatenate([mixed[2 * h + s] for h in range(n)], axis=0).T
-    for k, o in enumerate((o0, o1, o2, o3)):
-        start = pl.multiple_of(lax.rem(z + k, n) * quarter, quarter)
-        o[...] = turned[:, pl.ds(start, quarter), :]
-
-
-def to_heads_kernel(z_ref, g0, g1, g2, g3, out, turned):
-    z = z_ref[0]
-    n = 4
-    quarter = g0.shape[1]
-    for k, g in enumerate((g0, g1, g2, g3)):
-        start = pl.multiple_of(lax.rem(z - k + n, n) * quarter, quarter)
-        turned[:, pl.ds(start, quarter), :] = g[...]
-    for s in range(2):
-        t = turned[s].T
-        for h in range(n):
-            out[2 * h + s] = t[h * HD : (h + 1) * HD]
+        out[b % 2][b // 2, HD : 3 * HD] = acc[b]
 
 
 def norm_kernel(
-    z_ref, w_high, w_low, rows, u0, u1, u2, u3, m0, m1, m2, m3,
-    g0, g1, g2, g3, direct_sum, mixed, upstream, grad,
+    z_ref, w_high, w_low, rows0, rows1, u0, u1, u2, u3, pieces, out, direct_sum, upstream, mixed
 ):
     z = z_ref[0]
     n = 4
-    quarter, width = rows.shape[1:]
+    quarter, width = direct_sum.shape
     feats = width // n
-    for k, (u, m) in enumerate(((u0, m0), (u1, m1), (u2, m2), (u3, m3))):
+    for k, u in enumerate((u0, u1, u2, u3)):
         at = pl.ds(pl.multiple_of(lax.rem(z - k + n, n) * feats, feats), feats)
         upstream[:, at] = u[...]
-        for s in range(2):
-            mixed[s * quarter : (s + 1) * quarter, at] = m[s]
-    m_high, m_low = halves(mixed[...])
+    for group in range(n):
+        for h in range(n):
+            at = group * feats + h * HD
+            mixed[at : at + HD, :] = unfold(pieces[2 * h * n + group], pieces[(2 * h + 1) * n + group])
+    m_high, m_low = halves(mixed[...].T)
     projected = mm_nt(m_high, w_high[...]) + mm_nt(m_low, w_high[...]) + mm_nt(m_high, w_low[...])
-    summed = rows[...].reshape(2 * quarter, width) + projected
+    rows = jnp.where(z < 2, rows0[...], rows1[...])
+    summed = rows.reshape(2 * quarter, width) + projected
     mean = jnp.sum(summed, axis=-1, keepdims=True) / width
     second = jnp.sum(summed * summed, axis=-1, keepdims=True) / width
     inverse = lax.rsqrt(second - mean * mean + EPS)
@@ -345,28 +338,30 @@
     direct = inverse * (up - up_mean - normed * up_dot)
     direct_sum[...] = direct[:quarter] + direct[quarter:]
     d_high, d_low = halves(direct)
-    grad[...] = mm(d_high, w_high[...]) + mm(d_low, w_high[...]) + mm(d_high, w_low[...])
-    for k, g in enumerate((g0, g1, g2, g3)):
-        at = pl.ds(pl.multiple_of(lax.rem(z + k, n) * feats, feats), feats)
-        for s in range(2):
-            g[s] = grad[s * quarter : (s + 1) * quarter, at]
-
-
-def input_kernel(z_ref, w3, grads, direct_sum, f0, f1, f2, f3):
+    grad = mm(d_high, w_high[...]) + mm(d_low, w_high[...]) + mm(d_high, w_low[...])
+    grad = grad.T
+    for group in range(n):
+        for h in range(n):
+            at = group * feats + h * HD
+            out[2 * h * n + group], out[(2 * h + 1) * n + group] = fold(grad[at : at + HD])
+
+
+def input_kernel(half, z_ref, w3, grads, direct_sum, f0, f1, f2, f3):
     z = z_ref[0]
     n = 4
     quarter, width = direct_sum.shape
     feats = width // n
     g = jnp.concatenate([grads[2 * h] + grads[2 * h + 1] for h in range(n)], axis=0).T
     g_high, g_low = halves(g)
-    mine = pl.ds(pl.multiple_of(z * quarter, quarter), quarter)
+    mine = pl.ds(pl.multiple_of(lax.rem(z, 2) * quarter, quarter), quarter)
+    here = z // 2 == half
     for k, f in enumerate((f0, f1, f2, f3)):
         column = lax.rem(z + k, n) * feats
         at = pl.ds(pl.multiple_of(column, feats), feats)
         w_high = w3[:, at]
         w_low = w3[:, pl.ds(pl.multiple_of(width + column, feats), feats)]
         f[...] = mm(g_high, w_high) + mm(g_low, w_high) + mm(g_high, w_low)
-        f[mine, :] += direct_sum[:, at]
+        f[mine, :] += jnp.where(here, direct_sum[:, at], 0.0)
 
 
 HD = 64
@@ -391,22 +386,25 @@
     part = 3 * HD
 
     travel = packets - baseline
-    own = [baseline + alpha * travel for alpha in ALPHAS]
-    ups, downs = [own], [own]
-    for step in range(1, n):
-        ups.append([shift(x, 1, step - 1, n - 2) for x in ups[-1]])
-        downs.append([shift(x, -1, 1, n - step) for x in downs[-1]])
-
-    lists = lax.all_gather(block_lists, "ctx", axis=0, tiled=True)
-    slab_rows = lax.dynamic_slice_in_dim(w_out, lax.axis_index("ctx") * slab, slab, 0)
-    whole_out = lax.all_gather(slab_rows, ("head", "ctx"), axis=0, tiled=True)
-    out_high, out_low = halves_outside(whole_out)
+    half = tokens // 2
+    gathered = []
+    for e in range(2):
+        span = slice(e * half, (e + 1) * half)
+        own = jnp.concatenate([baseline[span] + alpha * travel[span] for alpha in ALPHAS])
+        ups, downs = [own], [own]
+        for step in range(1, n):
+            ups.append(shift(ups[-1], 1, step - 1, n - 2))
+            downs.append(shift(downs[-1], -1, 1, n - step))
+        gathered.append([own] + ups[1:] + downs[1:])
+
+    lists = lax.all_to_all(
+        jnp.broadcast_to(block_lists[None], (members,) + block_lists.shape), "ctx", 0, 0, tiled=True
+    ).reshape(-1, KVB)
     weights = jnp.concatenate(
         [w.reshape(heads, HD, width) for w in (w_query, w_key, w_value)], axis=1
     ).reshape(heads * part, width)
     high, low = halves_outside(weights)
     w3 = jnp.concatenate([high, low, high], axis=1)
-
     upstream = probe * gain
     up_pieces = exchange(
         [
@@ -414,23 +412,35 @@
             for k in range(n)
         ]
     )
-
-    received = [x for group in (ups[1:], downs[1:]) for pair in group for x in pair]
-    qkv, rows = call(
-        project_kernel,
-        (shape((members, part, tokens)), shape((2, quarter, width))),
-        [pltpu.VMEM((2 * tokens, 3 * width), BF16)],
-        1, z_ref, w3, own[0], own[1], *received,
-    )
-    qkv = lax.all_to_all(qkv, "ctx", 0, 0, tiled=True)
+    slab_rows = lax.dynamic_slice_in_dim(w_out, lax.axis_index("ctx") * slab, slab, 0)
+
+    gathered[0], w3, lists, slab_rows = lax.optimization_barrier(
+        (gathered[0], w3, lists, slab_rows)
+    )
+    gathered[1], up_pieces = lax.optimization_barrier((gathered[1], up_pieces))
+    whole_out = lax.all_gather(slab_rows, ("head", "ctx"), axis=0, tiled=True)
+    out_high, out_low = halves_outside(whole_out)
+
+    qkv, rows = [], []
+    for e in range(2):
+        projected, own_rows = call(
+            project_kernel,
+            (shape((members, part, half)), shape((2, quarter, width))),
+            [pltpu.VMEM((tokens, 3 * width), BF16)],
+            1, z_ref, w3, *gathered[e],
+        )
+        qkv.append(lax.all_to_all(projected, "ctx", 0, 0, tiled=True))
+        rows.append(own_rows)
 
     blocks = members * tokens // BLK
+    everyone = members * n
     session_row = sessions.reshape(blocks, BLK)
     session_col = sessions.reshape(blocks, BLK, 1)
-    mixed, p_high, p_low = call(
+    mixed, folded, p_high, p_low = call(
         attend_kernel,
         (
-            shape((members, HD, tokens)),
+            shape((blocks, HD, BLK)),
+            shape((everyone, HD // 2, BLK)),
             shape((blocks, KVB * BLK, BLK), BF16),
             shape((blocks, KVB * BLK, BLK), BF16),
         ),
@@ -439,55 +449,40 @@
             pltpu.VMEM((blocks, BLK, part), BF16),
             pltpu.VMEM((blocks, 2 * HD, BLK), BF16),
         ],
-        1, lists, session_col, session_row, qkv,
-    )
-    arrived = lax.all_to_all(mixed, "ctx", 0, 0, tiled=True)
-    pieces = call(
-        to_tokens_kernel,
-        (shape((2, quarter, feats)),) * n,
-        [pltpu.VMEM((2, tokens, feats), F32)],
-        1, z_ref, arrived,
-    )
-    pieces = exchange(pieces)
-    *grads, direct_sum = call(
+        1, lists, session_col, session_row, *qkv,
+    )
+    folded = lax.all_to_all(folded, ("ctx", "head"), 0, 0, tiled=True)
+    grad, direct_sum = call(
         norm_kernel,
-        (shape((2, quarter, feats)),) * n + (shape((quarter, width)),),
-        [
-            pltpu.VMEM((2 * quarter, width), F32),
-            pltpu.VMEM((quarter, width), F32),
-            pltpu.VMEM((2 * quarter, width), F32),
-        ],
-        1, z_ref, out_high, out_low, rows, *up_pieces, *pieces,
-    )
-    grads = exchange(grads)
-    grad = call(
-        to_heads_kernel,
-        shape((members, HD, tokens)),
-        [pltpu.VMEM((2, tokens, feats), F32)],
-        1, z_ref, *grads,
-    )
-    grad = lax.all_to_all(grad, "ctx", 0, 0, tiled=True)
+        (shape((everyone, HD // 2, BLK)), shape((quarter, width))),
+        [pltpu.VMEM((quarter, width), F32), pltpu.VMEM((width, 2 * quarter), F32)],
+        1, z_ref, out_high, out_low, *rows, *up_pieces, folded,
+    )
+    grad = lax.all_to_all(grad, ("ctx", "head"), 0, 0, tiled=True)
     grad_qkv = call(
         attend_back_kernel,
-        shape((members, part, tokens)),
+        (shape((members, part, half)),) * 2,
         [
             pltpu.VMEM((blocks, 2 * HD, BLK), BF16),
             pltpu.VMEM((blocks, 2 * HD, BLK), BF16),
             pltpu.VMEM((blocks, BLK, part), BF16),
             pltpu.VMEM((blocks, 2 * HD, BLK), F32),
         ],
-        1, lists, qkv, p_high, p_low, grad, mixed,
-    )
-    grad_qkv = lax.all_to_all(grad_qkv, "ctx", 0, 0, tiled=True)
-    totals = exchange(
-        call(
-            input_kernel,
-            (shape((tokens, feats)),) * n,
-            [],
-            1, z_ref, w3, grad_qkv, direct_sum,
+        1, lists, *qkv, p_high, p_low, grad, mixed,
+    )
+    grad_qkv = [lax.all_to_all(g, "ctx", 0, 0, tiled=True) for g in grad_qkv]
+    totals = []
+    for e in range(2):
+        parts = exchange(
+            call(
+                functools.partial(input_kernel, e),
+                (shape((half, feats)),) * n,
+                [],
+                1, z_ref, w3, grad_qkv[e], direct_sum,
+            )
         )
-    )
-    return travel * (totals[0] + totals[1] + totals[2] + totals[3]) / len(ALPHAS)
+        totals.append(parts[0] + parts[1] + parts[2] + parts[3])
+    return travel * jnp.concatenate(totals) / len(ALPHAS)
 
 
 def pick_shards(mesh):

time: 251 us -> 249 us (level)
  blocking collectives: 59.9 us -> 34.2 us
  waiting for transfers between devices: 48.1 us -> 59.2 us
  Pallas kernels: 40.8 us -> 49.4 us
  local copies, waits for them, and re-layouts: 9.46 us -> 16.8 us
    all_to_all x2 -> x5, waiting for transfers between devices: 0.01 us -> 26.3 us  [the longest x2 11.2 us: shards(): qkv.append(lax.all_to_all(projected, 'ctx', 0, 0, tiled=True))]
    all_gather x1 -> x0, blocking collectives: 22.7 us -> none  [shards(): lists = lax.all_gather(block_lists, 'ctx', axis=0, tiled=True)]
    ppermute x12 -> x9, starting transfers between devices: 33.5 us -> 16.5 us  [rotate(): return lax.ppermute(x, 'head', [(i, (i + by) % size) for i in range(size)])]
    all_to_all x2 -> x5, starting transfers between devices: 7.31 us -> 21.6 us  [the longest x2 8.34 us: shards(): qkv.append(lax.all_to_all(projected, 'ctx', 0, 0, tiled=True))]
    ppermute x12 -> x9, waiting for transfers between devices: 25.9 us -> 11.7 us  [rotate(): return lax.ppermute(x, 'head', [(i, (i + by) % size) for i in range(size)])]
    pallas_call x7, Pallas kernels: 40.8 us -> 49.4 us  [call(): pl.pallas_call(kernel, out_shape=outs, in_specs=[SM] * n_smem + [VM] * (l...]
    unnamed x38 -> x54, local copies, waits for them, and re-layouts: 6.77 us -> 12.5 us
    all_to_all x2, blocking collectives: 37.2 us -> 34.2 us  [the longest x1 18.3 us: shards(): grad = lax.all_to_all(grad, ('ctx', 'head'), 0, 0, tiled=True)]
  transfers between devices with their start and end apart: 27 -> 27, of which waited for: 11 -> 9; matrix products, arithmetic and copies ran while one was open for 6% -> 6% of each run, Pallas kernels for 8% -> 12%
where the time goes in v2:
time: 249 us; the launch traced here: 247 us
  starting transfers between devices  59.4 us (24%)
  waiting for transfers between devices  59.2 us (24%)
  Pallas kernels  49.4 us (20%)
  blocking collectives  34.2 us (14%)
  local copies, waits for them, and re-layouts  16.8 us (7%)
  other arithmetic  14.5 us (6%)
  between operations  13.8 us (6%)
    pallas_call x7, Pallas kernels, call(): pl.pallas_call(kernel, out_shape=outs, in_specs=[SM] * n_smem + [VM] * (l...  49.4 us
    ppermute x12, starting transfers between devices, shift(): return lax.ppermute(x, 'head', [(i, i + by) for i in range(low, high + 1)])  21.3 us
    ppermute x12, waiting for transfers between devices, shift(): return lax.ppermute(x, 'head', [(i, i + by) for i in range(low, high + 1)])  21.2 us
    all_to_all x1, blocking collectives, shards(): grad = lax.all_to_all(grad, ('ctx', 'head'), 0, 0, tiled=True)  18.3 us
    ppermute x9, starting transfers between devices, rotate(): return lax.ppermute(x, 'head', [(i, (i + by) % size) for i in range(size)])  16.5 us
    all_to_all x1, blocking collectives, shards(): grad_qkv = [lax.all_to_all(g, 'ctx', 0, 0, tiled=True) for g in grad_qkv]  15.9 us
    unnamed x54, local copies, waits for them, and re-layouts  12.5 us
    ppermute x9, waiting for transfers between devices, rotate(): return lax.ppermute(x, 'head', [(i, (i + by) % size) for i in range(size)])  11.7 us
  transfers between devices with their start and end apart: 27, of which 9 were waited for; matrix products, arithmetic and copies ran while one was open for 6% of the time, Pallas kernels for 12%

profile of v2, /device:TPU:0, one launch (start us, length us, event | category | flops | bytes accessed | tf_op | source)
XLA Modules:
  0.0 247.2 jit_solution(15713211017006717901)
XLA Ops:
  10.2 5.6 %collective-permute-start = (f32[256,256]{1,0:T(8,128)S(1)}, f32[256,256]{1,0:T(8,128)S(1)}, u32[]{:S(2)}, u32[]{:S(2)}) collective-permute-start(f32[256,256]{1,0:T(8,128)S(1)} %pad_maximum_fusion.2.own), channel_id=1, source_target_pairs={{0,1},{1,2},{2,3},{4,5},{5,6},{6,7},{8,9},{9,10},{10,11},{12,13},{... | collective-permute-start | bytes 786440 | tf_op jit(solution)/shard_map/ppermute | solution.py:176
  17.0 4.2 %all-to-all-start = ((s32[8,2,5]{2,1,0:T(2,128)}), s32[8,2,5]{2,1,0:T(2,128)S(1)}, u32[]{:S(2)}, u32[]{:S(2)}) async-start(s32[8,2,5]{2,1,0:T(2,128)} %broadcast_in_dim.2), calls=%async_computation | async-start | bytes 16384 | tf_op jit(solution)/shard_map/all_to_all | solution.py:400
  21.2 2.3 pad_maximum_fusion.1
  26.2 7.9 %collective-permute-done.4.d2 = f32[256,256]{1,0:T(8,128)S(1)} collective-permute-done((f32[256,256]{1,0:T(8,128)S(1)}, f32[256,256]{1,0:T(8,128)S(1)}, u32[]{:S(2)}, u32[]{:S(2)}) %collective-permute-start.4) | collective-permute-done | bytes 262176 | tf_op jit(solution)/shard_map/ppermute | solution.py:176
  36.1 2.3 pad_maximum_fusion.w3
  39.1 4.8 %collective-permute-done.5.d3 = f32[256,256]{1,0:T(8,128)S(1)} collective-permute-done((f32[256,256]{1,0:T(8,128)S(1)}, f32[256,256]{1,0:T(8,128)S(1)}, u32[]{:S(2)}, u32[]{:S(2)}) %collective-permute-start.5) | collective-permute-done | bytes 262176 | tf_op jit(solution)/shard_map/ppermute | solution.py:176
  45.9 4.6 %collective-permute-start.6 = (f32[256,256]{1,0:T(8,128)S(1)}, f32[256,256]{1,0:T(8,128)S(1)}, u32[]{:S(2)}, u32[]{:S(2)}) collective-permute-start(f32[256,256]{1,0:T(8,128)S(1)} %pad_maximum_fusion.3.own), channel_id=1, source_target_pairs={{0,1},{1,2},{2,3},{4,5},{5,6},{6,7},{8,9},{9,10},{10,11},{12,13},{... | collective-permute-start | bytes 786440 | tf_op jit(solution)/shard_map/ppermute | solution.py:176
  53.4 5.7 %shard_map.100 = (f32[8,192,128]{2,1,0:T(8,128)}, f32[2,64,1024]{2,1,0:T(8,128)S(1)}) custom-call(s32[1]{0:T(128)} %bitcast.z_ref, bf16[768,3072]{1,0:T(8,128)(2,1)} %pad_maximum_fusion.w3, f32[256,256]{1,0:T(8,128)S(1)} %pad_maximum_fusion.2.own, f32[256,256]{1,0:T(8,128)S(1)} %collective-permute-done.u1, f32[256,256]{1,0:T(8,128)S(1)} %copy-done.14, ...), custom_call_target="tpu_custom_call" | custom-call | tf_op jit(solution)/shard_map/pallas_call | solution.py:165
  59.9 3.5 %all-to-all-start.1 = ((f32[8,192,128]{2,1,0:T(8,128)}), f32[8,192,128]{2,1,0:T(8,128)S(1)}, u32[]{:S(2)}, u32[]{:S(2)}) async-start(f32[8,192,128]{2,1,0:T(8,128)} %get-tuple-element.55), calls=%async_computation.1 | async-start | bytes 1572864 | tf_op jit(solution)/shard_map/all_to_all | solution.py:432
  65.4 8.5 %collective-permute-done.10.d2 = f32[256,256]{1,0:T(8,128)S(1)} collective-permute-done((f32[256,256]{1,0:T(8,128)S(1)}, f32[256,256]{1,0:T(8,128)S(1)}, u32[]{:S(2)}, u32[]{:S(2)}) %collective-permute-start.10) | collective-permute-done | bytes 262176 | tf_op jit(solution)/shard_map/ppermute | solution.py:176
  79.3 4.4 %collective-permute-start.14 = (f32[64,256]{1,0:T(8,128)S(1)}, f32[64,256]{1,0:T(8,128)S(1)}, u32[]{:S(2)}, u32[]{:S(2)}) collective-permute-start(f32[64,256]{1,0:T(8,128)S(1)} %get-tuple-element.95), channel_id=1, source_target_pairs={{0,3},{1,0},{2,1},{3,2},{4,7},{5,4},{6,5},{7,6},{8,11},{9,8},{10,9... | collective-permute-start | bytes 196616 | tf_op jit(solution)/shard_map/ppermute | solution.py:181
  83.7 1.9 collective-permute-start.13
  85.6 1.9 collective-permute-start.12
  87.6 3.7 %collective-permute-done.14.u3 = f32[64,256]{1,0:T(8,128)S(1)} collective-permute-done((f32[64,256]{1,0:T(8,128)S(1)}, f32[64,256]{1,0:T(8,128)S(1)}, u32[]{:S(2)}, u32[]{:S(2)}) %collective-permute-start.14) | collective-permute-done | bytes 65568 | tf_op jit(solution)/shard_map/ppermute | solution.py:181
  92.6 5.7 %shard_map.101 = (f32[8,192,128]{2,1,0:T(8,128)}, f32[2,64,1024]{2,1,0:T(8,128)S(1)}) custom-call(s32[1]{0:T(128)} %bitcast.z_ref, bf16[768,3072]{1,0:T(8,128)(2,1)} %pad_maximum_fusion.w3, f32[256,256]{1,0:T(8,128)S(1)} %pad_maximum_fusion.3.own, f32[256,256]{1,0:T(8,128)S(1)} %collective-permute-done.6.u1, f32[256,256]{1,0:T(8,128)S(1)} %collective-permute-done.7.u2, ...), custom_call_target="tpu_custom_call" | custom-call | tf_op jit(solution)/shard_map/pallas_call | solution.py:165
  99.0 4.8 %all-to-all-start.2 = ((f32[8,192,128]{2,1,0:T(8,128)}), f32[8,192,128]{2,1,0:T(8,128)S(1)}, u32[]{:S(2)}, u32[]{:S(2)}) async-start(f32[8,192,128]{2,1,0:T(8,128)} %get-tuple-element.63), calls=%async_computation.2 | async-start | bytes 1572864 | tf_op jit(solution)/shard_map/all_to_all | solution.py:432
  105.2 11.2 %all-to-all-done.2.qkv1 = f32[8,192,128]{2,1,0:T(8,128)S(1)} async-done(((f32[8,192,128]{2,1,0:T(8,128)}), f32[8,192,128]{2,1,0:T(8,128)S(1)}, u32[]{:S(2)}, u32[]{:S(2)}) %all-to-all-start.2) | async-done | bytes 786464 | tf_op jit(solution)/shard_map/all_to_all | solution.py:432
  118.0 12.5 %shard_map.102 = (f32[16,64,128]{2,1,0:T(8,128)S(1)}, f32[32,32,128]{2,1,0:T(8,128)}, bf16[16,640,128]{2,1,0:T(8,128)(2,1)}, bf16[16,640,128]{2,1,0:T(8,128)(2,1)}) custom-call(s32[16,5]{1,0:T(8,128)S(1)} %bitcast.10, s32[16,128,1]{2,1,0:T(8,128)S(1)} %copy-done.5, s32[16,128]{1,0:T(8,128)S(1)} %bitcast.13, f32[8,192,128]{2,1,0:T(8,128)S(1)} %all-to-all-done.1.qkv0, ...), custom_call_target="tpu_custom_call" | custom-call | tf_op jit(solution)/shard_map/pallas_call | solution.py:165
  131.3 5.6 %all-to-all-start.3 = ((f32[32,32,128]{2,1,0:T(8,128)}), f32[32,32,128]{2,1,0:T(8,128)}, u32[]{:S(2)}, u32[]{:S(2)}) async-start(f32[32,32,128]{2,1,0:T(8,128)} %get-tuple-element.73), calls=%async_computation.3 | async-start | bytes 1048576 | tf_op jit(solution)/shard_map/all_to_all | solution.py:454
  136.9 4.4 %fusion = (bf16[1024,1024]{1,0:T(8,128)(2,1)}, bf16[1024,1024]{1,0:T(8,128)(2,1)S(1)}) fusion(f32[1024,1024]{1,0:T(8,128)} %all-gather.2.cloned.1.call-done), kind=kLoop, calls=%fused_computation.5 | loop fusion | flops 4194304 | bytes 8388608 | tf_op jit(solution)/shard_map/convert_element_type | solution.py:153
  141.3 9.9 %all-to-all-done.3.pieces = f32[32,32,128]{2,1,0:T(8,128)} async-done(((f32[32,32,128]{2,1,0:T(8,128)}), f32[32,32,128]{2,1,0:T(8,128)}, u32[]{:S(2)}, u32[]{:S(2)}) %all-to-all-start.3) | async-done | bytes 524320 | tf_op jit(solution)/shard_map/all_to_all | solution.py:454
  155.0 5.6 %shard_map.103 = (f32[32,32,128]{2,1,0:T(8,128)S(1)}, f32[64,1024]{1,0:T(8,128)S(1)}) custom-call(s32[1]{0:T(128)} %bitcast.z_ref, bf16[1024,1024]{1,0:T(8,128)(2,1)S(1)} %get-tuple-element.88.w_high, bf16[1024,1024]{1,0:T(8,128)(2,1)} %get-tuple-element.87.w_low, f32[2,64,1024]{2,1,0:T(8,128)S(1)} %copy-done.8, f32[2,64,1024]{2,1,0:T(8,128)S(1)} %copy-done.10, ...), custom_call_target="tpu_custom_call" | custom-call | tf_op jit(solution)/shard_map/pallas_call | solution.py:165
  160.6 18.3 %all_to_all.35.grad = f32[32,32,128]{2,1,0:T(8,128)S(1)} all-to-all(f32[32,32,128]{2,1,0:T(8,128)S(1)} %get-tuple-element.74), channel_id=1, replica_groups=mesh['ctx'=8,'head'=4] {'ctx','head'}, dimensions={0} | all-to-all | bytes 1048576 | tf_op jit(solution)/shard_map/all_to_all | solution.py:461
  178.9 13.3 %shard_map.104 = (f32[8,192,128]{2,1,0:T(8,128)S(1)}, f32[8,192,128]{2,1,0:T(8,128)S(1)}) custom-call(s32[16,5]{1,0:T(8,128)S(1)} %bitcast.11, f32[8,192,128]{2,1,0:T(8,128)S(1)} %copy-done.2, f32[8,192,128]{2,1,0:T(8,128)S(1)} %copy-done.4, bf16[16,640,128]{2,1,0:T(8,128)(2,1)} %get-tuple-element.64.p_high, bf16[16,640,128]{2,1,0:T(8,128)(2,1)} %get-tuple-element.65.p_low, ...), custom_call_target="tpu_custom_call" | custom-call | tf_op jit(solution)/shard_map/pallas_call | solution.py:165
  192.2 15.9 %all_to_all.36.grads = f32[8,192,128]{2,1,0:T(8,128)S(1)} all-to-all(f32[8,192,128]{2,1,0:T(8,128)S(1)} %get-tuple-element.82), channel_id=1, replica_groups=mesh['ctx'=8,'head'=4] {'ctx'}, dimensions={0} | all-to-all | bytes 1572864 | tf_op jit(solution)/shard_map/all_to_all | solution.py:473
  208.1 3.5 %all-to-all-start.5 = ((f32[8,192,128]{2,1,0:T(8,128)}), f32[8,192,128]{2,1,0:T(8,128)S(1)}, u32[]{:S(2)}, u32[]{:S(2)}) async-start(f32[8,192,128]{2,1,0:T(8,128)} %copy-done.6), calls=%async_computation.5 | async-start | bytes 1572864 | tf_op jit(solution)/shard_map/all_to_all | solution.py:473
  211.7 3.2 %shard_map.106 = (f32[128,256]{1,0:T(8,128)S(1)}, f32[128,256]{1,0:T(8,128)S(1)}, f32[128,256]{1,0:T(8,128)S(1)}, f32[128,256]{1,0:T(8,128)S(1)}) custom-call(s32[1]{0:T(128)} %bitcast.z_ref, bf16[768,3072]{1,0:T(8,128)(2,1)} %pad_maximum_fusion.w3, f32[8,192,128]{2,1,0:T(8,128)S(1)} %all_to_all.36.grads, f32[64,1024]{1,0:T(8,128)S(1)} %get-tuple-element.77.direct_sum), custom_call_target="tpu_custom_call" | custom-call | tf_op jit(solution)/shard_map/pallas_call | solution.py:165
  219.1 5.2 %all-to-all-done.5.grads = f32[8,192,128]{2,1,0:T(8,128)S(1)} async-done(((f32[8,192,128]{2,1,0:T(8,128)}), f32[8,192,128]{2,1,0:T(8,128)S(1)}, u32[]{:S(2)}, u32[]{:S(2)}) %all-to-all-start.5) | async-done | bytes 786464 | tf_op jit(solution)/shard_map/all_to_all | solution.py:473
  224.2 3.2 %shard_map.105 = (f32[128,256]{1,0:T(8,128)S(1)}, f32[128,256]{1,0:T(8,128)S(1)}, f32[128,256]{1,0:T(8,128)S(1)}, f32[128,256]{1,0:T(8,128)S(1)}) custom-call(s32[1]{0:T(128)} %bitcast.z_ref, bf16[768,3072]{1,0:T(8,128)(2,1)} %pad_maximum_fusion.w3, f32[8,192,128]{2,1,0:T(8,128)S(1)} %all-to-all-done.5.grads, f32[64,1024]{1,0:T(8,128)S(1)} %get-tuple-element.77.direct_sum), custom_call_target="tpu_custom_call" | custom-call | tf_op jit(solution)/shard_map/pallas_call | solution.py:165
  227.5 1.7 collective-permute-start.15
  231.6 3.1 %collective-permute-done.15 = f32[128,256]{1,0:T(8,128)S(1)} collective-permute-done((f32[128,256]{1,0:T(8,128)S(1)}, f32[128,256]{1,0:T(8,128)S(1)}, u32[]{:S(2)}, u32[]{:S(2)}) %collective-permute-start.15) | collective-permute-done | bytes 131104 | tf_op jit(solution)/shard_map/ppermute | solution.py:181
  234.7 4.9 %collective-permute-done.16 = f32[128,256]{1,0:T(8,128)S(1)} collective-permute-done((f32[128,256]{1,0:T(8,128)S(1)}, f32[128,256]{1,0:T(8,128)S(1)}, u32[]{:S(2)}, u32[]{:S(2)}) %collective-permute-start.16) | collective-permute-done | bytes 131104 | tf_op jit(solution)/shard_map/ppermute | solution.py:181
  (102 shorter events, 40.0 us)
Async XLA Ops:
  6.5 31.9 %copy-start = (f32[256,1024]{1,0:T(8,128)S(1)}, f32[256,1024]{1,0:T(8,128)}, u32[]{:S(2)}) copy-start(f32[256,1024]{1,0:T(8,128)} %param.15) | copy-start | bytes 3145732
  8.9 14.6 %collective-permute-start.3 = (f32[256,256]{1,0:T(8,128)S(1)}, f32[256,256]{1,0:T(8,128)S(1)}, u32[]{:S(2)}, u32[]{:S(2)}) collective-permute-start(f32[256,256]{1,0:T(8,128)S(1)} %pad_maximum_fusion.2.own), channel_id=1, source_target_pairs={{1,0},{2,1},{3,2},{5,4},{6,5},{7,6},{9,8},{10,9},{11,10},{13,12},{... | collective-permute-start | bytes 786440 | tf_op jit(solution)/shard_map/ppermute | solution.py:176
  10.2 14.7 %collective-permute-start = (f32[256,256]{1,0:T(8,128)S(1)}, f32[256,256]{1,0:T(8,128)S(1)}, u32[]{:S(2)}, u32[]{:S(2)}) collective-permute-start(f32[256,256]{1,0:T(8,128)S(1)} %pad_maximum_fusion.2.own), channel_id=1, source_target_pairs={{0,1},{1,2},{2,3},{4,5},{5,6},{6,7},{8,9},{9,10},{10,11},{12,13},{... | collective-permute-start | bytes 786440 | tf_op jit(solution)/shard_map/ppermute | solution.py:176
  17.0 22.1 %all-to-all-start = ((s32[8,2,5]{2,1,0:T(2,128)}), s32[8,2,5]{2,1,0:T(2,128)S(1)}, u32[]{:S(2)}, u32[]{:S(2)}) async-start(s32[8,2,5]{2,1,0:T(2,128)} %broadcast_in_dim.2), calls=%async_computation | async-start | bytes 16384 | tf_op jit(solution)/shard_map/all_to_all | solution.py:400
  21.2 115.7 %all-gather.2.cloned.1.call-start = ((), (), s32[]{:S(2)}) async-start(), calls=%async_computation.7 | async-start | bytes 4325376 | tf_op jit(solution)/shard_map/all_gather | solution.py:421
  23.5 10.6 %collective-permute-start.4 = (f32[256,256]{1,0:T(8,128)S(1)}, f32[256,256]{1,0:T(8,128)S(1)}, u32[]{:S(2)}, u32[]{:S(2)}) collective-permute-start(f32[256,256]{1,0:T(8,128)S(1)} %collective-permute-done.3.d1), channel_id=1, source_target_pairs={{1,0},{2,1},{5,4},{6,5},{9,8},{10,9},{13,12},{14,13},{17,16},{18,1... | collective-permute-start | bytes 786440 | tf_op jit(solution)/shard_map/ppermute | solution.py:176
  24.8 10.5 %collective-permute-start.1 = (f32[256,256]{1,0:T(8,128)S(1)}, f32[256,256]{1,0:T(8,128)S(1)}, u32[]{:S(2)}, u32[]{:S(2)}) collective-permute-start(f32[256,256]{1,0:T(8,128)S(1)} %collective-permute-done.u1), channel_id=1, source_target_pairs={{1,2},{2,3},{5,6},{6,7},{9,10},{10,11},{13,14},{14,15},{17,18},{18... | collective-permute-start | bytes 786440 | tf_op jit(solution)/shard_map/ppermute | solution.py:176
  34.1 9.8 %collective-permute-start.5 = (f32[256,256]{1,0:T(8,128)S(1)}, f32[256,256]{1,0:T(8,128)S(1)}, u32[]{:S(2)}, u32[]{:S(2)}) collective-permute-start(f32[256,256]{1,0:T(8,128)S(1)} %collective-permute-done.4.d2), channel_id=1, source_target_pairs={{1,0},{5,4},{9,8},{13,12},{17,16},{21,20},{25,24},{29,28}} | collective-permute-start | bytes 786440 | tf_op jit(solution)/shard_map/ppermute | solution.py:176
  35.4 8.5 %collective-permute-start.2 = (f32[256,256]{1,0:T(8,128)S(1)}, f32[256,256]{1,0:T(8,128)S(1)}, u32[]{:S(2)}, u32[]{:S(2)}) collective-permute-start(f32[256,256]{1,0:T(8,128)S(1)} %collective-permute-done.1.u2), channel_id=1, source_target_pairs={{2,3},{6,7},{10,11},{14,15},{18,19},{22,23},{26,27},{30,31}} | collective-permute-start | bytes 786440 | tf_op jit(solution)/shard_map/ppermute | solution.py:176
  44.6 18.8 %collective-permute-start.9 = (f32[256,256]{1,0:T(8,128)S(1)}, f32[256,256]{1,0:T(8,128)S(1)}, u32[]{:S(2)}, u32[]{:S(2)}) collective-permute-start(f32[256,256]{1,0:T(8,128)S(1)} %pad_maximum_fusion.3.own), channel_id=1, source_target_pairs={{1,0},{2,1},{3,2},{5,4},{6,5},{7,6},{9,8},{10,9},{11,10},{13,12},{... | collective-permute-start | bytes 786440 | tf_op jit(solution)/shard_map/ppermute | solution.py:176
  45.9 18.8 %collective-permute-start.6 = (f32[256,256]{1,0:T(8,128)S(1)}, f32[256,256]{1,0:T(8,128)S(1)}, u32[]{:S(2)}, u32[]{:S(2)}) collective-permute-start(f32[256,256]{1,0:T(8,128)S(1)} %pad_maximum_fusion.3.own), channel_id=1, source_target_pairs={{0,1},{1,2},{2,3},{4,5},{5,6},{6,7},{8,9},{9,10},{10,11},{12,13},{... | collective-permute-start | bytes 786440 | tf_op jit(solution)/shard_map/ppermute | solution.py:176
  59.9 39.2 %all-to-all-start.1 = ((f32[8,192,128]{2,1,0:T(8,128)}), f32[8,192,128]{2,1,0:T(8,128)S(1)}, u32[]{:S(2)}, u32[]{:S(2)}) async-start(f32[8,192,128]{2,1,0:T(8,128)} %get-tuple-element.55), calls=%async_computation.1 | async-start | bytes 1572864 | tf_op jit(solution)/shard_map/all_to_all | solution.py:432
  63.4 10.5 %collective-permute-start.10 = (f32[256,256]{1,0:T(8,128)S(1)}, f32[256,256]{1,0:T(8,128)S(1)}, u32[]{:S(2)}, u32[]{:S(2)}) collective-permute-start(f32[256,256]{1,0:T(8,128)S(1)} %collective-permute-done.9.d1), channel_id=1, source_target_pairs={{1,0},{2,1},{5,4},{6,5},{9,8},{10,9},{13,12},{14,13},{17,16},{18,1... | collective-permute-start | bytes 786440 | tf_op jit(solution)/shard_map/ppermute | solution.py:176
  64.8 10.5 %collective-permute-start.7 = (f32[256,256]{1,0:T(8,128)S(1)}, f32[256,256]{1,0:T(8,128)S(1)}, u32[]{:S(2)}, u32[]{:S(2)}) collective-permute-start(f32[256,256]{1,0:T(8,128)S(1)} %collective-permute-done.6.u1), channel_id=1, source_target_pairs={{1,2},{2,3},{5,6},{6,7},{9,10},{10,11},{13,14},{14,15},{17,18},{18... | collective-permute-start | bytes 786440 | tf_op jit(solution)/shard_map/ppermute | solution.py:176
  74.0 18.6 %collective-permute-start.11 = (f32[256,256]{1,0:T(8,128)S(1)}, f32[256,256]{1,0:T(8,128)S(1)}, u32[]{:S(2)}, u32[]{:S(2)}) collective-permute-start(f32[256,256]{1,0:T(8,128)S(1)} %collective-permute-done.10.d2), channel_id=1, source_target_pairs={{1,0},{5,4},{9,8},{13,12},{17,16},{21,20},{25,24},{29,28}} | collective-permute-start | bytes 786440 | tf_op jit(solution)/shard_map/ppermute | solution.py:176
  75.3 17.3 %collective-permute-start.8 = (f32[256,256]{1,0:T(8,128)S(1)}, f32[256,256]{1,0:T(8,128)}, u32[]{:S(2)}, u32[]{:S(2)}) collective-permute-start(f32[256,256]{1,0:T(8,128)S(1)} %collective-permute-done.7.u2), channel_id=1, source_target_pairs={{2,3},{6,7},{10,11},{14,15},{18,19},{22,23},{26,27},{30,31}} | collective-permute-start | bytes 786440 | tf_op jit(solution)/shard_map/ppermute | solution.py:176
  79.3 12.0 %collective-permute-start.14 = (f32[64,256]{1,0:T(8,128)S(1)}, f32[64,256]{1,0:T(8,128)S(1)}, u32[]{:S(2)}, u32[]{:S(2)}) collective-permute-start(f32[64,256]{1,0:T(8,128)S(1)} %get-tuple-element.95), channel_id=1, source_target_pairs={{0,3},{1,0},{2,1},{3,2},{4,7},{5,4},{6,5},{7,6},{8,11},{9,8},{10,9... | collective-permute-start | bytes 196616 | tf_op jit(solution)/shard_map/ppermute | solution.py:181
  83.7 7.6 %collective-permute-start.13 = (f32[64,256]{1,0:T(8,128)S(1)}, f32[64,256]{1,0:T(8,128)S(1)}, u32[]{:S(2)}, u32[]{:S(2)}) collective-permute-start(f32[64,256]{1,0:T(8,128)S(1)} %get-tuple-element.96), channel_id=1, source_target_pairs={{0,2},{1,3},{2,0},{3,1},{4,6},{5,7},{6,4},{7,5},{8,10},{9,11},{10,... | collective-permute-start | bytes 196616 | tf_op jit(solution)/shard_map/ppermute | solution.py:181
  85.6 6.3 %collective-permute-start.12 = (f32[64,256]{1,0:T(8,128)S(1)}, f32[64,256]{1,0:T(8,128)S(1)}, u32[]{:S(2)}, u32[]{:S(2)}) collective-permute-start(f32[64,256]{1,0:T(8,128)S(1)} %get-tuple-element.97), channel_id=1, source_target_pairs={{0,1},{1,2},{2,3},{3,0},{4,5},{5,6},{6,7},{7,4},{8,9},{9,10},{10,1... | collective-permute-start | bytes 196616 | tf_op jit(solution)/shard_map/ppermute | solution.py:181
  99.0 32.2 %copy-start.1 = (f32[8,192,128]{2,1,0:T(8,128)}, f32[8,192,128]{2,1,0:T(8,128)S(1)}, u32[]{:S(2)}) copy-start(f32[8,192,128]{2,1,0:T(8,128)S(1)} %all-to-all-done.1.qkv0) | copy-start | bytes 2359300
  99.0 17.4 %all-to-all-start.2 = ((f32[8,192,128]{2,1,0:T(8,128)}), f32[8,192,128]{2,1,0:T(8,128)S(1)}, u32[]{:S(2)}, u32[]{:S(2)}) async-start(f32[8,192,128]{2,1,0:T(8,128)} %get-tuple-element.63), calls=%async_computation.2 | async-start | bytes 1572864 | tf_op jit(solution)/shard_map/all_to_all | solution.py:432
  131.3 19.9 %all-to-all-start.3 = ((f32[32,32,128]{2,1,0:T(8,128)}), f32[32,32,128]{2,1,0:T(8,128)}, u32[]{:S(2)}, u32[]{:S(2)}) async-start(f32[32,32,128]{2,1,0:T(8,128)} %get-tuple-element.73), calls=%async_computation.3 | async-start | bytes 1048576 | tf_op jit(solution)/shard_map/all_to_all | solution.py:454
  155.0 23.9 %copy-start.2 = (f32[8,192,128]{2,1,0:T(8,128)S(1)}, f32[8,192,128]{2,1,0:T(8,128)}, u32[]{:S(2)}) copy-start(f32[8,192,128]{2,1,0:T(8,128)} %copy-done.1) | copy-start | bytes 2359300
  155.0 23.9 %copy-start.4 = (f32[8,192,128]{2,1,0:T(8,128)S(1)}, f32[8,192,128]{2,1,0:T(8,128)}, u32[]{:S(2)}) copy-start(f32[8,192,128]{2,1,0:T(8,128)} %copy-done.3) | copy-start | bytes 2359300
  155.0 23.9 %copy-start.12 = (f32[16,64,128]{2,1,0:T(8,128)S(1)}, f32[16,64,128]{2,1,0:T(8,128)}, u32[]{:S(2)}) copy-start(f32[16,64,128]{2,1,0:T(8,128)} %copy-done.11) | copy-start | bytes 1572868
  208.1 16.1 %all-to-all-start.5 = ((f32[8,192,128]{2,1,0:T(8,128)}), f32[8,192,128]{2,1,0:T(8,128)S(1)}, u32[]{:S(2)}, u32[]{:S(2)}) async-start(f32[8,192,128]{2,1,0:T(8,128)} %copy-done.6), calls=%async_computation.5 | async-start | bytes 1572864 | tf_op jit(solution)/shard_map/all_to_all | solution.py:473
  214.9 15.1 %collective-permute-start.18 = (f32[128,256]{1,0:T(8,128)S(1)}, f32[128,256]{1,0:T(8,128)S(1)}, u32[]{:S(2)}, u32[]{:S(2)}) collective-permute-start(f32[128,256]{1,0:T(8,128)S(1)} %get-tuple-element.84), channel_id=1, source_target_pairs={{0,1},{1,2},{2,3},{3,0},{4,5},{5,6},{6,7},{7,4},{8,9},{9,10},{10,1... | collective-permute-start | bytes 393224 | tf_op jit(solution)/shard_map/ppermute | solution.py:181
  216.6 15.0 %collective-permute-start.19 = (f32[128,256]{1,0:T(8,128)S(1)}, f32[128,256]{1,0:T(8,128)S(1)}, u32[]{:S(2)}, u32[]{:S(2)}) collective-permute-start(f32[128,256]{1,0:T(8,128)S(1)} %get-tuple-element.85), channel_id=1, source_target_pairs={{0,2},{1,3},{2,0},{3,1},{4,6},{5,7},{6,4},{7,5},{8,10},{9,11},{10,... | collective-permute-start | bytes 393224 | tf_op jit(solution)/shard_map/ppermute | solution.py:181
  217.6 14.0 %collective-permute-start.20 = (f32[128,256]{1,0:T(8,128)S(1)}, f32[128,256]{1,0:T(8,128)S(1)}, u32[]{:S(2)}, u32[]{:S(2)}) collective-permute-start(f32[128,256]{1,0:T(8,128)S(1)} %get-tuple-element.86), channel_id=1, source_target_pairs={{0,3},{1,0},{2,1},{3,2},{4,7},{5,4},{6,5},{7,6},{8,11},{9,8},{10,9... | collective-permute-start | bytes 393224 | tf_op jit(solution)/shard_map/ppermute | solution.py:181
  227.5 7.3 %collective-permute-start.15 = (f32[128,256]{1,0:T(8,128)S(1)}, f32[128,256]{1,0:T(8,128)S(1)}, u32[]{:S(2)}, u32[]{:S(2)}) collective-permute-start(f32[128,256]{1,0:T(8,128)S(1)} %get-tuple-element.79), channel_id=1, source_target_pairs={{0,1},{1,2},{2,3},{3,0},{4,5},{5,6},{6,7},{7,4},{8,9},{9,10},{10,1... | collective-permute-start | bytes 393224 | tf_op jit(solution)/shard_map/ppermute | solution.py:181
  229.1 10.4 %collective-permute-start.16 = (f32[128,256]{1,0:T(8,128)S(1)}, f32[128,256]{1,0:T(8,128)S(1)}, u32[]{:S(2)}, u32[]{:S(2)}) collective-permute-start(f32[128,256]{1,0:T(8,128)S(1)} %get-tuple-element.80), channel_id=1, source_target_pairs={{0,2},{1,3},{2,0},{3,1},{4,6},{5,7},{6,4},{7,5},{8,10},{9,11},{10,... | collective-permute-start | bytes 393224 | tf_op jit(solution)/shard_map/ppermute | solution.py:181
  230.1 9.5 %collective-permute-start.17 = (f32[128,256]{1,0:T(8,128)S(1)}, f32[128,256]{1,0:T(8,128)S(1)}, u32[]{:S(2)}, u32[]{:S(2)}) collective-permute-start(f32[128,256]{1,0:T(8,128)S(1)} %get-tuple-element.81), channel_id=1, source_target_pairs={{0,3},{1,0},{2,1},{3,2},{4,7},{5,4},{6,5},{7,6},{8,11},{9,8},{10,9... | collective-permute-start | bytes 393224 | tf_op jit(solution)/shard_map/ppermute | solution.py:181
  (22 other events, 116.3 us)
Sparse Core Ops, SparseCore 0:
  44.7 64.1 all-gather.1

commit v3 on v2

--- a/solution.py
+++ b/solution.py
@@ -137,7 +137,7 @@
 
 F32 = jnp.float32
 BF16 = jnp.bfloat16
-LIMIT = 48 * 1024 * 1024
+MIB = 1 << 20
 VM = pl.BlockSpec(memory_space=pltpu.VMEM)
 SM = pl.BlockSpec(memory_space=pltpu.SMEM)
 
@@ -161,14 +161,14 @@
     return lax.dot_general(a, b, (((1,), (1,)), ((), ())), preferred_element_type=F32)
 
 
-def call(kernel, outs, scratch, n_smem, *args):
+def call(kernel, mib, outs, scratch, n_smem, *args):
     return pl.pallas_call(
         kernel,
         out_shape=outs,
         in_specs=[SM] * n_smem + [VM] * (len(args) - n_smem),
         out_specs=jax.tree.map(lambda _: VM, outs),
         scratch_shapes=scratch,
-        compiler_params=pltpu.CompilerParams(vmem_limit_bytes=LIMIT),
+        compiler_params=pltpu.CompilerParams(vmem_limit_bytes=mib * MIB),
     )(*args)
 
 
@@ -194,16 +194,20 @@
     tokens = both // 2
     for k in range(n):
         column = pl.multiple_of(lax.rem(z - k + n, n) * feats, feats)
-        x = own[...] if k == 0 else ups[k - 1][...] + downs[n - k - 1][...]
         for s in range(2):
-            t = x[s * tokens : (s + 1) * tokens]
-            rows[s, :, pl.ds(column, feats)] = jnp.where(
-                lax.rem(z, 2) == 0, t[:quarter], t[quarter:]
-            )
-        high, low = halves(x)
-        x3[:, pl.ds(column, feats)] = high
-        x3[:, pl.ds(pl.multiple_of(width + column, feats), feats)] = high
-        x3[:, pl.ds(pl.multiple_of(2 * width + column, feats), feats)] = low
+            span = pl.ds(s * tokens, tokens)
+            if k == 0:
+                x = own[span]
+            else:
+                x = ups[k - 1][span] + downs[n - k - 1][span]
+            for q in range(n):
+                @pl.when(z == q)
+                def _(x=x, q=q, s=s):
+                    rows[s, :, pl.ds(column, feats)] = x[q * quarter : (q + 1) * quarter]
+            high, low = halves(x)
+            x3[span, pl.ds(column, feats)] = high
+            x3[span, pl.ds(pl.multiple_of(width + column, feats), feats)] = high
+            x3[span, pl.ds(pl.multiple_of(2 * width + column, feats), feats)] = low
     part = out.shape[1]
     for h in range(n):
         r = mm_nt(w3[h * part : (h + 1) * part, :], x3[...])
@@ -227,11 +231,10 @@
 
 
 def attend_kernel(
-    lists, session_col, session_row, qkv0, qkv1, mixed, folded, p_high, p_low, q3, k3, v2
+    lists, session_col, session_row, qkv, mixed, folded, p_high, p_low, q3, k3, v2
 ):
-    qkv = (qkv0, qkv1)
     for b in range(NBLOCKS):
-        t = qkv[b % 2][b // 2]
+        t = qkv[b // 2, :, (b % 2) * BLK : (b % 2 + 1) * BLK]
         q_high, q_low = halves(t[:HD] * SCALE)
         q3[b] = jnp.concatenate([q_high, q_high, q_low], axis=0)
         k_high, k_low = halves(t[HD : 2 * HD].T)
@@ -240,38 +243,39 @@
         v2[b] = jnp.concatenate([v_high, v_low], axis=0)
 
     def body(c, carry):
-        for e in range(2):
-            b = 2 * c + e
-            query = q3[b]
+        blocks = [GROUP * c + e for e in range(GROUP)]
+        scores = []
+        for b in blocks:
             mine = session_row[pl.ds(b, 1), :]
-            scores = []
+            tiles = []
             for j in range(KVB):
                 other = lists[b, j]
-                s = mm(k3[other], query)
-                scores.append(jnp.where(session_col[other] == mine, s, -1e30))
-            s = jnp.concatenate(scores, axis=0)
-            top = jnp.max(s, axis=0, keepdims=True)
-            expo = jnp.exp(s - top)
-            probs = expo * (1.0 / jnp.sum(expo, axis=0, keepdims=True))
-            high, low = halves(probs)
+                s = mm(k3[other], q3[b])
+                tiles.append(jnp.where(session_col[other] == mine, s, -1e30))
+            scores.append(jnp.concatenate(tiles, axis=0))
+        tops = [jnp.max(s, axis=0, keepdims=True) for s in scores]
+        expos = [jnp.exp(s - top) for s, top in zip(scores, tops)]
+        scales = [1.0 / jnp.sum(expo, axis=0, keepdims=True) for expo in expos]
+        for b, e, expo, each in zip(blocks, range(GROUP), expos, scales):
+            high, low = halves(expo * each)
             p_high[b] = high
             p_low[b] = low
             values = jnp.concatenate([v2[lists[b, j]] for j in range(KVB)], axis=1)
             both = mm(values, high)
             block = both[:HD] + both[HD:] + mm(values[:HD], low)
             mixed[b] = block
-            folded[4 * c + 2 * e], folded[4 * c + 2 * e + 1] = fold(block)
+            folded[2 * b], folded[2 * b + 1] = fold(block)
         return carry
 
-    lax.fori_loop(0, NBLOCKS // 2, body, 0)
+    lax.fori_loop(0, NBLOCKS // GROUP, body, 0)
 
 
 def attend_back_kernel(
-    lists, qkv0, qkv1, p_high, p_low, grad, mixed, out0, out1, q2, k2, v3, acc
+    lists, qkv, p_high, p_low, grad, mixed, out0, out1, q2, k2, v3, acc
 ):
-    qkv, out = (qkv0, qkv1), (out0, out1)
+    out = (out0, out1)
     for b in range(NBLOCKS):
-        t = qkv[b % 2][b // 2]
+        t = qkv[b // 2, :, (b % 2) * BLK : (b % 2 + 1) * BLK]
         q_high, q_low = halves(t[:HD])
         q2[b] = jnp.concatenate([q_high, q_low], axis=0)
         k_high, k_low = halves(t[HD : 2 * HD])
@@ -281,53 +285,58 @@
     acc[...] = jnp.zeros_like(acc)
 
     def body(c, carry):
-        for e in range(2):
-            b = 2 * c + e
-            g = unfold(grad[4 * c + 2 * e], grad[4 * c + 2 * e + 1])
-            delta = jnp.sum(g * mixed[b], axis=0, keepdims=True)
-            g_high, g_low = halves(g)
+        blocks = [GROUP * c + e for e in range(GROUP)]
+        grads = [unfold(grad[2 * b], grad[2 * b + 1]) for b in blocks]
+        parts = [halves(g) for g in grads]
+        probs_grads = []
+        for b, (g_high, g_low) in zip(blocks, parts):
             g3 = jnp.concatenate([g_high, g_high, g_low], axis=0)
-            g2 = jnp.concatenate([g_high, g_low], axis=0)
-            grad_probs = jnp.concatenate([mm(v3[lists[b, j]], g3) for j in range(KVB)], axis=0)
+            probs_grads.append(
+                jnp.concatenate([mm(v3[lists[b, j]], g3) for j in range(KVB)], axis=0)
+            )
+        added = []
+        for e, b in enumerate(blocks):
+            delta = jnp.sum(grads[e] * mixed[b], axis=0, keepdims=True)
+            g2 = jnp.concatenate(parts[e], axis=0)
             ph, pw = p_high[b], p_low[b]
             probs = ph.astype(F32) + pw.astype(F32)
-            s_high, s_low = halves(probs * (grad_probs - delta) * SCALE)
+            s_high, s_low = halves(probs * (probs_grads[e] - delta) * SCALE)
             keys = jnp.concatenate([k2[lists[b, j]] for j in range(KVB)], axis=1)
             both = mm(keys, s_high)
-            out[e][c, 0:HD] = both[:HD] + both[HD:] + mm(keys[:HD], s_low)
+            out[e % 2][(GROUP // 2) * c + e // 2, 0:HD] = (
+                both[:HD] + both[HD:] + mm(keys[:HD], s_low)
+            )
             query = q2[b]
             both = mm_nt(query, s_high)
             grad_keys = both[:HD] + both[HD:] + mm_nt(query[:HD], s_low)
             both = mm_nt(g2, ph)
             grad_values = both[:HD] + both[HD:] + mm_nt(g2[:HD], pw)
+            added.append(jnp.concatenate([grad_keys, grad_values], axis=0))
+        for b, both in zip(blocks, added):
             for j in range(KVB):
-                at = slice(j * BLK, (j + 1) * BLK)
-                acc[lists[b, j]] += jnp.concatenate([grad_keys[:, at], grad_values[:, at]], axis=0)
+                acc[lists[b, j]] += both[:, j * BLK : (j + 1) * BLK]
         return carry
 
-    lax.fori_loop(0, NBLOCKS // 2, body, 0)
+    lax.fori_loop(0, NBLOCKS // GROUP, body, 0)
     for b in range(NBLOCKS):
         out[b % 2][b // 2, HD : 3 * HD] = acc[b]
 
 
 def norm_kernel(
-    z_ref, w_high, w_low, rows0, rows1, u0, u1, u2, u3, pieces, out, direct_sum, upstream, mixed
+    w_high, w_low, rows, ups, pieces, out, direct_sum, upstream, mixed
 ):
-    z = z_ref[0]
     n = 4
     quarter, width = direct_sum.shape
     feats = width // n
-    for k, u in enumerate((u0, u1, u2, u3)):
-        at = pl.ds(pl.multiple_of(lax.rem(z - k + n, n) * feats, feats), feats)
-        upstream[:, at] = u[...]
+    for k in range(n):
+        upstream[:, k * feats : (k + 1) * feats] = ups[k]
     for group in range(n):
         for h in range(n):
             at = group * feats + h * HD
             mixed[at : at + HD, :] = unfold(pieces[2 * h * n + group], pieces[(2 * h + 1) * n + group])
     m_high, m_low = halves(mixed[...].T)
     projected = mm_nt(m_high, w_high[...]) + mm_nt(m_low, w_high[...]) + mm_nt(m_high, w_low[...])
-    rows = jnp.where(z < 2, rows0[...], rows1[...])
-    summed = rows.reshape(2 * quarter, width) + projected
+    summed = rows[...].reshape(2 * quarter, width) + projected
     mean = jnp.sum(summed, axis=-1, keepdims=True) / width
     second = jnp.sum(summed * summed, axis=-1, keepdims=True) / width
     inverse = lax.rsqrt(second - mean * mean + EPS)
@@ -366,6 +375,7 @@
 
 HD = 64
 NBLOCKS = 16
+GROUP = 4
 SCALE = 1.0 / math.sqrt(HD)
 
 
@@ -387,15 +397,12 @@
 
     travel = packets - baseline
     half = tokens // 2
-    gathered = []
-    for e in range(2):
-        span = slice(e * half, (e + 1) * half)
-        own = jnp.concatenate([baseline[span] + alpha * travel[span] for alpha in ALPHAS])
-        ups, downs = [own], [own]
-        for step in range(1, n):
-            ups.append(shift(ups[-1], 1, step - 1, n - 2))
-            downs.append(shift(downs[-1], -1, 1, n - step))
-        gathered.append([own] + ups[1:] + downs[1:])
+    own = jnp.concatenate([baseline + alpha * travel for alpha in ALPHAS])
+    ups, downs = [own], [own]
+    for step in range(1, n):
+        ups.append(shift(ups[-1], 1, step - 1, n - 2))
+        downs.append(shift(downs[-1], -1, 1, n - step))
+    gathered = [own] + ups[1:] + downs[1:]
 
     lists = lax.all_to_all(
         jnp.broadcast_to(block_lists[None], (members,) + block_lists.shape), "ctx", 0, 0, tiled=True
@@ -405,39 +412,30 @@
     ).reshape(heads * part, width)
     high, low = halves_outside(weights)
     w3 = jnp.concatenate([high, low, high], axis=1)
-    upstream = probe * gain
-    up_pieces = exchange(
-        [
-            lax.dynamic_slice_in_dim(upstream, lax.rem(z + k, n) * quarter, quarter, 0)
-            for k in range(n)
-        ]
-    )
     slab_rows = lax.dynamic_slice_in_dim(w_out, lax.axis_index("ctx") * slab, slab, 0)
-
-    gathered[0], w3, lists, slab_rows = lax.optimization_barrier(
-        (gathered[0], w3, lists, slab_rows)
-    )
-    gathered[1], up_pieces = lax.optimization_barrier((gathered[1], up_pieces))
+    upstream = (probe * gain).reshape(n, quarter, feats)
+    gathered, w3, lists, slab_rows, upstream = lax.optimization_barrier(
+        (gathered, w3, lists, slab_rows, upstream)
+    )
     whole_out = lax.all_gather(slab_rows, ("head", "ctx"), axis=0, tiled=True)
     out_high, out_low = halves_outside(whole_out)
 
-    qkv, rows = [], []
-    for e in range(2):
-        projected, own_rows = call(
-            project_kernel,
-            (shape((members, part, half)), shape((2, quarter, width))),
-            [pltpu.VMEM((tokens, 3 * width), BF16)],
-            1, z_ref, w3, *gathered[e],
-        )
-        qkv.append(lax.all_to_all(projected, "ctx", 0, 0, tiled=True))
-        rows.append(own_rows)
+    qkv, rows = call(
+        project_kernel, 20,
+        (shape((members, part, tokens)), shape((2, quarter, width))),
+        [pltpu.VMEM((2 * tokens, 3 * width), BF16)],
+        1, z_ref, w3, *gathered,
+    )
+    qkv = lax.all_to_all(qkv, "ctx", 0, 0, tiled=True)
+    upstream = lax.all_to_all(upstream, "head", 0, 0, tiled=True)
+    qkv, upstream = lax.optimization_barrier((qkv, upstream))
 
     blocks = members * tokens // BLK
     everyone = members * n
     session_row = sessions.reshape(blocks, BLK)
     session_col = sessions.reshape(blocks, BLK, 1)
     mixed, folded, p_high, p_low = call(
-        attend_kernel,
+        attend_kernel, 20,
         (
             shape((blocks, HD, BLK)),
             shape((everyone, HD // 2, BLK)),
@@ -449,18 +447,18 @@
             pltpu.VMEM((blocks, BLK, part), BF16),
             pltpu.VMEM((blocks, 2 * HD, BLK), BF16),
         ],
-        1, lists, session_col, session_row, *qkv,
+        1, lists, session_col, session_row, qkv,
     )
     folded = lax.all_to_all(folded, ("ctx", "head"), 0, 0, tiled=True)
     grad, direct_sum = call(
-        norm_kernel,
+        norm_kernel, 20,
         (shape((everyone, HD // 2, BLK)), shape((quarter, width))),
         [pltpu.VMEM((quarter, width), F32), pltpu.VMEM((width, 2 * quarter), F32)],
-        1, z_ref, out_high, out_low, *rows, *up_pieces, folded,
+        0, out_high, out_low, rows, upstream, folded,
     )
     grad = lax.all_to_all(grad, ("ctx", "head"), 0, 0, tiled=True)
     grad_qkv = call(
-        attend_back_kernel,
+        attend_back_kernel, 20,
         (shape((members, part, half)),) * 2,
         [
             pltpu.VMEM((blocks, 2 * HD, BLK), BF16),
@@ -468,14 +466,14 @@
             pltpu.VMEM((blocks, BLK, part), BF16),
             pltpu.VMEM((blocks, 2 * HD, BLK), F32),
         ],
-        1, lists, *qkv, p_high, p_low, grad, mixed,
+        1, lists, qkv, p_high, p_low, grad, mixed,
     )
     grad_qkv = [lax.all_to_all(g, "ctx", 0, 0, tiled=True) for g in grad_qkv]
     totals = []
     for e in range(2):
         parts = exchange(
             call(
-                functools.partial(input_kernel, e),
+                functools.partial(input_kernel, e), 16,
                 (shape((half, feats)),) * n,
                 [],
                 1, z_ref, w3, grad_qkv[e], direct_sum,

time: 249 us -> 225 us (0.904)
  Pallas kernels: 49.4 us -> 26.4 us
  starting transfers between devices: 59.4 us -> 42.5 us
  waiting for transfers between devices: 59.2 us -> 67 us
  local copies, waits for them, and re-layouts: 16.8 us -> 23.9 us
    pallas_call x7 -> x6, Pallas kernels: 49.4 us -> 26.4 us  [call(): pl.pallas_call(kernel, out_shape=outs, in_specs=[SM] * n_smem + [VM] * (l...]
    all_to_all x2, waiting for transfers between devices: 11.2 us -> 23.4 us  [the longest x1 23.4 us: shards(): qkv = lax.all_to_all(qkv, 'ctx', 0, 0, tiled=True)]
    ppermute x12 -> x6, starting transfers between devices: 21.3 us -> 12.4 us  [shift(): return lax.ppermute(x, 'head', [(i, i + by) for i in range(low, high + 1)])]
    ppermute x9 -> x6, starting transfers between devices: 16.5 us -> 8.21 us  [rotate(): return lax.ppermute(x, 'head', [(i, (i + by) % size) for i in range(size)])]
    all_gather x1, waiting for transfers between devices: 0.02 us -> 8.24 us  [shards(): whole_out = lax.all_gather(slab_rows, ('head', 'ctx'), axis=0, tiled=True)]
    unnamed x54 -> x46, local copies, waits for them, and re-layouts: 12.5 us -> 20.6 us
    all_to_all x1, waiting for transfers between devices: 9.89 us -> 2.67 us  [shards(): folded = lax.all_to_all(folded, ('ctx', 'head'), 0, 0, tiled=True)]
    ppermute x9 -> x6, waiting for transfers between devices: 11.7 us -> 7.06 us  [rotate(): return lax.ppermute(x, 'head', [(i, (i + by) % size) for i in range(size)])]
  transfers between devices with their start and end apart: 27 -> 18, of which waited for: 9 -> 9; matrix products, arithmetic and copies ran while one was open for 6% -> 7% of each run, Pallas kernels for 12% -> 6%
where the time goes in v3:
time: 225 us; the launch traced here: 223 us
  waiting for transfers between devices  67 us (30%)
  starting transfers between devices  42.5 us (19%)
  blocking collectives  33.7 us (15%)
  Pallas kernels  26.4 us (12%)
  local copies, waits for them, and re-layouts  23.9 us (11%)
  other arithmetic  16 us (7%)
  between operations  13.6 us (6%)
    pallas_call x6, Pallas kernels, call(): pl.pallas_call(kernel, out_shape=outs, in_specs=[SM] * n_smem + [VM] * (l...  26.4 us
    all_to_all x1, waiting for transfers between devices, shards(): qkv = lax.all_to_all(qkv, 'ctx', 0, 0, tiled=True)  23.4 us
    unnamed x46, local copies, waits for them, and re-layouts  20.6 us
    ppermute x6, waiting for transfers between devices, shift(): return lax.ppermute(x, 'head', [(i, i + by) for i in range(low, high + 1)])  20.5 us
    all_to_all x1, blocking collectives, shards(): grad = lax.all_to_all(grad, ('ctx', 'head'), 0, 0, tiled=True)  17.8 us
    all_to_all x1, blocking collectives, shards(): grad_qkv = [lax.all_to_all(g, 'ctx', 0, 0, tiled=True) for g in grad_qkv]  15.9 us
    ppermute x6, starting transfers between devices, shift(): return lax.ppermute(x, 'head', [(i, i + by) for i in range(low, high + 1)])  12.4 us
    all_gather x1, waiting for transfers between devices, shards(): whole_out = lax.all_gather(slab_rows, ('head', 'ctx'), axis=0, tiled=True)  8.24 us
  transfers between devices with their start and end apart: 18, of which 9 were waited for; matrix products, arithmetic and copies ran while one was open for 7% of the time, Pallas kernels for 6%

profile of v3, /device:TPU:0, one launch (start us, length us, event | category | flops | bytes accessed | tf_op | source)
XLA Modules:
  0.0 223.1 jit_solution(524469077043682011)
XLA Ops:
  10.2 5.6 %collective-permute-start = (f32[512,256]{1,0:T(8,128)S(1)}, f32[512,256]{1,0:T(8,128)S(1)}, u32[]{:S(2)}, u32[]{:S(2)}) collective-permute-start(f32[512,256]{1,0:T(8,128)S(1)} %pad_maximum_fusion.2.own), channel_id=1, source_target_pairs={{0,1},{1,2},{2,3},{4,5},{5,6},{6,7},{8,9},{9,10},{10,11},{12,13},{... | collective-permute-start | bytes 1572872 | tf_op jit(solution)/shard_map/ppermute | solution.py:176
  17.0 4.2 %all-to-all-start = ((s32[8,2,5]{2,1,0:T(2,128)}), s32[8,2,5]{2,1,0:T(2,128)S(1)}, u32[]{:S(2)}, u32[]{:S(2)}) async-start(s32[8,2,5]{2,1,0:T(2,128)} %broadcast_in_dim.2), calls=%async_computation | async-start | bytes 16384 | tf_op jit(solution)/shard_map/all_to_all | solution.py:407
  21.2 1.7 broadcast_multiply_fusion
  22.9 2.8 %collective-permute-done.3.d1 = f32[512,256]{1,0:T(8,128)S(1)} collective-permute-done((f32[512,256]{1,0:T(8,128)S(1)}, f32[512,256]{1,0:T(8,128)S(1)}, u32[]{:S(2)}, u32[]{:S(2)}) %collective-permute-start.3) | collective-permute-done | bytes 524320 | tf_op jit(solution)/shard_map/ppermute | solution.py:176
  28.5 2.3 %pad_maximum_fusion.1 = f32[4,192,1024]{2,1,0:T(8,128)S(1)} fusion(f32[4,64,1024]{2,1,0:T(8,128)} %bitcast.16, f32[4,64,1024]{2,1,0:T(8,128)} %bitcast.17, f32[4,64,1024]{2,1,0:T(8,128)} %bitcast.18), kind=kLoop, calls=%fused_computation.7 | loop fusion | flops 1572864 | bytes 6291456 | tf_op jit(solution)/shard_map/concatenate | solution.py:410
  31.4 9.3 %collective-permute-done.4.d2 = f32[512,256]{1,0:T(8,128)S(1)} collective-permute-done((f32[512,256]{1,0:T(8,128)S(1)}, f32[512,256]{1,0:T(8,128)S(1)}, u32[]{:S(2)}, u32[]{:S(2)}) %collective-permute-start.4) | collective-permute-done | bytes 524320 | tf_op jit(solution)/shard_map/ppermute | solution.py:176
  43.5 2.3 %pad_maximum_fusion.w3 = bf16[768,3072]{1,0:T(8,128)(2,1)} fusion(bf16[768,1024]{1,0:T(8,128)(2,1)S(1)} %get-tuple-element.72, bf16[768,1024]{1,0:T(8,128)(2,1)S(1)} %get-tuple-element.71), kind=kLoop, calls=%fused_computation.2 | loop fusion | flops 14155776 | bytes 7864320 | tf_op jit(solution)/shard_map/concatenate | solution.py:414
  46.5 8.4 %collective-permute-done.5.d3 = f32[512,256]{1,0:T(8,128)} collective-permute-done((f32[512,256]{1,0:T(8,128)S(1)}, f32[512,256]{1,0:T(8,128)}, u32[]{:S(2)}, u32[]{:S(2)}) %collective-permute-start.5) | collective-permute-done | bytes 524320 | tf_op jit(solution)/shard_map/ppermute | solution.py:176
  54.9 6.2 %all-to-all-start.2 = ((f32[4,64,256]{2,1,0:T(8,128)}), f32[4,64,256]{2,1,0:T(8,128)S(1)}, u32[]{:S(2)}, u32[]{:S(2)}) async-start(f32[4,64,256]{2,1,0:T(8,128)} %bitcast.15), calls=%async_computation.2 | async-start | bytes 524288 | tf_op jit(solution)/shard_map/all_to_all | solution.py:430
  61.1 2.3 %copy-done.1 = bf16[768,3072]{1,0:T(8,128)(2,1)S(1)} copy-done((bf16[768,3072]{1,0:T(8,128)(2,1)S(1)}, bf16[768,3072]{1,0:T(8,128)(2,1)}, u32[]{:S(2)}) %copy-start.1) | copy-done | bytes 4718616
  63.4 6.1 %shard_map.100 = (f32[8,192,256]{2,1,0:T(8,128)S(1)}, f32[2,64,1024]{2,1,0:T(8,128)S(1)}) custom-call(s32[1]{0:T(128)} %bitcast.z_ref, bf16[768,3072]{1,0:T(8,128)(2,1)S(1)} %copy-done.1, f32[512,256]{1,0:T(8,128)S(1)} %pad_maximum_fusion.2.own, f32[512,256]{1,0:T(8,128)S(1)} %collective-permute-done.u1, f32[512,256]{1,0:T(8,128)} %collective-permute-done.1.u2, ...), custom_call_target="tpu_custom_call" | custom-call | tf_op jit(solution)/shard_map/pallas_call | solution.py:165
  72.2 3.7 %all-to-all-start.1 = ((f32[8,192,256]{2,1,0:T(8,128)}), f32[8,192,256]{2,1,0:T(8,128)S(1)}, u32[]{:S(2)}, u32[]{:S(2)}) async-start(f32[8,192,256]{2,1,0:T(8,128)} %copy-done.11), calls=%async_computation.1 | async-start | bytes 3145728 | tf_op jit(solution)/shard_map/all_to_all | solution.py:429
  77.2 23.4 %all-to-all-done.1.qkv = f32[8,192,256]{2,1,0:T(8,128)S(1)} async-done(((f32[8,192,256]{2,1,0:T(8,128)}), f32[8,192,256]{2,1,0:T(8,128)S(1)}, u32[]{:S(2)}, u32[]{:S(2)}) %all-to-all-start.1) | async-done | bytes 1572896 | tf_op jit(solution)/shard_map/all_to_all | solution.py:429
  101.8 6.0 %shard_map.101 = (f32[16,64,128]{2,1,0:T(8,128)S(1)}, f32[32,32,128]{2,1,0:T(8,128)S(1)}, bf16[16,640,128]{2,1,0:T(8,128)(2,1)S(1)}, bf16[16,640,128]{2,1,0:T(8,128)(2,1)S(1)}) custom-call(s32[16,5]{1,0:T(8,128)S(1)} %bitcast.11, s32[16,128,1]{2,1,0:T(8,128)S(1)} %copy-done.6, s32[16,128]{1,0:T(8,128)S(1)} %bitcast.14, f32[8,192,256]{2,1,0:T(8,128)S(1)} %all-to-all-done.1.qkv), custom_call_target="tpu_custom_call" | custom-call | tf_op jit(solution)/shard_map/pallas_call | solution.py:165
  112.4 4.2 %all-to-all-start.3 = ((f32[32,32,128]{2,1,0:T(8,128)}), f32[32,32,128]{2,1,0:T(8,128)S(1)}, u32[]{:S(2)}, u32[]{:S(2)}) async-start(f32[32,32,128]{2,1,0:T(8,128)} %copy-done.17), calls=%async_computation.3 | async-start | bytes 1048576 | tf_op jit(solution)/shard_map/all_to_all | solution.py:452
  116.6 8.2 %all-gather.2.cloned.1.call-done = f32[1024,1024]{1,0:T(8,128)} async-done(((f32[32,1024]{1,0:T(8,128)}), f32[1024,1024]{1,0:T(8,128)}) %all-gather.2.cloned.1.call-update) | async-done | bytes 4194320 | tf_op jit(solution)/shard_map/all_gather | solution.py:420
  124.9 5.1 %fusion = (bf16[1024,1024]{1,0:T(8,128)(2,1)}, bf16[1024,1024]{1,0:T(8,128)(2,1)}) fusion(f32[1024,1024]{1,0:T(8,128)} %all-gather.2.cloned.1.call-done), kind=kLoop, calls=%fused_computation.5 | loop fusion | flops 4194304 | bytes 8388608 | tf_op jit(solution)/shard_map/convert_element_type | solution.py:153
  129.9 2.7 %all-to-all-done.3.pieces = f32[32,32,128]{2,1,0:T(8,128)S(1)} async-done(((f32[32,32,128]{2,1,0:T(8,128)}), f32[32,32,128]{2,1,0:T(8,128)S(1)}, u32[]{:S(2)}, u32[]{:S(2)}) %all-to-all-start.3) | async-done | bytes 524320 | tf_op jit(solution)/shard_map/all_to_all | solution.py:452
  132.6 1.6 copy-done.4
  134.2 1.6 copy-done.5
  137.8 3.8 %shard_map.102 = (f32[32,32,128]{2,1,0:T(8,128)S(1)}, f32[64,1024]{1,0:T(8,128)S(1)}) custom-call(bf16[1024,1024]{1,0:T(8,128)(2,1)S(1)} %copy-done.5, bf16[1024,1024]{1,0:T(8,128)(2,1)S(1)} %copy-done.4, f32[2,64,1024]{2,1,0:T(8,128)S(1)} %copy-done.19, f32[4,64,256]{2,1,0:T(8,128)S(1)} %copy-done.13, f32[32,32,128]{2,1,0:T(8,128)S(1)} %all-to-all-done.3.pieces), custom_call_target="tpu_custom_call" | custom-call | tf_op jit(solution)/shard_map/pallas_call | solution.py:165
  141.6 17.8 %all_to_all.35.grad = f32[32,32,128]{2,1,0:T(8,128)S(1)} all-to-all(f32[32,32,128]{2,1,0:T(8,128)S(1)} %get-tuple-element.54), channel_id=1, replica_groups=mesh['ctx'=8,'head'=4] {'ctx','head'}, dimensions={0} | all-to-all | bytes 1048576 | tf_op jit(solution)/shard_map/all_to_all | solution.py:459
  159.3 8.7 %shard_map.103 = (f32[8,192,128]{2,1,0:T(8,128)S(1)}, f32[8,192,128]{2,1,0:T(8,128)S(1)}) custom-call(s32[16,5]{1,0:T(8,128)S(1)} %bitcast.12, f32[8,192,256]{2,1,0:T(8,128)S(1)} %all-to-all-done.1.qkv, bf16[16,640,128]{2,1,0:T(8,128)(2,1)S(1)} %copy-done.8, bf16[16,640,128]{2,1,0:T(8,128)(2,1)S(1)} %copy-done.10, f32[32,32,128]{2,1,0:T(8,128)S(1)} %all_to_all.35.grad, ...), custom_call_target="tpu_custom_call" | custom-call | tf_op jit(solution)/shard_map/pallas_call | solution.py:165
  168.1 15.9 %all_to_all.36.grads = f32[8,192,128]{2,1,0:T(8,128)S(1)} all-to-all(f32[8,192,128]{2,1,0:T(8,128)S(1)} %get-tuple-element.62), channel_id=1, replica_groups=mesh['ctx'=8,'head'=4] {'ctx'}, dimensions={0} | all-to-all | bytes 1572864 | tf_op jit(solution)/shard_map/all_to_all | solution.py:471
  184.0 3.5 %all-to-all-start.5 = ((f32[8,192,128]{2,1,0:T(8,128)}), f32[8,192,128]{2,1,0:T(8,128)S(1)}, u32[]{:S(2)}, u32[]{:S(2)}) async-start(f32[8,192,128]{2,1,0:T(8,128)} %copy-done.14), calls=%async_computation.5 | async-start | bytes 1572864 | tf_op jit(solution)/shard_map/all_to_all | solution.py:471
  187.5 2.3 %copy-done.2 = bf16[768,3072]{1,0:T(8,128)(2,1)S(1)} copy-done((bf16[768,3072]{1,0:T(8,128)(2,1)S(1)}, bf16[768,3072]{1,0:T(8,128)(2,1)}, u32[]{:S(2)}) %copy-start.2) | copy-done | bytes 4718616
  190.8 1.7 collective-permute-start.9
  194.9 5.2 %all-to-all-done.5.grads = f32[8,192,128]{2,1,0:T(8,128)S(1)} async-done(((f32[8,192,128]{2,1,0:T(8,128)}), f32[8,192,128]{2,1,0:T(8,128)S(1)}, u32[]{:S(2)}, u32[]{:S(2)}) %all-to-all-start.5) | async-done | bytes 786464 | tf_op jit(solution)/shard_map/all_to_all | solution.py:471
  200.1 2.3 %copy-done.3 = bf16[768,3072]{1,0:T(8,128)(2,1)S(1)} copy-done((bf16[768,3072]{1,0:T(8,128)(2,1)S(1)}, bf16[768,3072]{1,0:T(8,128)(2,1)}, u32[]{:S(2)}) %copy-start.3) | copy-done | bytes 4718616
  203.3 1.7 collective-permute-start.6
  208.4 2.2 collective-permute-done.6
  210.6 4.8 %collective-permute-done.7 = f32[128,256]{1,0:T(8,128)S(1)} collective-permute-done((f32[128,256]{1,0:T(8,128)S(1)}, f32[128,256]{1,0:T(8,128)S(1)}, u32[]{:S(2)}, u32[]{:S(2)}) %collective-permute-start.7) | collective-permute-done | bytes 131104 | tf_op jit(solution)/shard_map/ppermute | solution.py:181
  (73 shorter events, 32.0 us)
Async XLA Ops:
  6.5 39.3 %copy-start = (f32[256,1024]{1,0:T(8,128)S(1)}, f32[256,1024]{1,0:T(8,128)}, u32[]{:S(2)}) copy-start(f32[256,1024]{1,0:T(8,128)} %param.15) | copy-start | bytes 3145732
  8.9 16.8 %collective-permute-start.3 = (f32[512,256]{1,0:T(8,128)S(1)}, f32[512,256]{1,0:T(8,128)S(1)}, u32[]{:S(2)}, u32[]{:S(2)}) collective-permute-start(f32[512,256]{1,0:T(8,128)S(1)} %pad_maximum_fusion.2.own), channel_id=1, source_target_pairs={{1,0},{2,1},{3,2},{5,4},{6,5},{7,6},{9,8},{10,9},{11,10},{13,12},{... | collective-permute-start | bytes 1572872 | tf_op jit(solution)/shard_map/ppermute | solution.py:176
  10.2 16.8 %collective-permute-start = (f32[512,256]{1,0:T(8,128)S(1)}, f32[512,256]{1,0:T(8,128)S(1)}, u32[]{:S(2)}, u32[]{:S(2)}) collective-permute-start(f32[512,256]{1,0:T(8,128)S(1)} %pad_maximum_fusion.2.own), channel_id=1, source_target_pairs={{0,1},{1,2},{2,3},{4,5},{5,6},{6,7},{8,9},{9,10},{10,11},{12,13},{... | collective-permute-start | bytes 1572872 | tf_op jit(solution)/shard_map/ppermute | solution.py:176
  17.0 29.5 %all-to-all-start = ((s32[8,2,5]{2,1,0:T(2,128)}), s32[8,2,5]{2,1,0:T(2,128)S(1)}, u32[]{:S(2)}, u32[]{:S(2)}) async-start(s32[8,2,5]{2,1,0:T(2,128)} %broadcast_in_dim.2), calls=%async_computation | async-start | bytes 16384 | tf_op jit(solution)/shard_map/all_to_all | solution.py:407
  21.2 103.7 %all-gather.2.cloned.1.call-start = ((), (), s32[]{:S(2)}) async-start(), calls=%async_computation.7 | async-start | bytes 4325376 | tf_op jit(solution)/shard_map/all_gather | solution.py:420
  25.7 15.0 %collective-permute-start.4 = (f32[512,256]{1,0:T(8,128)S(1)}, f32[512,256]{1,0:T(8,128)S(1)}, u32[]{:S(2)}, u32[]{:S(2)}) collective-permute-start(f32[512,256]{1,0:T(8,128)S(1)} %collective-permute-done.3.d1), channel_id=1, source_target_pairs={{1,0},{2,1},{5,4},{6,5},{9,8},{10,9},{13,12},{14,13},{17,16},{18,1... | collective-permute-start | bytes 1572872 | tf_op jit(solution)/shard_map/ppermute | solution.py:176
  27.0 15.0 %collective-permute-start.1 = (f32[512,256]{1,0:T(8,128)S(1)}, f32[512,256]{1,0:T(8,128)}, u32[]{:S(2)}, u32[]{:S(2)}) collective-permute-start(f32[512,256]{1,0:T(8,128)S(1)} %collective-permute-done.u1), channel_id=1, source_target_pairs={{1,2},{2,3},{5,6},{6,7},{9,10},{10,11},{13,14},{14,15},{17,18},{18... | collective-permute-start | bytes 1572872 | tf_op jit(solution)/shard_map/ppermute | solution.py:176
  40.7 14.2 %collective-permute-start.5 = (f32[512,256]{1,0:T(8,128)S(1)}, f32[512,256]{1,0:T(8,128)}, u32[]{:S(2)}, u32[]{:S(2)}) collective-permute-start(f32[512,256]{1,0:T(8,128)S(1)} %collective-permute-done.4.d2), channel_id=1, source_target_pairs={{1,0},{5,4},{9,8},{13,12},{17,16},{21,20},{25,24},{29,28}} | collective-permute-start | bytes 1572872 | tf_op jit(solution)/shard_map/ppermute | solution.py:176
  42.0 12.9 %collective-permute-start.2 = (f32[512,256]{1,0:T(8,128)}, f32[512,256]{1,0:T(8,128)}, u32[]{:S(2)}, u32[]{:S(2)}) collective-permute-start(f32[512,256]{1,0:T(8,128)} %collective-permute-done.1.u2), channel_id=1, source_target_pairs={{2,3},{6,7},{10,11},{14,15},{18,19},{22,23},{26,27},{30,31}} | collective-permute-start | bytes 1572872 | tf_op jit(solution)/shard_map/ppermute | solution.py:176
  54.9 16.6 %all-to-all-start.2 = ((f32[4,64,256]{2,1,0:T(8,128)}), f32[4,64,256]{2,1,0:T(8,128)S(1)}, u32[]{:S(2)}, u32[]{:S(2)}) async-start(f32[4,64,256]{2,1,0:T(8,128)} %bitcast.15), calls=%async_computation.2 | async-start | bytes 524288 | tf_op jit(solution)/shard_map/all_to_all | solution.py:430
  61.1 2.3 %copy-start.1 = (bf16[768,3072]{1,0:T(8,128)(2,1)S(1)}, bf16[768,3072]{1,0:T(8,128)(2,1)}, u32[]{:S(2)}) copy-start(bf16[768,3072]{1,0:T(8,128)(2,1)} %pad_maximum_fusion.w3) | copy-start | bytes 14155780
  71.5 4.4 %copy-start.20 = (s32[2048]{0:T(1024)S(1)}, s32[2048]{0:T(1024)}, u32[]{:S(2)}) copy-start(s32[2048]{0:T(1024)} %param.18) | copy-start | bytes 24580
  72.2 28.4 %all-to-all-start.1 = ((f32[8,192,256]{2,1,0:T(8,128)}), f32[8,192,256]{2,1,0:T(8,128)S(1)}, u32[]{:S(2)}, u32[]{:S(2)}) async-start(f32[8,192,256]{2,1,0:T(8,128)} %copy-done.11), calls=%async_computation.1 | async-start | bytes 3145728 | tf_op jit(solution)/shard_map/all_to_all | solution.py:429
  107.9 1.5 copy-start.7
  109.3 1.5 copy-start.9
  112.4 20.2 %all-to-all-start.3 = ((f32[32,32,128]{2,1,0:T(8,128)}), f32[32,32,128]{2,1,0:T(8,128)S(1)}, u32[]{:S(2)}, u32[]{:S(2)}) async-start(f32[32,32,128]{2,1,0:T(8,128)} %copy-done.17), calls=%async_computation.3 | async-start | bytes 1048576 | tf_op jit(solution)/shard_map/all_to_all | solution.py:452
  132.6 1.6 copy-start.4
  134.2 1.6 copy-start.5
  137.8 21.5 %copy-start.8 = (bf16[16,640,128]{2,1,0:T(8,128)(2,1)S(1)}, bf16[16,640,128]{2,1,0:T(8,128)(2,1)}, u32[]{:S(2)}) copy-start(bf16[16,640,128]{2,1,0:T(8,128)(2,1)} %copy-done.7) | copy-start | bytes 7864324
  137.8 21.5 %copy-start.10 = (bf16[16,640,128]{2,1,0:T(8,128)(2,1)S(1)}, bf16[16,640,128]{2,1,0:T(8,128)(2,1)}, u32[]{:S(2)}) copy-start(bf16[16,640,128]{2,1,0:T(8,128)(2,1)} %copy-done.9) | copy-start | bytes 7864324
  137.8 21.5 %copy-start.16 = (f32[16,64,128]{2,1,0:T(8,128)S(1)}, f32[16,64,128]{2,1,0:T(8,128)}, u32[]{:S(2)}) copy-start(f32[16,64,128]{2,1,0:T(8,128)} %copy-done.15) | copy-start | bytes 1572868
  168.1 15.9 %copy-start.14 = (f32[8,192,128]{2,1,0:T(8,128)}, f32[8,192,128]{2,1,0:T(8,128)S(1)}, u32[]{:S(2)}) copy-start(f32[8,192,128]{2,1,0:T(8,128)S(1)} %get-tuple-element.56) | copy-start | bytes 2359300
  184.0 16.1 %all-to-all-start.5 = ((f32[8,192,128]{2,1,0:T(8,128)}), f32[8,192,128]{2,1,0:T(8,128)S(1)}, u32[]{:S(2)}, u32[]{:S(2)}) async-start(f32[8,192,128]{2,1,0:T(8,128)} %copy-done.14), calls=%async_computation.5 | async-start | bytes 1572864 | tf_op jit(solution)/shard_map/all_to_all | solution.py:471
  187.5 2.3 %copy-start.2 = (bf16[768,3072]{1,0:T(8,128)(2,1)S(1)}, bf16[768,3072]{1,0:T(8,128)(2,1)}, u32[]{:S(2)}) copy-start(bf16[768,3072]{1,0:T(8,128)(2,1)} %pad_maximum_fusion.w3) | copy-start | bytes 14155780
  190.8 15.1 %collective-permute-start.9 = (f32[128,256]{1,0:T(8,128)S(1)}, f32[128,256]{1,0:T(8,128)S(1)}, u32[]{:S(2)}, u32[]{:S(2)}) collective-permute-start(f32[128,256]{1,0:T(8,128)S(1)} %get-tuple-element.64), channel_id=1, source_target_pairs={{0,1},{1,2},{2,3},{3,0},{4,5},{5,6},{6,7},{7,4},{8,9},{9,10},{10,1... | collective-permute-start | bytes 393224 | tf_op jit(solution)/shard_map/ppermute | solution.py:181
  192.5 15.0 %collective-permute-start.10 = (f32[128,256]{1,0:T(8,128)S(1)}, f32[128,256]{1,0:T(8,128)S(1)}, u32[]{:S(2)}, u32[]{:S(2)}) collective-permute-start(f32[128,256]{1,0:T(8,128)S(1)} %get-tuple-element.65), channel_id=1, source_target_pairs={{0,2},{1,3},{2,0},{3,1},{4,6},{5,7},{6,4},{7,5},{8,10},{9,11},{10,... | collective-permute-start | bytes 393224 | tf_op jit(solution)/shard_map/ppermute | solution.py:181
  193.4 14.0 %collective-permute-start.11 = (f32[128,256]{1,0:T(8,128)S(1)}, f32[128,256]{1,0:T(8,128)}, u32[]{:S(2)}, u32[]{:S(2)}) collective-permute-start(f32[128,256]{1,0:T(8,128)S(1)} %get-tuple-element.66), channel_id=1, source_target_pairs={{0,3},{1,0},{2,1},{3,2},{4,7},{5,4},{6,5},{7,6},{8,11},{9,8},{10,9... | collective-permute-start | bytes 393224 | tf_op jit(solution)/shard_map/ppermute | solution.py:181
  200.1 2.3 %copy-start.3 = (bf16[768,3072]{1,0:T(8,128)(2,1)S(1)}, bf16[768,3072]{1,0:T(8,128)(2,1)}, u32[]{:S(2)}) copy-start(bf16[768,3072]{1,0:T(8,128)(2,1)} %pad_maximum_fusion.w3) | copy-start | bytes 14155780
  202.4 13.1 %copy-start.22 = (f32[256,256]{1,0:T(8,128)S(1)}, f32[256,256]{1,0:T(8,128)}, u32[]{:S(2)}) copy-start(f32[256,256]{1,0:T(8,128)} %copy-done.21) | copy-start | bytes 786436
  203.3 7.3 %collective-permute-start.6 = (f32[128,256]{1,0:T(8,128)S(1)}, f32[128,256]{1,0:T(8,128)S(1)}, u32[]{:S(2)}, u32[]{:S(2)}) collective-permute-start(f32[128,256]{1,0:T(8,128)S(1)} %get-tuple-element.59), channel_id=1, source_target_pairs={{0,1},{1,2},{2,3},{3,0},{4,5},{5,6},{6,7},{7,4},{8,9},{9,10},{10,1... | collective-permute-start | bytes 393224 | tf_op jit(solution)/shard_map/ppermute | solution.py:181
  205.0 10.4 %collective-permute-start.7 = (f32[128,256]{1,0:T(8,128)S(1)}, f32[128,256]{1,0:T(8,128)S(1)}, u32[]{:S(2)}, u32[]{:S(2)}) collective-permute-start(f32[128,256]{1,0:T(8,128)S(1)} %get-tuple-element.60), channel_id=1, source_target_pairs={{0,2},{1,3},{2,0},{3,1},{4,6},{5,7},{6,4},{7,5},{8,10},{9,11},{10,... | collective-permute-start | bytes 393224 | tf_op jit(solution)/shard_map/ppermute | solution.py:181
  205.9 9.5 %collective-permute-start.8 = (f32[128,256]{1,0:T(8,128)S(1)}, f32[128,256]{1,0:T(8,128)S(1)}, u32[]{:S(2)}, u32[]{:S(2)}) collective-permute-start(f32[128,256]{1,0:T(8,128)S(1)} %get-tuple-element.61), channel_id=1, source_target_pairs={{0,3},{1,0},{2,1},{3,2},{4,7},{5,4},{6,5},{7,6},{8,11},{9,8},{10,9... | collective-permute-start | bytes 393224 | tf_op jit(solution)/shard_map/ppermute | solution.py:181
  (9 other events, 8.6 us)
Sparse Core Ops, SparseCore 0:
  55.0 69.8 all-gather.1

commit v4 on v3

--- a/solution.py
+++ b/solution.py
@@ -161,12 +161,21 @@
     return lax.dot_general(a, b, (((1,), (1,)), ((), ())), preferred_element_type=F32)
 
 
-def call(kernel, mib, outs, scratch, n_smem, *args):
+def call(kernel, mib, outs, scratch, n_smem, *args, streamed_in=(), streamed_out=()):
+    grid = (NBLOCKS // GROUP,) if streamed_in or streamed_out else ()
+    one_in = pl.BlockSpec((GROUP, KVB * BLK, BLK), lambda c: (c, 0, 0))
+    in_specs = [SM] * n_smem + [VM] * (len(args) - n_smem)
+    for i in streamed_in:
+        in_specs[i] = one_in
+    out_specs = jax.tree.map(lambda _: VM, outs)
+    if streamed_out:
+        out_specs = tuple(one_in if i in streamed_out else VM for i in range(len(outs)))
     return pl.pallas_call(
         kernel,
         out_shape=outs,
-        in_specs=[SM] * n_smem + [VM] * (len(args) - n_smem),
-        out_specs=jax.tree.map(lambda _: VM, outs),
+        grid=grid,
+        in_specs=in_specs,
+        out_specs=out_specs,
         scratch_shapes=scratch,
         compiler_params=pltpu.CompilerParams(vmem_limit_bytes=mib * MIB),
     )(*args)
@@ -233,103 +242,116 @@
 def attend_kernel(
     lists, session_col, session_row, qkv, mixed, folded, p_high, p_low, q3, k3, v2
 ):
-    for b in range(NBLOCKS):
-        t = qkv[b // 2, :, (b % 2) * BLK : (b % 2 + 1) * BLK]
-        q_high, q_low = halves(t[:HD] * SCALE)
-        q3[b] = jnp.concatenate([q_high, q_high, q_low], axis=0)
-        k_high, k_low = halves(t[HD : 2 * HD].T)
-        k3[b] = jnp.concatenate([k_high, k_low, k_high], axis=1)
-        v_high, v_low = halves(t[2 * HD :])
-        v2[b] = jnp.concatenate([v_high, v_low], axis=0)
-
-    def body(c, carry):
-        blocks = [GROUP * c + e for e in range(GROUP)]
-        scores = []
-        for b in blocks:
-            mine = session_row[pl.ds(b, 1), :]
-            tiles = []
-            for j in range(KVB):
-                other = lists[b, j]
-                s = mm(k3[other], q3[b])
-                tiles.append(jnp.where(session_col[other] == mine, s, -1e30))
-            scores.append(jnp.concatenate(tiles, axis=0))
-        tops = [jnp.max(s, axis=0, keepdims=True) for s in scores]
-        expos = [jnp.exp(s - top) for s, top in zip(scores, tops)]
-        scales = [1.0 / jnp.sum(expo, axis=0, keepdims=True) for expo in expos]
-        for b, e, expo, each in zip(blocks, range(GROUP), expos, scales):
-            high, low = halves(expo * each)
-            p_high[b] = high
-            p_low[b] = low
-            values = jnp.concatenate([v2[lists[b, j]] for j in range(KVB)], axis=1)
-            both = mm(values, high)
-            block = both[:HD] + both[HD:] + mm(values[:HD], low)
-            mixed[b] = block
-            folded[2 * b], folded[2 * b + 1] = fold(block)
-        return carry
-
-    lax.fori_loop(0, NBLOCKS // GROUP, body, 0)
+    c = pl.program_id(0)
+
+    @pl.when(c == 0)
+    def _():
+        for b in range(NBLOCKS):
+            t = qkv[b // 2, :, (b % 2) * BLK : (b % 2 + 1) * BLK]
+            q_high, q_low = halves(t[:HD] * SCALE)
+            q3[b] = jnp.concatenate([q_high, q_high, q_low], axis=0)
+            k_high, k_low = halves(t[HD : 2 * HD].T)
+            k3[b] = jnp.concatenate([k_high, k_low, k_high], axis=1)
+            v_high, v_low = halves(t[2 * HD :])
+            v2[b] = jnp.concatenate([v_high, v_low], axis=0)
+
+    blocks = [GROUP * c + e for e in range(GROUP)]
+    scores = []
+    for b in blocks:
+        mine = session_row[pl.ds(b, 1), :]
+        tiles = []
+        for j in range(KVB):
+            other = lists[b, j]
+            s = mm(k3[other], q3[b])
+            tiles.append(jnp.where(session_col[other] == mine, s, -1e30))
+        scores.append(jnp.concatenate(tiles, axis=0))
+    tops = [jnp.max(s, axis=0, keepdims=True) for s in scores]
+    expos = [jnp.exp(s - top) for s, top in zip(scores, tops)]
+    scales = [1.0 / jnp.sum(expo, axis=0, keepdims=True) for expo in expos]
+    for b, e, expo, each in zip(blocks, range(GROUP), expos, scales):
+        high, low = halves(expo * each)
+        p_high[e] = high
+        p_low[e] = low
+        values = jnp.concatenate([v2[lists[b, j]] for j in range(KVB)], axis=1)
+        both = mm(values, high)
+        block = both[:HD] + both[HD:] + mm(values[:HD], low)
+        mixed[b] = block
+        folded[2 * b], folded[2 * b + 1] = fold(block)
 
 
 def attend_back_kernel(
     lists, qkv, p_high, p_low, grad, mixed, out0, out1, q2, k2, v3, acc
 ):
     out = (out0, out1)
-    for b in range(NBLOCKS):
-        t = qkv[b // 2, :, (b % 2) * BLK : (b % 2 + 1) * BLK]
-        q_high, q_low = halves(t[:HD])
-        q2[b] = jnp.concatenate([q_high, q_low], axis=0)
-        k_high, k_low = halves(t[HD : 2 * HD])
-        k2[b] = jnp.concatenate([k_high, k_low], axis=0)
-        v_high, v_low = halves(t[2 * HD :].T)
-        v3[b] = jnp.concatenate([v_high, v_low, v_high], axis=1)
-    acc[...] = jnp.zeros_like(acc)
-
-    def body(c, carry):
-        blocks = [GROUP * c + e for e in range(GROUP)]
-        grads = [unfold(grad[2 * b], grad[2 * b + 1]) for b in blocks]
-        parts = [halves(g) for g in grads]
-        probs_grads = []
-        for b, (g_high, g_low) in zip(blocks, parts):
-            g3 = jnp.concatenate([g_high, g_high, g_low], axis=0)
-            probs_grads.append(
-                jnp.concatenate([mm(v3[lists[b, j]], g3) for j in range(KVB)], axis=0)
-            )
-        added = []
-        for e, b in enumerate(blocks):
-            delta = jnp.sum(grads[e] * mixed[b], axis=0, keepdims=True)
-            g2 = jnp.concatenate(parts[e], axis=0)
-            ph, pw = p_high[b], p_low[b]
-            probs = ph.astype(F32) + pw.astype(F32)
-            s_high, s_low = halves(probs * (probs_grads[e] - delta) * SCALE)
-            keys = jnp.concatenate([k2[lists[b, j]] for j in range(KVB)], axis=1)
-            both = mm(keys, s_high)
-            out[e % 2][(GROUP // 2) * c + e // 2, 0:HD] = (
-                both[:HD] + both[HD:] + mm(keys[:HD], s_low)
-            )
-            query = q2[b]
-            both = mm_nt(query, s_high)
-            grad_keys = both[:HD] + both[HD:] + mm_nt(query[:HD], s_low)
-            both = mm_nt(g2, ph)
-            grad_values = both[:HD] + both[HD:] + mm_nt(g2[:HD], pw)
-            added.append(jnp.concatenate([grad_keys, grad_values], axis=0))
-        for b, both in zip(blocks, added):
-            for j in range(KVB):
-                acc[lists[b, j]] += both[:, j * BLK : (j + 1) * BLK]
-        return carry
-
-    lax.fori_loop(0, NBLOCKS // GROUP, body, 0)
-    for b in range(NBLOCKS):
-        out[b % 2][b // 2, HD : 3 * HD] = acc[b]
+    c = pl.program_id(0)
+
+    @pl.when(c == 0)
+    def _():
+        for b in range(NBLOCKS):
+            t = qkv[b // 2, :, (b % 2) * BLK : (b % 2 + 1) * BLK]
+            q_high, q_low = halves(t[:HD])
+            q2[b] = jnp.concatenate([q_high, q_low], axis=0)
+            k_high, k_low = halves(t[HD : 2 * HD])
+            k2[b] = jnp.concatenate([k_high, k_low], axis=0)
+            v_high, v_low = halves(t[2 * HD :].T)
+            v3[b] = jnp.concatenate([v_high, v_low, v_high], axis=1)
+        acc[...] = jnp.zeros_like(acc)
+
+    blocks = [GROUP * c + e for e in range(GROUP)]
+    grads = [unfold(grad[2 * b], grad[2 * b + 1]) for b in blocks]
+    parts = [halves(g) for g in grads]
+    probs_grads = []
+    for b, (g_high, g_low) in zip(blocks, parts):
+        g3 = jnp.concatenate([g_high, g_high, g_low], axis=0)
+        probs_grads.append(
+            jnp.concatenate([mm(v3[lists[b, j]], g3) for j in range(KVB)], axis=0)
+        )
+    added = []
+    for e, b in enumerate(blocks):
+        delta = jnp.sum(grads[e] * mixed[b], axis=0, keepdims=True)
+        g2 = jnp.concatenate(parts[e], axis=0)
+        ph, pw = p_high[e], p_low[e]
+        probs = ph.astype(F32) + pw.astype(F32)
+        s_high, s_low = halves(probs * (probs_grads[e] - delta) * SCALE)
+        keys = jnp.concatenate([k2[lists[b, j]] for j in range(KVB)], axis=1)
+        both = mm(keys, s_high)
+        out[e % 2][(GROUP // 2) * c + e // 2, 0:HD] = (
+            both[:HD] + both[HD:] + mm(keys[:HD], s_low)
+        )
+        query = q2[b]
+        both = mm_nt(query, s_high)
+        grad_keys = both[:HD] + both[HD:] + mm_nt(query[:HD], s_low)
+        both = mm_nt(g2, ph)
+        grad_values = both[:HD] + both[HD:] + mm_nt(g2[:HD], pw)
+        added.append(jnp.concatenate([grad_keys, grad_values], axis=0))
+    for b, both in zip(blocks, added):
+        for j in range(KVB):
+            acc[lists[b, j]] += both[:, j * BLK : (j + 1) * BLK]
+
+    @pl.when(c == NBLOCKS // GROUP - 1)
+    def _():
+        for b in range(NBLOCKS):
+            out[b % 2][b // 2, HD : 3 * HD] = acc[b]
+
+
+def split_kernel(slabs, high, low):
+    members, n = slabs.shape[:2]
+    slab = high.shape[0] // (members * n)
+    for i in range(members):
+        for j in range(n):
+            at = slice((j * members + i) * slab, (j * members + i + 1) * slab)
+            high[at], low[at] = halves(slabs[i, j, :slab])
 
 
 def norm_kernel(
-    w_high, w_low, rows, ups, pieces, out, direct_sum, upstream, mixed
+    z_ref, w_high, w_low, rows, ups, pieces, out, direct_sum, upstream, mixed
 ):
     n = 4
     quarter, width = direct_sum.shape
     feats = width // n
     for k in range(n):
-        upstream[:, k * feats : (k + 1) * feats] = ups[k]
+        start = pl.multiple_of(z_ref[0] * quarter, quarter)
+        upstream[:, k * feats : (k + 1) * feats] = ups[k, pl.ds(start, quarter)]
     for group in range(n):
         for h in range(n):
             at = group * feats + h * HD
@@ -404,31 +426,29 @@
         downs.append(shift(downs[-1], -1, 1, n - step))
     gathered = [own] + ups[1:] + downs[1:]
 
-    lists = lax.all_to_all(
-        jnp.broadcast_to(block_lists[None], (members,) + block_lists.shape), "ctx", 0, 0, tiled=True
-    ).reshape(-1, KVB)
+    slab_rows = lax.dynamic_slice_in_dim(w_out, lax.axis_index("ctx") * slab, slab, 0)
+    listed = block_lists.reshape(1, -1).astype(F32)
+    listed = jnp.pad(listed, ((0, 7), (0, width - listed.shape[1])))
+    slabs = lax.all_gather(jnp.concatenate([slab_rows, listed]), "head", axis=0)
+    slabs = lax.all_gather(slabs, "ctx", axis=0)
+    lists = slabs[:, 0, slab, : block_lists.size].astype(jnp.int32).reshape(-1, KVB)
+    out_high, out_low = call(
+        split_kernel, 24, (shape((width, width), BF16),) * 2, [], 0, slabs
+    )
     weights = jnp.concatenate(
         [w.reshape(heads, HD, width) for w in (w_query, w_key, w_value)], axis=1
     ).reshape(heads * part, width)
     high, low = halves_outside(weights)
     w3 = jnp.concatenate([high, low, high], axis=1)
-    slab_rows = lax.dynamic_slice_in_dim(w_out, lax.axis_index("ctx") * slab, slab, 0)
-    upstream = (probe * gain).reshape(n, quarter, feats)
-    gathered, w3, lists, slab_rows, upstream = lax.optimization_barrier(
-        (gathered, w3, lists, slab_rows, upstream)
-    )
-    whole_out = lax.all_gather(slab_rows, ("head", "ctx"), axis=0, tiled=True)
-    out_high, out_low = halves_outside(whole_out)
-
     qkv, rows = call(
         project_kernel, 20,
         (shape((members, part, tokens)), shape((2, quarter, width))),
         [pltpu.VMEM((2 * tokens, 3 * width), BF16)],
         1, z_ref, w3, *gathered,
     )
+    qkv, upstream = lax.optimization_barrier((qkv, probe * gain))
     qkv = lax.all_to_all(qkv, "ctx", 0, 0, tiled=True)
-    upstream = lax.all_to_all(upstream, "head", 0, 0, tiled=True)
-    qkv, upstream = lax.optimization_barrier((qkv, upstream))
+    upstream = lax.all_gather(upstream, "head", axis=0)
 
     blocks = members * tokens // BLK
     everyone = members * n
@@ -447,14 +467,14 @@
             pltpu.VMEM((blocks, BLK, part), BF16),
             pltpu.VMEM((blocks, 2 * HD, BLK), BF16),
         ],
-        1, lists, session_col, session_row, qkv,
+        1, lists, session_col, session_row, qkv, streamed_out=(2, 3),
     )
     folded = lax.all_to_all(folded, ("ctx", "head"), 0, 0, tiled=True)
     grad, direct_sum = call(
         norm_kernel, 20,
         (shape((everyone, HD // 2, BLK)), shape((quarter, width))),
         [pltpu.VMEM((quarter, width), F32), pltpu.VMEM((width, 2 * quarter), F32)],
-        0, out_high, out_low, rows, upstream, folded,
+        1, z_ref, out_high, out_low, rows, upstream, folded,
     )
     grad = lax.all_to_all(grad, ("ctx", "head"), 0, 0, tiled=True)
     grad_qkv = call(
@@ -466,7 +486,7 @@
             pltpu.VMEM((blocks, BLK, part), BF16),
             pltpu.VMEM((blocks, 2 * HD, BLK), F32),
         ],
-        1, lists, qkv, p_high, p_low, grad, mixed,
+        1, lists, qkv, p_high, p_low, grad, mixed, streamed_in=(2, 3),
     )
     grad_qkv = [lax.all_to_all(g, "ctx", 0, 0, tiled=True) for g in grad_qkv]
     totals = []

time: 225 us -> 223 us (level)
  blocking collectives: 33.7 us -> 53.6 us
  starting transfers between devices: 42.5 us -> 31.1 us
  waiting for transfers between devices: 67 us -> 58.4 us
  other arithmetic: 16 us -> 11.9 us
    all_gather x0 -> x1, blocking collectives: none -> 19.4 us  [shards(): slabs = lax.all_gather(jnp.concatenate([slab_rows, listed]), 'head', axis=0)]
    all_to_all x2 -> x0, starting transfers between devices: 10.4 us -> none  [the longest x1 6.19 us: shards(): upstream = lax.all_to_all(upstream, 'head', 0, 0, tiled=True)]
    all_gather x1 -> x2, waiting for transfers between devices: 8.24 us -> 0.01 us  [the longest x1 0.01 us: shards(): upstream = lax.all_gather(upstream, 'head', axis=0)]
    all_to_all x1, waiting for transfers between devices: 2.67 us -> 8.67 us  [shards(): folded = lax.all_to_all(folded, ('ctx', 'head'), 0, 0, tiled=True)]
    all_to_all x1, waiting for transfers between devices: 23.4 us -> 18 us  [shards(): qkv = lax.all_to_all(qkv, 'ctx', 0, 0, tiled=True)]
    convert_element_type x2 -> x1, other arithmetic: 5.72 us -> 2.31 us  [halves_outside(): return (rounded.astype(BF16), (x - rounded).astype(BF16))]
    unnamed x46 -> x60, local copies, waits for them, and re-layouts: 20.6 us -> 23.6 us
    pallas_call x6 -> x7, Pallas kernels: 26.4 us -> 27.1 us  [call(): pl.pallas_call(kernel, out_shape=outs, grid=grid, in_specs=in_specs, out_...]
  transfers between devices with their start and end apart: 18 -> 17, of which waited for: 9 -> 8; matrix products, arithmetic and copies ran while one was open for 7% -> 5% of each run, Pallas kernels for 6% -> 7%
where the time goes in v4:
time: 223 us; the launch traced here: 221 us
  waiting for transfers between devices  58.4 us (26%)
  blocking collectives  53.6 us (24%)
  starting transfers between devices  31.1 us (14%)
  Pallas kernels  27.1 us (12%)
  local copies, waits for them, and re-layouts  25.2 us (11%)
  between operations  13.7 us (6%)
  other arithmetic  11.9 us (5%)
    pallas_call x7, Pallas kernels, call(): pl.pallas_call(kernel, out_shape=outs, grid=grid, in_specs=in_specs, out_...  27.1 us
    unnamed x60, local copies, waits for them, and re-layouts  23.6 us
    all_gather x1, blocking collectives, shards(): slabs = lax.all_gather(jnp.concatenate([slab_rows, listed]), 'head', axis=0)  19.4 us
    ppermute x6, waiting for transfers between devices, shift(): return lax.ppermute(x, 'head', [(i, i + by) for i in range(low, high + 1)])  18.8 us
    all_to_all x1, blocking collectives, shards(): grad = lax.all_to_all(grad, ('ctx', 'head'), 0, 0, tiled=True)  18.3 us
    all_to_all x1, waiting for transfers between devices, shards(): qkv = lax.all_to_all(qkv, 'ctx', 0, 0, tiled=True)  18 us
    all_to_all x1, blocking collectives, shards(): grad_qkv = [lax.all_to_all(g, 'ctx', 0, 0, tiled=True) for g in grad_qkv]  15.9 us
    ppermute x6, starting transfers between devices, shift(): return lax.ppermute(x, 'head', [(i, i + by) for i in range(low, high + 1)])  11.4 us
  transfers between devices with their start and end apart: 17, of which 8 were waited for; matrix products, arithmetic and copies ran while one was open for 5% of the time, Pallas kernels for 7%

profile of v4, /device:TPU:0, one launch (start us, length us, event | category | flops | bytes accessed | tf_op | source)
XLA Modules:
  0.0 220.9 jit_solution(6531142777158138137)
XLA Ops:
  7.8 19.4 %all-gather = f32[160,1024]{1,0:T(8,128)} all-gather(f32[40,1024]{1,0:T(8,128)S(1)} %select_maximum_fusion), channel_id=2, replica_groups=mesh['ctx'=8,'head'=4] {'head'}, dimensions={0}, use_global_device_ids=true | all-gather | bytes 819200 | tf_op jit(solution)/shard_map/all_gather | solution.py:432
  29.9 4.6 %collective-permute-start = (f32[512,256]{1,0:T(8,128)S(1)}, f32[512,256]{1,0:T(8,128)S(1)}, u32[]{:S(2)}, u32[]{:S(2)}) collective-permute-start(f32[512,256]{1,0:T(8,128)S(1)} %pad_maximum_fusion.2.own), channel_id=1, source_target_pairs={{0,1},{1,2},{2,3},{4,5},{5,6},{6,7},{8,9},{9,10},{10,11},{12,13},{... | collective-permute-start | bytes 1572872 | tf_op jit(solution)/shard_map/ppermute | solution.py:185
  34.5 7.5 %collective-permute-done.3.d1 = f32[512,256]{1,0:T(8,128)S(1)} collective-permute-done((f32[512,256]{1,0:T(8,128)S(1)}, f32[512,256]{1,0:T(8,128)S(1)}, u32[]{:S(2)}, u32[]{:S(2)}) %collective-permute-start.3) | collective-permute-done | bytes 524320 | tf_op jit(solution)/shard_map/ppermute | solution.py:185
  44.8 1.6 pad_maximum_fusion.1
  46.5 2.3 %fusion = (bf16[768,1024]{1,0:T(8,128)(2,1)}, bf16[768,1024]{1,0:T(8,128)(2,1)}) fusion(f32[4,192,1024]{2,1,0:T(8,128)S(1)} %pad_maximum_fusion.1), kind=kLoop, calls=%fused_computation.3 | loop fusion | flops 3145728 | bytes 6291456 | tf_op jit(solution)/shard_map/convert_element_type | solution.py:153
  48.8 5.7 %collective-permute-done.4.d2 = f32[512,256]{1,0:T(8,128)S(1)} collective-permute-done((f32[512,256]{1,0:T(8,128)S(1)}, f32[512,256]{1,0:T(8,128)S(1)}, u32[]{:S(2)}, u32[]{:S(2)}) %collective-permute-start.4) | collective-permute-done | bytes 524320 | tf_op jit(solution)/shard_map/ppermute | solution.py:185
  58.0 2.6 %pad_maximum_fusion.w3 = bf16[768,3072]{1,0:T(8,128)(2,1)S(1)} fusion(bf16[768,1024]{1,0:T(8,128)(2,1)} %get-tuple-element.52, bf16[768,1024]{1,0:T(8,128)(2,1)} %get-tuple-element.51), kind=kLoop, calls=%fused_computation | loop fusion | flops 14155776 | bytes 7864320 | tf_op jit(solution)/shard_map/concatenate | solution.py:442
  60.7 5.5 %collective-permute-done.5.d3 = f32[512,256]{1,0:T(8,128)} collective-permute-done((f32[512,256]{1,0:T(8,128)S(1)}, f32[512,256]{1,0:T(8,128)}, u32[]{:S(2)}, u32[]{:S(2)}) %collective-permute-start.5) | collective-permute-done | bytes 524320 | tf_op jit(solution)/shard_map/ppermute | solution.py:185
  66.2 6.1 %shard_map.100 = (f32[8,192,256]{2,1,0:T(8,128)S(1)}, f32[2,64,1024]{2,1,0:T(8,128)S(1)}) custom-call(s32[1]{0:T(128)} %bitcast.z_ref, bf16[768,3072]{1,0:T(8,128)(2,1)S(1)} %pad_maximum_fusion.w3, f32[512,256]{1,0:T(8,128)S(1)} %pad_maximum_fusion.2.own, f32[512,256]{1,0:T(8,128)S(1)} %collective-permute-done.u1, f32[512,256]{1,0:T(8,128)} %collective-permute-done.1.u2, ...), custom_call_target="tpu_custom_call" | custom-call | tf_op jit(solution)/shard_map/pallas_call | solution.py:173
  74.3 4.1 %all-to-all-start = ((f32[8,192,256]{2,1,0:T(8,128)}), f32[8,192,256]{2,1,0:T(8,128)S(1)}, u32[]{:S(2)}, u32[]{:S(2)}) async-start(f32[8,192,256]{2,1,0:T(8,128)} %copy-done.14), calls=%async_computation | async-start | bytes 3145728 | tf_op jit(solution)/shard_map/all_to_all | solution.py:450
  81.4 18.0 %all-to-all-done.qkv = f32[8,192,256]{2,1,0:T(8,128)S(1)} async-done(((f32[8,192,256]{2,1,0:T(8,128)}), f32[8,192,256]{2,1,0:T(8,128)S(1)}, u32[]{:S(2)}, u32[]{:S(2)}) %all-to-all-start) | async-done | bytes 1572896 | tf_op jit(solution)/shard_map/all_to_all | solution.py:450
  100.6 6.1 %shard_map.101 = (f32[16,64,128]{2,1,0:T(8,128)S(1)}, f32[32,32,128]{2,1,0:T(8,128)S(1)}, bf16[16,640,128]{2,1,0:T(8,128)(2,1)S(1)}, bf16[16,640,128]{2,1,0:T(8,128)(2,1)S(1)}) custom-call(s32[16,5]{1,0:T(8,128)S(1)} %convert_element_type.34.lists, s32[16,128,1]{2,1,0:T(8,128)S(1)} %copy-done.5, s32[16,128]{1,0:T(8,128)S(1)} %bitcast.16, ...), custom_call_target="tpu_custom_call" | custom-call | tf_op jit(solution)/shard_map/pallas_call | solution.py:173
  106.7 1.6 copy-done.6
  111.3 3.8 %all-to-all-start.1 = ((f32[32,32,128]{2,1,0:T(8,128)}), f32[32,32,128]{2,1,0:T(8,128)S(1)}, u32[]{:S(2)}, u32[]{:S(2)}) async-start(f32[32,32,128]{2,1,0:T(8,128)} %copy-done.21), calls=%async_computation.1 | async-start | bytes 1048576 | tf_op jit(solution)/shard_map/all_to_all | solution.py:472
  115.2 2.5 %copy-done.4 = f32[32,40,1024]{2,1,0:T(8,128)S(1)} copy-done((f32[32,40,1024]{2,1,0:T(8,128)S(1)}, f32[32,40,1024]{2,1,0:T(8,128)}, u32[]{:S(2)}) %copy-start.4) | copy-done | bytes 5242904
  120.9 8.7 %all-to-all-done.1.pieces = f32[32,32,128]{2,1,0:T(8,128)S(1)} async-done(((f32[32,32,128]{2,1,0:T(8,128)}), f32[32,32,128]{2,1,0:T(8,128)S(1)}, u32[]{:S(2)}, u32[]{:S(2)}) %all-to-all-start.1) | async-done | bytes 524320 | tf_op jit(solution)/shard_map/all_to_all | solution.py:472
  129.5 1.6 copy-done.11
  131.1 1.6 copy-done.13
  135.0 3.8 %shard_map.103 = (f32[32,32,128]{2,1,0:T(8,128)S(1)}, f32[64,1024]{1,0:T(8,128)S(1)}) custom-call(s32[1]{0:T(128)} %bitcast.z_ref, bf16[1024,1024]{1,0:T(8,128)(2,1)S(1)} %copy-done.11, bf16[1024,1024]{1,0:T(8,128)(2,1)S(1)} %copy-done.13, f32[2,64,1024]{2,1,0:T(8,128)S(1)} %copy-done.18, f32[4,256,256]{2,1,0:T(8,128)S(1)} %bitcast.14, ...), custom_call_target="tpu_custom_call" | custom-call | tf_op jit(solution)/shard_map/pallas_call | solution.py:173
  138.8 18.3 %all_to_all.25.grad = f32[32,32,128]{2,1,0:T(8,128)S(1)} all-to-all(f32[32,32,128]{2,1,0:T(8,128)S(1)} %get-tuple-element.36), channel_id=1, replica_groups=mesh['ctx'=8,'head'=4] {'ctx','head'}, dimensions={0} | all-to-all | bytes 1048576 | tf_op jit(solution)/shard_map/all_to_all | solution.py:479
  157.0 8.8 %shard_map.104 = (f32[8,192,128]{2,1,0:T(8,128)S(1)}, f32[8,192,128]{2,1,0:T(8,128)S(1)}) custom-call(s32[16,5]{1,0:T(8,128)S(1)} %convert_element_type.34.lists, f32[8,192,256]{2,1,0:T(8,128)S(1)} %all-to-all-done.qkv, bf16[16,640,128]{2,1,0:T(8,128)(2,1)S(1)} %copy-done.7, bf16[16,640,128]{2,1,0:T(8,128)(2,1)S(1)} %copy-done.9, ...), custom_call_target="tpu_custom_call" | custom-call | tf_op jit(solution)/shard_map/pallas_call | solution.py:173
  165.9 15.9 %all_to_all.26.grads = f32[8,192,128]{2,1,0:T(8,128)S(1)} all-to-all(f32[8,192,128]{2,1,0:T(8,128)S(1)} %get-tuple-element.44), channel_id=1, replica_groups=mesh['ctx'=8,'head'=4] {'ctx'}, dimensions={0} | all-to-all | bytes 1572864 | tf_op jit(solution)/shard_map/all_to_all | solution.py:491
  181.8 3.5 %all-to-all-start.3 = ((f32[8,192,128]{2,1,0:T(8,128)}), f32[8,192,128]{2,1,0:T(8,128)S(1)}, u32[]{:S(2)}, u32[]{:S(2)}) async-start(f32[8,192,128]{2,1,0:T(8,128)} %copy-done.16), calls=%async_computation.3 | async-start | bytes 1572864 | tf_op jit(solution)/shard_map/all_to_all | solution.py:491
  185.4 2.3 %copy-done.2 = bf16[768,3072]{1,0:T(8,128)(2,1)S(1)} copy-done((bf16[768,3072]{1,0:T(8,128)(2,1)S(1)}, bf16[768,3072]{1,0:T(8,128)(2,1)}, u32[]{:S(2)}) %copy-start.2) | copy-done | bytes 4718616
  188.6 1.7 collective-permute-start.9
  191.2 1.5 collective-permute-start.11
  192.8 5.1 %all-to-all-done.3.grads = f32[8,192,128]{2,1,0:T(8,128)S(1)} async-done(((f32[8,192,128]{2,1,0:T(8,128)}), f32[8,192,128]{2,1,0:T(8,128)S(1)}, u32[]{:S(2)}, u32[]{:S(2)}) %all-to-all-start.3) | async-done | bytes 786464 | tf_op jit(solution)/shard_map/all_to_all | solution.py:491
  197.9 2.3 %copy-done.3 = bf16[768,3072]{1,0:T(8,128)(2,1)S(1)} copy-done((bf16[768,3072]{1,0:T(8,128)(2,1)S(1)}, bf16[768,3072]{1,0:T(8,128)(2,1)}, u32[]{:S(2)}) %copy-start.3) | copy-done | bytes 4718616
  201.1 1.7 collective-permute-start.6
  203.8 1.5 collective-permute-start.8
  206.2 2.2 collective-permute-done.6
  208.4 4.9 %collective-permute-done.7 = f32[128,256]{1,0:T(8,128)S(1)} collective-permute-done((f32[128,256]{1,0:T(8,128)S(1)}, f32[128,256]{1,0:T(8,128)S(1)}, u32[]{:S(2)}, u32[]{:S(2)}) %collective-permute-start.7) | collective-permute-done | bytes 131104 | tf_op jit(solution)/shard_map/ppermute | solution.py:190
  (91 shorter events, 30.3 us)
Async XLA Ops:
  6.5 22.0 %copy-start.25 = (f32[256,256]{1,0:T(8,128)S(1)}, f32[256,256]{1,0:T(8,128)}, u32[]{:S(2)}) copy-start(f32[256,256]{1,0:T(8,128)} %param.11) | copy-start | bytes 786436
  6.5 74.0 %all-gather.6.cloned.1.call-start = ((), (), s32[]{:S(2)}) async-start(), calls=%async_computation.5 | async-start | bytes 5898240 | tf_op jit(solution)/shard_map/all_gather | solution.py:433
  27.3 17.6 %copy-start.26 = (f32[256,1024]{1,0:T(8,128)S(1)}, f32[256,1024]{1,0:T(8,128)}, u32[]{:S(2)}) copy-start(f32[256,1024]{1,0:T(8,128)} %param.14) | copy-start | bytes 3145732
  27.3 17.6 %copy-start.27 = (f32[256,1024]{1,0:T(8,128)S(1)}, f32[256,1024]{1,0:T(8,128)}, u32[]{:S(2)}) copy-start(f32[256,1024]{1,0:T(8,128)} %param.13) | copy-start | bytes 3145732
  28.5 16.3 %copy-start.23 = (f32[256,256]{1,0:T(8,128)}, f32[256,256]{1,0:T(8,128)S(1)}, u32[]{:S(2)}) copy-start(f32[256,256]{1,0:T(8,128)S(1)} %get-tuple-element.50) | copy-start | bytes 786436
  28.6 13.4 %collective-permute-start.3 = (f32[512,256]{1,0:T(8,128)S(1)}, f32[512,256]{1,0:T(8,128)S(1)}, u32[]{:S(2)}, u32[]{:S(2)}) collective-permute-start(f32[512,256]{1,0:T(8,128)S(1)} %pad_maximum_fusion.2.own), channel_id=1, source_target_pairs={{1,0},{2,1},{3,2},{5,4},{6,5},{7,6},{9,8},{10,9},{11,10},{13,12},{... | collective-permute-start | bytes 1572872 | tf_op jit(solution)/shard_map/ppermute | solution.py:185
  29.9 13.4 %collective-permute-start = (f32[512,256]{1,0:T(8,128)S(1)}, f32[512,256]{1,0:T(8,128)S(1)}, u32[]{:S(2)}, u32[]{:S(2)}) collective-permute-start(f32[512,256]{1,0:T(8,128)S(1)} %pad_maximum_fusion.2.own), channel_id=1, source_target_pairs={{0,1},{1,2},{2,3},{4,5},{5,6},{6,7},{8,9},{9,10},{10,11},{12,13},{... | collective-permute-start | bytes 1572872 | tf_op jit(solution)/shard_map/ppermute | solution.py:185
  42.0 12.5 %collective-permute-start.4 = (f32[512,256]{1,0:T(8,128)S(1)}, f32[512,256]{1,0:T(8,128)S(1)}, u32[]{:S(2)}, u32[]{:S(2)}) collective-permute-start(f32[512,256]{1,0:T(8,128)S(1)} %collective-permute-done.3.d1), channel_id=1, source_target_pairs={{1,0},{2,1},{5,4},{6,5},{9,8},{10,9},{13,12},{14,13},{17,16},{18,1... | collective-permute-start | bytes 1572872 | tf_op jit(solution)/shard_map/ppermute | solution.py:185
  43.3 12.5 %collective-permute-start.1 = (f32[512,256]{1,0:T(8,128)S(1)}, f32[512,256]{1,0:T(8,128)}, u32[]{:S(2)}, u32[]{:S(2)}) collective-permute-start(f32[512,256]{1,0:T(8,128)S(1)} %collective-permute-done.u1), channel_id=1, source_target_pairs={{1,2},{2,3},{5,6},{6,7},{9,10},{10,11},{13,14},{14,15},{17,18},{18... | collective-permute-start | bytes 1572872 | tf_op jit(solution)/shard_map/ppermute | solution.py:185
  46.5 10.8 %copy-start.28 = (f32[256,256]{1,0:T(8,128)S(1)}, f32[256,256]{1,0:T(8,128)}, u32[]{:S(2)}) copy-start(f32[256,256]{1,0:T(8,128)} %param.17) | copy-start | bytes 786436
  46.5 10.8 %copy-start.29 = (f32[256]{0:T(256)S(1)}, f32[256]{0:T(256)}, u32[]{:S(2)}) copy-start(f32[256]{0:T(256)} %param.16) | copy-start | bytes 3076
  54.5 11.7 %collective-permute-start.5 = (f32[512,256]{1,0:T(8,128)S(1)}, f32[512,256]{1,0:T(8,128)}, u32[]{:S(2)}, u32[]{:S(2)}) collective-permute-start(f32[512,256]{1,0:T(8,128)S(1)} %collective-permute-done.4.d2), channel_id=1, source_target_pairs={{1,0},{5,4},{9,8},{13,12},{17,16},{21,20},{25,24},{29,28}} | collective-permute-start | bytes 1572872 | tf_op jit(solution)/shard_map/ppermute | solution.py:185
  55.8 10.4 %collective-permute-start.2 = (f32[512,256]{1,0:T(8,128)}, f32[512,256]{1,0:T(8,128)}, u32[]{:S(2)}, u32[]{:S(2)}) collective-permute-start(f32[512,256]{1,0:T(8,128)} %collective-permute-done.1.u2), channel_id=1, source_target_pairs={{2,3},{6,7},{10,11},{14,15},{18,19},{22,23},{26,27},{30,31}} | collective-permute-start | bytes 1572872 | tf_op jit(solution)/shard_map/ppermute | solution.py:185
  60.7 11.6 %copy-start.1 = (bf16[768,3072]{1,0:T(8,128)(2,1)}, bf16[768,3072]{1,0:T(8,128)(2,1)S(1)}, u32[]{:S(2)}) copy-start(bf16[768,3072]{1,0:T(8,128)(2,1)S(1)} %pad_maximum_fusion.w3) | copy-start | bytes 14155780
  74.3 4.8 %copy-start.22 = (s32[2048]{0:T(1024)S(1)}, s32[2048]{0:T(1024)}, u32[]{:S(2)}) copy-start(s32[2048]{0:T(1024)} %param.18) | copy-start | bytes 24580
  74.3 25.1 %all-to-all-start = ((f32[8,192,256]{2,1,0:T(8,128)}), f32[8,192,256]{2,1,0:T(8,128)S(1)}, u32[]{:S(2)}, u32[]{:S(2)}) async-start(f32[8,192,256]{2,1,0:T(8,128)} %copy-done.14), calls=%async_computation | async-start | bytes 3145728 | tf_op jit(solution)/shard_map/all_to_all | solution.py:450
  78.3 42.5 %all-gather.8.cloned.1.call-start = ((), (), s32[]{:S(2)}) async-start(), calls=%async_computation.6 | async-start | bytes 1310720 | tf_op jit(solution)/shard_map/all_gather | solution.py:451
  111.3 18.2 %all-to-all-start.1 = ((f32[32,32,128]{2,1,0:T(8,128)}), f32[32,32,128]{2,1,0:T(8,128)S(1)}, u32[]{:S(2)}, u32[]{:S(2)}) async-start(f32[32,32,128]{2,1,0:T(8,128)} %copy-done.21), calls=%async_computation.1 | async-start | bytes 1048576 | tf_op jit(solution)/shard_map/all_to_all | solution.py:472
  115.2 2.5 %copy-start.4 = (f32[32,40,1024]{2,1,0:T(8,128)S(1)}, f32[32,40,1024]{2,1,0:T(8,128)}, u32[]{:S(2)}) copy-start(f32[32,40,1024]{2,1,0:T(8,128)} %all-gather.6.cloned.1.call-done) | copy-start | bytes 15728644
  135.0 22.0 %copy-start.7 = (bf16[16,640,128]{2,1,0:T(8,128)(2,1)S(1)}, bf16[16,640,128]{2,1,0:T(8,128)(2,1)}, u32[]{:S(2)}) copy-start(bf16[16,640,128]{2,1,0:T(8,128)(2,1)} %copy-done.6) | copy-start | bytes 7864324
  135.0 22.0 %copy-start.9 = (bf16[16,640,128]{2,1,0:T(8,128)(2,1)S(1)}, bf16[16,640,128]{2,1,0:T(8,128)(2,1)}, u32[]{:S(2)}) copy-start(bf16[16,640,128]{2,1,0:T(8,128)(2,1)} %copy-done.8) | copy-start | bytes 7864324
  135.0 22.0 %copy-start.20 = (f32[16,64,128]{2,1,0:T(8,128)S(1)}, f32[16,64,128]{2,1,0:T(8,128)}, u32[]{:S(2)}) copy-start(f32[16,64,128]{2,1,0:T(8,128)} %copy-done.19) | copy-start | bytes 1572868
  165.9 15.9 %copy-start.16 = (f32[8,192,128]{2,1,0:T(8,128)}, f32[8,192,128]{2,1,0:T(8,128)S(1)}, u32[]{:S(2)}) copy-start(f32[8,192,128]{2,1,0:T(8,128)S(1)} %get-tuple-element.38) | copy-start | bytes 2359300
  181.8 16.1 %all-to-all-start.3 = ((f32[8,192,128]{2,1,0:T(8,128)}), f32[8,192,128]{2,1,0:T(8,128)S(1)}, u32[]{:S(2)}, u32[]{:S(2)}) async-start(f32[8,192,128]{2,1,0:T(8,128)} %copy-done.16), calls=%async_computation.3 | async-start | bytes 1572864 | tf_op jit(solution)/shard_map/all_to_all | solution.py:491
  185.3 2.3 %copy-start.2 = (bf16[768,3072]{1,0:T(8,128)(2,1)S(1)}, bf16[768,3072]{1,0:T(8,128)(2,1)}, u32[]{:S(2)}) copy-start(bf16[768,3072]{1,0:T(8,128)(2,1)} %copy-done.1) | copy-start | bytes 14155780
  188.6 15.2 %collective-permute-start.9 = (f32[128,256]{1,0:T(8,128)S(1)}, f32[128,256]{1,0:T(8,128)S(1)}, u32[]{:S(2)}, u32[]{:S(2)}) collective-permute-start(f32[128,256]{1,0:T(8,128)S(1)} %get-tuple-element.46), channel_id=1, source_target_pairs={{0,1},{1,2},{2,3},{3,0},{4,5},{5,6},{6,7},{7,4},{8,9},{9,10},{10,1... | collective-permute-start | bytes 393224 | tf_op jit(solution)/shard_map/ppermute | solution.py:190
  190.3 14.9 %collective-permute-start.10 = (f32[128,256]{1,0:T(8,128)S(1)}, f32[128,256]{1,0:T(8,128)S(1)}, u32[]{:S(2)}, u32[]{:S(2)}) collective-permute-start(f32[128,256]{1,0:T(8,128)S(1)} %get-tuple-element.47), channel_id=1, source_target_pairs={{0,2},{1,3},{2,0},{3,1},{4,6},{5,7},{6,4},{7,5},{8,10},{9,11},{10,... | collective-permute-start | bytes 393224 | tf_op jit(solution)/shard_map/ppermute | solution.py:190
  191.2 14.0 %collective-permute-start.11 = (f32[128,256]{1,0:T(8,128)S(1)}, f32[128,256]{1,0:T(8,128)}, u32[]{:S(2)}, u32[]{:S(2)}) collective-permute-start(f32[128,256]{1,0:T(8,128)S(1)} %get-tuple-element.48), channel_id=1, source_target_pairs={{0,3},{1,0},{2,1},{3,2},{4,7},{5,4},{6,5},{7,6},{8,11},{9,8},{10,9... | collective-permute-start | bytes 393224 | tf_op jit(solution)/shard_map/ppermute | solution.py:190
  200.2 13.1 %copy-start.24 = (f32[256,256]{1,0:T(8,128)S(1)}, f32[256,256]{1,0:T(8,128)}, u32[]{:S(2)}) copy-start(f32[256,256]{1,0:T(8,128)} %copy-done.23) | copy-start | bytes 786436
  201.1 7.3 %collective-permute-start.6 = (f32[128,256]{1,0:T(8,128)S(1)}, f32[128,256]{1,0:T(8,128)S(1)}, u32[]{:S(2)}, u32[]{:S(2)}) collective-permute-start(f32[128,256]{1,0:T(8,128)S(1)} %get-tuple-element.41), channel_id=1, source_target_pairs={{0,1},{1,2},{2,3},{3,0},{4,5},{5,6},{6,7},{7,4},{8,9},{9,10},{10,1... | collective-permute-start | bytes 393224 | tf_op jit(solution)/shard_map/ppermute | solution.py:190
  202.8 10.5 %collective-permute-start.7 = (f32[128,256]{1,0:T(8,128)S(1)}, f32[128,256]{1,0:T(8,128)S(1)}, u32[]{:S(2)}, u32[]{:S(2)}) collective-permute-start(f32[128,256]{1,0:T(8,128)S(1)} %get-tuple-element.42), channel_id=1, source_target_pairs={{0,2},{1,3},{2,0},{3,1},{4,6},{5,7},{6,4},{7,5},{8,10},{9,11},{10,... | collective-permute-start | bytes 393224 | tf_op jit(solution)/shard_map/ppermute | solution.py:190
  203.8 9.5 %collective-permute-start.8 = (f32[128,256]{1,0:T(8,128)S(1)}, f32[128,256]{1,0:T(8,128)S(1)}, u32[]{:S(2)}, u32[]{:S(2)}) collective-permute-start(f32[128,256]{1,0:T(8,128)S(1)} %get-tuple-element.43), channel_id=1, source_target_pairs={{0,3},{1,0},{2,1},{3,2},{4,7},{5,4},{6,5},{7,6},{8,11},{9,8},{10,9... | collective-permute-start | bytes 393224 | tf_op jit(solution)/shard_map/ppermute | solution.py:190
  (15 other events, 19.6 us)
Sparse Core Ops, SparseCore 0:
  27.4 42.3 all-gather.5
  80.7 29.4 all-gather.7
